TPU v7x, 32 devices: a whole 2x2x4 slice. The times are simulated.
32 devices in a mesh: band: 4 (over y, x), domain: 8 (over z, core).
Axes of the slice: x: 2, y: 2, z: 4, core: 2. Of those that a mesh axis runs over, the one named last changes fastest.
Arguments:
- functions: bfloat16 [512, 24576], P(('band', 'domain')), may hold values from -6 to 6
- pattern: int32 [4, 4], replicated, may hold values from 0 to 3, as said below
Outputs:
- corrected: bfloat16 [512, 24576], P(('band', 'domain'))
Inputs may be any that keep to these rules, and one draw needn't show every extreme that they name: Row b of pattern holds 4 different block numbers, and its first entry is b itself. The pattern is symmetric: j stands in row b exactly when b stands in row j.
All inputs are finite; a program needn't handle non-finite values.
Results may differ from a plain program's by a relative error of at most 0.0037.
Values may be sent and summed in bfloat16 or wider, within the bound.
No kernel may reach another device: no remote copies, remote signals or barrier semaphores. Data moves between devices by JAX's collectives and lax.ppermute only.
A program may use at most 192 MiB of HBM per device.

v0:
```python
import jax
import jax.numpy as jnp
from jax import lax
from jax.sharding import PartitionSpec as P

NC = 24576
BLOCK = 128


def apply_blocks(excess, block_index, source_blocks):
    picked = jnp.take(source_blocks, block_index, axis=0)
    return jnp.einsum("bkij,bkjc->bic", excess, picked, preferred_element_type=jnp.float32)


def per_device(functions, pattern):
    domains = lax.axis_size("domain")
    fdev = functions.shape[0]
    my_band = lax.axis_index("band")
    group = domains * fdev
    pieces = lax.all_to_all(functions, "domain", split_axis=1, concat_axis=0, tiled=True)
    every = lax.all_gather(pieces, "band", axis=0, tiled=True)
    width = every.shape[1]
    nblocks = every.shape[0] // BLOCK
    blocks = every.reshape(nblocks, BLOCK, width)
    rowblk = group // BLOCK
    block_index = lax.dynamic_slice_in_dim(pattern, my_band * rowblk, rowblk, 0)
    own_rows = pieces.reshape(rowblk, BLOCK, width)
    partners = jnp.take(blocks, block_index, axis=0)
    partial_sums = jnp.einsum(
        "bic,bkjc->bkij", own_rows, partners, preferred_element_type=jnp.float32
    )
    block_ids = my_band * rowblk + jnp.arange(rowblk, dtype=jnp.int32)
    on_diagonal = (block_index == block_ids[:, None]).astype(jnp.float32)
    total = lax.psum(partial_sums, "domain") * (1.0 / NC)
    identity = jnp.eye(BLOCK, dtype=jnp.float32)
    excess = (total - on_diagonal[:, :, None, None] * identity).astype(jnp.bfloat16)
    first = apply_blocks(excess, block_index, blocks)
    first_half = first.astype(jnp.bfloat16).reshape(group, width)
    all_first = lax.all_gather(first_half, "band", axis=0, tiled=True)
    first_blocks = all_first.reshape(nblocks, BLOCK, width)
    second = apply_blocks(excess, block_index, first_blocks)
    updated = own_rows.astype(jnp.float32) - 0.5 * first + 0.375 * second
    updated = updated.astype(jnp.bfloat16).reshape(group, width)
    return lax.all_to_all(updated, "domain", split_axis=0, concat_axis=1, tiled=True)


def solution(mesh):
    placed = (P(("band", "domain"), None), P())
    return jax.shard_map(
        per_device,
        mesh=mesh,
        in_specs=placed,
        out_specs=P(("band", "domain"), None),
        check_vma=False,
    )
```

profile of v0, /device:TPU:0, one launch (start us, length us, event | category | flops | bytes accessed | tf_op | source)
XLA Modules:
  0.0 222.8 jit_solution(7686187597460847485)
XLA Ops:
  6.5 0.0 all-gather.3.cloned.1.call-start
  6.5 1.2 copy.12
  7.7 27.2 %all_to_all.35 = bf16[16,8,3072]{2,0,1:T(8,128)(2,1)} all-to-all(bf16[16,8,3072]{2,0,1:T(8,128)(2,1)S(1)} %bitcast.78), channel_id=1, replica_groups=mesh['band'=4,'domain'=8] {'domain'}, dimensions={1} | all-to-all | bytes 1572864 | tf_op jit(solution)/shard_map/all_to_all | solution.py:20
  34.9 0.0 all-gather.3.cloned.1.call-update
  35.0 0.0 all-reduce.2.cloned.1.call-start
  35.0 0.7 and_bitcast_fusion
  35.7 42.3 %all-gather.3.cloned.1.call-done = bf16[512,3072]{1,0:T(8,128)(2,1)} async-done(((bf16[128,3072]{1,0:T(8,128)(2,1)}), bf16[512,3072]{1,0:T(8,128)(2,1)}) %all-gather.3.cloned.1.call-update) | async-done | bytes 3145744 | tf_op jit(solution)/shard_map/all_gather | solution.py:21
  78.0 2.6 %gather_fusion = bf16[4,128,3072]{2,1,0:T(8,128)(2,1)S(1)} fusion(bf16[4,128,3072]{2,1,0:T(8,128)(2,1)} %bitcast.72, s32[1024]{0:T(1024)S(1)} %pad_clamp_fusion), kind=kCustom, calls=%fused_computation.clone | custom fusion | bytes 6291472 | tf_op jit(solution)/shard_map/jit(_take)/gather | solution.py:28
  80.6 2.9 %fusion.9 = f32[1,4,128,128]{2,3,1,0:T(8,128)} fusion(bf16[128,3072,1]{1,0,2:T(8,128)(2,1)} %bitcast.75, bf16[4,128,3072]{2,1,0:T(8,128)(2,1)S(1)} %gather_fusion, pred[4]{0:T(512)(128)(4,1)S(1)} %get-tuple-element.6), kind=kOutput, calls=%fused_computation.15 | convolution fusion | flops 404226048 | bytes 4194308 | tf_op jit(solution)/shard_map/bic,bkjc->bkij/dot_general | solution.py:29
  83.5 0.0 all-reduce.2.cloned.1.call-update
  83.5 0.0 all-gather.5.cloned.1.call-start
  83.6 55.0 %all-reduce.2.cloned.1.call-done = f32[1,4,128,128]{2,3,1,0:T(8,128)} async-done(((f32[1,4,128,128]{2,3,1,0:T(8,128)}), f32[1,4,128,128]{2,3,1,0:T(8,128)}) %all-reduce.2.cloned.1.call-update) | async-done | bytes 262160 | tf_op jit(solution)/shard_map/psum | solution.py:34
  138.6 3.1 %fusion.20 = (bf16[128,3072]{1,0:T(8,128)(2,1)}, f32[128,3072]{1,0:T(8,128)}) fusion(bf16[4,128,3072]{2,1,0:T(8,128)(2,1)S(1)} %gather_fusion, pred[4]{0:T(512)(128)(4,1)S(1)} %get-tuple-element.6, f32[1,4,128,128]{2,3,1,0:T(8,128)} %all-reduce.2.cloned.1.call-done, f32[128,128]{0,1:T(8,128)S(1)} %fusion.13, f32[4]{0:T(128)S(1)} %get-tuple-element.8), kind=kOutput, calls=%fused_computation.30 | convolution fusion | flops 404881408 | bytes 5832724 | tf_op jit(solution)/shard_map/bkij,bkjc->bic/dot_general | solution.py:12
  141.7 0.0 all-gather.5.cloned.1.call-update
  141.7 43.1 %all-gather.5.cloned.1.call-done = bf16[512,3072]{1,0:T(8,128)(2,1)} async-done(((bf16[128,3072]{1,0:T(8,128)(2,1)}), bf16[512,3072]{1,0:T(8,128)(2,1)}) %all-gather.5.cloned.1.call-update) | async-done | bytes 3145744 | tf_op jit(solution)/shard_map/all_gather | solution.py:39
  184.8 0.0 copy-start
  184.8 2.7 %gather_fusion.1 = bf16[4,128,3072]{2,1,0:T(8,128)(2,1)S(1)} fusion(bf16[4,128,3072]{2,1,0:T(8,128)(2,1)} %bitcast.73, s32[1024]{0:T(1024)S(1)} %pad_clamp_fusion), kind=kCustom, calls=%fused_computation.1.clone | custom fusion | bytes 6291472 | tf_op jit(solution)/shard_map/jit(_take)/gather | solution.py:11
  187.5 0.0 copy-done
  187.5 2.4 %fusion.2 = bf16[128,3072]{1,0:T(8,128)(2,1)S(1)} fusion(bf16[4,128,3072]{2,1,0:T(8,128)(2,1)S(1)} %gather_fusion.1, pred[4]{0:T(512)(128)(4,1)S(1)} %get-tuple-element.6, f32[128,3072]{1,0:T(8,128)} %get-tuple-element.10, bf16[128,3072]{1,0:T(8,128)(2,1)} %bitcast.76, f32[1,4,128,128]{2,3,1,0:T(8,128)S(1)} %copy-done, f32[128,128]{0,1:T(8,128)S(1)} %fusion.13, ...), kind=kOutput, calls=%fused_computation.6 | convolution fusion | flops 406847488 | bytes 6619156 | tf_op jit(solution)/shard_map/bkij,bkjc->bic/dot_general | solution.py:12
  190.0 25.4 %all_to_all.36 = bf16[8,16,3072]{2,1,0:T(8,128)(2,1)S(1)} all-to-all(bf16[8,16,3072]{2,1,0:T(8,128)(2,1)S(1)} %bitcast.80), channel_id=1, replica_groups=mesh['band'=4,'domain'=8] {'domain'}, dimensions={0} | all-to-all | bytes 1572864 | tf_op jit(solution)/shard_map/all_to_all | solution.py:44
  215.3 0.9 copy.10
  (2 shorter events, 0.0 us)
Async XLA Ops:
  6.5 71.5 %all-gather.3.cloned.1.call-start = ((), (), s32[]{:S(2)}) async-start(), calls=%async_computation.2 | async-start | bytes 3932160 | tf_op jit(solution)/shard_map/all_gather | solution.py:21
  35.0 103.7 %all-reduce.2.cloned.1.call-start = ((), (), s32[]{:S(2)}) async-start(), calls=%async_computation.3 | async-start | bytes 524288 | tf_op jit(solution)/shard_map/psum | solution.py:34
  83.5 101.3 %all-gather.5.cloned.1.call-start = ((), (), s32[]{:S(2)}) async-start(), calls=%async_computation.4 | async-start | bytes 3932160 | tf_op jit(solution)/shard_map/all_gather | solution.py:39
  184.8 2.7 %copy-start = (f32[1,4,128,128]{2,3,1,0:T(8,128)S(1)}, f32[1,4,128,128]{2,3,1,0:T(8,128)}, u32[]{:S(2)}) copy-start(f32[1,4,128,128]{2,3,1,0:T(8,128)} %all-reduce.2.cloned.1.call-done) | copy-start | bytes 786436
Sparse Core Ops, SparseCore 0:
  35.1 42.8 all-gather.2
  83.6 54.9 all-reduce.1
  141.8 42.9 all-gather.4
where the time goes:
time: 223 us
  waiting for transfers between devices  140 us (63%)
  blocking collectives  52.6 us (24%)
  between operations  13.2 us (6%)
  matrix products  8.34 us (4%)
  local copies, waits for them, and re-layouts  7.44 us (3%)
    psum x1, waiting for transfers between devices, per_device(): total = lax.psum(partial_sums, 'domain') * (1.0 / NC)  55 us
    all_gather x1, waiting for transfers between devices, per_device(): all_first = lax.all_gather(first_half, 'band', axis=0, tiled=True)  43.1 us
    all_gather x1, waiting for transfers between devices, per_device(): every = lax.all_gather(pieces, 'band', axis=0, tiled=True)  42.3 us
    all_to_all x1, blocking collectives, per_device(): lax.all_to_all(functions, 'domain', split_axis=1, concat_axis=0, tiled=True)  27.2 us
    all_to_all x1, blocking collectives, per_device(): lax.all_to_all(updated, 'domain', split_axis=0, concat_axis=1, tiled=True)  25.4 us
    dot_general x2, matrix products, apply_blocks(): jnp.einsum('bkij,bkjc->bic', excess, picked, preferred_element_type=jnp.f...  5.49 us
  transfers between devices with their start and end apart: 3, of which 3 were waited for; matrix products, arithmetic and copies ran while one was open for 0% of the time, Pallas kernels for 0%

commit v1 on v0

--- a/solution.py
+++ b/solution.py
@@ -1,10 +1,160 @@
+import functools
+
 import jax
 import jax.numpy as jnp
 from jax import lax
+from jax.experimental import pallas as pl
+from jax.experimental.pallas import tpu as pltpu
 from jax.sharding import PartitionSpec as P
 
 NC = 24576
 BLOCK = 128
+BOTH = ("band", "domain")
+
+
+def vmem_call(body, outs, scratch=(), flops=0, moved=0):
+    return pl.pallas_call(
+        body,
+        out_shape=outs,
+        scratch_shapes=list(scratch),
+        cost_estimate=pl.CostEstimate(flops=flops, bytes_accessed=moved, transcendentals=0),
+        compiler_params=pltpu.CompilerParams(vmem_limit_bytes=48 * 1024 * 1024),
+    )
+
+
+def swap(value, axis, mask):
+    count = lax.axis_size(axis)
+    return lax.ppermute(value, axis, [(i, i ^ mask) for i in range(count)])
+
+
+def upper_blocks(nblocks):
+    return [(i, j) for i in range(nblocks) for j in range(i, nblocks)]
+
+
+def gram_halves(x, share):
+    rows, width = x.shape
+    nblocks = rows // BLOCK
+    pairs = upper_blocks(nblocks)
+    half = len(pairs) * BLOCK // 2
+    tile = 2 * BLOCK
+
+    def body(core_ref, x_ref, keep_ref, give_ref):
+        core = core_ref[0]
+        eye = (
+            lax.broadcasted_iota(jnp.int32, (BLOCK, BLOCK), 0) == lax.broadcasted_iota(jnp.int32, (BLOCK, BLOCK), 1)
+        ).astype(jnp.float32) * share
+        for a in range(rows // tile):
+            for b in range(a, rows // tile):
+                got = lax.dot_general(
+                    x_ref[a * tile:(a + 1) * tile, :],
+                    x_ref[b * tile:(b + 1) * tile, :],
+                    (((1,), (1,)), ((), ())),
+                    preferred_element_type=jnp.float32,
+                )
+                for i in range(2):
+                    for j in range(2):
+                        pair = (2 * a + i, 2 * b + j)
+                        if pair not in pairs:
+                            continue
+                        block = got[i * BLOCK:(i + 1) * BLOCK, j * BLOCK:(j + 1) * BLOCK]
+                        if pair[0] == pair[1]:
+                            block = block - eye
+                        start = pairs.index(pair) * BLOCK
+                        side, at = start // half, start % half
+
+                        @pl.when(core == side)
+                        def _():
+                            keep_ref[at:at + BLOCK, :] = block
+
+                        @pl.when(core != side)
+                        def _():
+                            give_ref[at:at + BLOCK, :] = block
+
+    stacked = jax.ShapeDtypeStruct((half, BLOCK), jnp.float32)
+    return pl.pallas_call(
+        body,
+        out_shape=(stacked, stacked),
+        in_specs=[pl.BlockSpec(memory_space=pltpu.SMEM), pl.BlockSpec(memory_space=pltpu.VMEM)],
+        compiler_params=pltpu.CompilerParams(vmem_limit_bytes=48 * 1024 * 1024),
+    )
+
+
+def band_pieces(half, bands):
+    piece = half // bands
+
+    def body(band_ref, keep_ref, got_ref, *piece_refs):
+        band = band_ref[0]
+        for m in range(bands):
+            at = pl.ds(pl.multiple_of((band ^ m) * piece, piece), piece)
+            piece_refs[m][...] = keep_ref[at, :] + got_ref[at, :]
+
+    return pl.pallas_call(
+        body,
+        out_shape=tuple(jax.ShapeDtypeStruct((piece, BLOCK), jnp.float32) for _ in range(bands)),
+        in_specs=[pl.BlockSpec(memory_space=pltpu.SMEM)] + [pl.BlockSpec(memory_space=pltpu.VMEM)] * 2,
+    )
+
+
+def correct(x, pieces, bands):
+    rows, width = x.shape
+    nblocks = rows // BLOCK
+    pairs = upper_blocks(nblocks)
+    half = len(pairs) * BLOCK // 2
+    piece = half // bands
+
+    def body(place_ref, x_ref, *refs):
+        piece_refs, out_ref, packed, excess = refs[:-3], refs[-3], refs[-2], refs[-1]
+        band, core = place_ref[0], place_ref[1]
+        for m in range(bands):
+            for c in range(2):
+                start = (core ^ c) * half + (band ^ m) * piece
+                packed[pl.ds(pl.multiple_of(start, 16), piece), :] = piece_refs[c * bands + m][...]
+        for p, (i, j) in enumerate(pairs):
+            block = packed[p * BLOCK:(p + 1) * BLOCK, :]
+            excess[i * BLOCK:(i + 1) * BLOCK, j * BLOCK:(j + 1) * BLOCK] = block
+            if i != j:
+                excess[j * BLOCK:(j + 1) * BLOCK, i * BLOCK:(i + 1) * BLOCK] = block.T
+        first = jnp.dot(excess[...], x_ref[...], preferred_element_type=jnp.float32)
+        second = jnp.dot(excess[...], first.astype(jnp.bfloat16), preferred_element_type=jnp.float32)
+        out = x_ref[...].astype(jnp.float32) - 0.5 * first + 0.375 * second
+        out_ref[...] = out.astype(jnp.bfloat16)
+
+    return pl.pallas_call(
+        body,
+        out_shape=jax.ShapeDtypeStruct(x.shape, jnp.bfloat16),
+        in_specs=[pl.BlockSpec(memory_space=pltpu.SMEM)] + [pl.BlockSpec(memory_space=pltpu.VMEM)] * (1 + 2 * bands),
+        scratch_shapes=[
+            pltpu.VMEM((2 * half, BLOCK), jnp.bfloat16),
+            pltpu.VMEM((rows, rows), jnp.bfloat16),
+        ],
+        compiler_params=pltpu.CompilerParams(vmem_limit_bytes=48 * 1024 * 1024),
+    )
+
+
+def full_rows(functions, pattern):
+    bands, domains = lax.axis_size("band"), lax.axis_size("domain")
+    devices = bands * domains
+    fdev, ncoef = functions.shape
+    width = ncoef // devices
+    x = lax.all_to_all(functions, BOTH, split_axis=1, concat_axis=0, tiled=True)
+    band = lax.axis_index("band").astype(jnp.int32)
+    core = lax.rem(lax.axis_index("domain"), 2).astype(jnp.int32)
+    keep, give = gram_halves(x, NC // devices)(core.reshape(1), x)
+    got = swap(give, "domain", 1)
+    pieces = band_pieces(keep.shape[0], bands)(band.reshape(1), keep, got)
+    total = pieces[0]
+    for m in range(1, bands):
+        total = total + swap(pieces[m], "band", m)
+    levels = domains // 2
+    heard = [total] + [swap(total, "domain", 2 * m) for m in range(1, levels)]
+    while len(heard) > 1:
+        heard = [heard[k] + heard[k + 1] for k in range(0, len(heard), 2)]
+    excess = (heard[0] * (1.0 / NC)).astype(jnp.bfloat16)
+    mine = [excess] + [swap(excess, "band", m) for m in range(1, bands)]
+    other = [swap(e, "domain", 1) for e in mine]
+    place = jnp.stack([band, core])
+    out = correct(x, mine, bands)(place, x, *mine, *other)
+    return lax.all_to_all(out, BOTH, split_axis=0, concat_axis=1, tiled=True)
 
 
 def apply_blocks(excess, block_index, source_blocks):
@@ -12,7 +162,7 @@
     return jnp.einsum("bkij,bkjc->bic", excess, picked, preferred_element_type=jnp.float32)
 
 
-def per_device(functions, pattern):
+def some_rows(functions, pattern):
     domains = lax.axis_size("domain")
     fdev = functions.shape[0]
     my_band = lax.axis_index("band")
@@ -44,12 +194,17 @@
     return lax.all_to_all(updated, "domain", split_axis=0, concat_axis=1, tiled=True)
 
 
+def per_device(functions, pattern):
+    nblocks, nonzero = pattern.shape
+    return (full_rows if nonzero == nblocks else some_rows)(functions, pattern)
+
+
 def solution(mesh):
-    placed = (P(("band", "domain"), None), P())
+    placed = (P(BOTH, None), P())
     return jax.shard_map(
         per_device,
         mesh=mesh,
         in_specs=placed,
-        out_specs=P(("band", "domain"), None),
+        out_specs=P(BOTH, None),
         check_vma=False,
     )

time: 223 us -> 89.4 us (0.40)
  waiting for transfers between devices: 140 us -> 35.9 us
  blocking collectives: 52.6 us -> 24.2 us
  starting transfers between devices: 0.09 us -> 18.9 us
  between operations: 13.2 us -> 0.07 us
  matrix products: 8.34 us -> 0 us
  Pallas kernels: 0 us -> 4.58 us
  local copies, waits for them, and re-layouts: 7.44 us -> 4.44 us
    all_gather x2 -> x0, waiting for transfers between devices: 85.4 us -> none  [the longest x1 43.1 us: per_device(): all_first = lax.all_gather(first_half, 'band', axis=0, tiled=True)]
    psum x1 -> x0, waiting for transfers between devices: 55 us -> none  [per_device(): total = lax.psum(partial_sums, 'domain') * (1.0 / NC)]
    all_to_all x2 -> x1, blocking collectives: 52.6 us -> 24.2 us  [full_rows(): return lax.all_to_all(out, BOTH, split_axis=0, concat_axis=1, tiled=True)]
    all_to_all x0 -> x1, waiting for transfers between devices: none -> 22 us  [full_rows(): x = lax.all_to_all(functions, BOTH, split_axis=1, concat_axis=0, tiled=True)]
    ppermute x0 -> x14, waiting for transfers between devices: none -> 13.9 us  [swap(): return lax.ppermute(value, axis, [(i, i ^ mask) for i in range(count)])]
    ppermute x0 -> x14, starting transfers between devices: none -> 11.6 us  [swap(): return lax.ppermute(value, axis, [(i, i ^ mask) for i in range(count)])]
    dot_general x3 -> x0, matrix products: 8.34 us -> none  [the longest x2 5.49 us: apply_blocks(): jnp.einsum('bkij,bkjc->bic', excess, picked, preferred_element_type=jnp.f...]
    all_to_all x0 -> x1, starting transfers between devices: none -> 7.3 us  [full_rows(): x = lax.all_to_all(functions, BOTH, split_axis=1, concat_axis=0, tiled=True)]
  transfers between devices with their start and end apart: 3 -> 15, of which waited for: 3 -> 10; matrix products, arithmetic and copies ran while one was open for 0% -> 0% of each run, Pallas kernels for 0% -> 0%
where the time goes in v1:
time: 89.4 us; the launch traced here: 89.1 us
  waiting for transfers between devices  35.9 us (40%)
  blocking collectives  24.2 us (27%)
  starting transfers between devices  18.9 us (21%)
  Pallas kernels  4.58 us (5%)
  local copies, waits for them, and re-layouts  4.44 us (5%)
  other arithmetic  1 us (1%)
    all_to_all x1, blocking collectives, full_rows(): return lax.all_to_all(out, BOTH, split_axis=0, concat_axis=1, tiled=True)  24.2 us
    all_to_all x1, waiting for transfers between devices, full_rows(): x = lax.all_to_all(functions, BOTH, split_axis=1, concat_axis=0, tiled=True)  22 us
    ppermute x14, waiting for transfers between devices, swap(): return lax.ppermute(value, axis, [(i, i ^ mask) for i in range(count)])  13.9 us
    ppermute x14, starting transfers between devices, swap(): return lax.ppermute(value, axis, [(i, i ^ mask) for i in range(count)])  11.6 us
    all_to_all x1, starting transfers between devices, full_rows(): x = lax.all_to_all(functions, BOTH, split_axis=1, concat_axis=0, tiled=True)  7.3 us
    all_to_all x1, local copies, waits for them, and re-layouts, full_rows(): x = lax.all_to_all(functions, BOTH, split_axis=1, concat_axis=0, tiled=True)  2.07 us
    pallas_call x1, Pallas kernels, full_rows(): pieces = band_pieces(keep.shape[0], bands)(band.reshape(1), keep, got)  1.83 us
  transfers between devices with their start and end apart: 15, of which 10 were waited for; matrix products, arithmetic and copies ran while one was open for 0% of the time, Pallas kernels for 0%

profile of v1, /device:TPU:0, one launch (start us, length us, event | category | flops | bytes accessed | tf_op | source)
XLA Modules:
  0.0 89.1 jit_solution(174900907191938858)
XLA Ops:
  0.0 2.1 %copy.7 = bf16[2,32,8,768]{3,2,0,1:T(8,128)(2,1)} copy(bf16[2,32,8,768]{3,2,1,0:T(8,128)(2,1)} %bitcast.17) | data formatting | bytes 1572864 | tf_op jit(solution)/shard_map/all_to_all | solution.py:139
  2.1 7.3 %all-to-all-start = ((bf16[16,32,768]{2,0,1:T(8,128)(2,1)}), bf16[16,32,768]{2,0,1:T(8,128)(2,1)S(1)}, u32[]{:S(2)}, u32[]{:S(2)}) async-start(bf16[16,32,768]{2,0,1:T(8,128)(2,1)} %bitcast.12), calls=%async_computation | async-start | bytes 1572864 | tf_op jit(solution)/shard_map/all_to_all | solution.py:139
  9.4 22.0 %all-to-all-done = bf16[16,32,768]{2,0,1:T(8,128)(2,1)S(1)} async-done(((bf16[16,32,768]{2,0,1:T(8,128)(2,1)}), bf16[16,32,768]{2,0,1:T(8,128)(2,1)S(1)}, u32[]{:S(2)}, u32[]{:S(2)}) %all-to-all-start) | async-done | bytes 786464 | tf_op jit(solution)/shard_map/all_to_all | solution.py:139
  31.3 1.1 %shard_map.17 = (f32[640,128]{1,0:T(8,128)S(1)}, f32[640,128]{1,0:T(8,128)S(1)}) custom-call(s32[1]{0:T(128)} %bitcast.1.core_ref, bf16[512,768]{1,0:T(8,128)(2,1)S(1)} %bitcast.13), custom_call_target="tpu_custom_call" | custom-call | tf_op jit(solution)/shard_map/pallas_call | solution.py:142
  32.5 0.0 copy-start
  32.5 0.7 copy-done
  33.2 0.0 collective-permute-start
  33.2 1.6 %collective-permute-done.got_ref = f32[640,128]{1,0:T(8,128)S(1)} collective-permute-done((f32[640,128]{1,0:T(8,128)S(1)}, f32[640,128]{1,0:T(8,128)S(1)}, u32[]{:S(2)}, u32[]{:S(2)}) %collective-permute-start) | collective-permute-done | bytes 327712 | tf_op jit(solution)/shard_map/ppermute | solution.py:27
  34.8 0.7 copy-done.1
  35.5 1.8 %shard_map.18 = (f32[160,128]{1,0:T(8,128)}, f32[160,128]{1,0:T(8,128)}, f32[160,128]{1,0:T(8,128)}, f32[160,128]{1,0:T(8,128)}) custom-call(s32[1]{0:T(128)} %bitcast.band_ref, f32[640,128]{1,0:T(8,128)} %copy-done, f32[640,128]{1,0:T(8,128)} %copy-done.1), custom_call_target="tpu_custom_call" | custom-call | tf_op jit(solution)/shard_map/pallas_call | solution.py:144
  37.4 0.5 collective-permute-start.1
  37.9 0.6 collective-permute-start.2
  38.5 2.4 %collective-permute-start.3 = (f32[160,128]{1,0:T(8,128)}, f32[160,128]{1,0:T(8,128)S(1)}, u32[]{:S(2)}, u32[]{:S(2)}) collective-permute-start(f32[160,128]{1,0:T(8,128)} %get-tuple-element.16), channel_id=1, source_target_pairs={{0,24},{8,16},{16,8},{24,0},{1,25},{9,17},{17,9},{25,1},{2,26},{10... | collective-permute-start | bytes 245768 | tf_op jit(solution)/shard_map/ppermute | solution.py:27
  40.9 1.3 %collective-permute-done.1 = f32[160,128]{1,0:T(8,128)S(1)} collective-permute-done((f32[160,128]{1,0:T(8,128)}, f32[160,128]{1,0:T(8,128)S(1)}, u32[]{:S(2)}, u32[]{:S(2)}) %collective-permute-start.1) | collective-permute-done | bytes 81952 | tf_op jit(solution)/shard_map/ppermute | solution.py:27
  42.2 2.1 %collective-permute-done.2 = f32[160,128]{1,0:T(8,128)S(1)} collective-permute-done((f32[160,128]{1,0:T(8,128)}, f32[160,128]{1,0:T(8,128)S(1)}, u32[]{:S(2)}, u32[]{:S(2)}) %collective-permute-start.2) | collective-permute-done | bytes 81952 | tf_op jit(solution)/shard_map/ppermute | solution.py:27
  44.3 0.9 %add_add_fusion = f32[160,128]{1,0:T(8,128)S(1)} fusion(f32[160,128]{1,0:T(8,128)S(1)} %collective-permute-done.3, f32[160,128]{1,0:T(8,128)S(1)} %collective-permute-done.2, f32[160,128]{1,0:T(8,128)} %get-tuple-element.13, f32[160,128]{1,0:T(8,128)S(1)} %collective-permute-done.1), kind=kLoop, calls=%fused_computation.2 | loop fusion | flops 61440 | bytes 409600 | tf_op jit(solution)/shard_map/add | solution.py:147
  45.2 1.7 %collective-permute-start.6 = (f32[160,128]{1,0:T(8,128)S(1)}, f32[160,128]{1,0:T(8,128)S(1)}, u32[]{:S(2)}, u32[]{:S(2)}) collective-permute-start(f32[160,128]{1,0:T(8,128)S(1)} %add_add_fusion), channel_id=1, source_target_pairs={{0,6},{1,7},{2,4},{3,5},{4,2},{5,3},{6,0},{7,1},{8,14},{9,15},{10,... | collective-permute-start | bytes 245768 | tf_op jit(solution)/shard_map/ppermute | solution.py:27
  46.9 2.8 %collective-permute-start.4 = (f32[160,128]{1,0:T(8,128)S(1)}, f32[160,128]{1,0:T(8,128)S(1)}, u32[]{:S(2)}, u32[]{:S(2)}) collective-permute-start(f32[160,128]{1,0:T(8,128)S(1)} %add_add_fusion), channel_id=1, source_target_pairs={{0,2},{1,3},{2,0},{3,1},{4,6},{5,7},{6,4},{7,5},{8,10},{9,11},{10,... | collective-permute-start | bytes 245768 | tf_op jit(solution)/shard_map/ppermute | solution.py:27
  49.7 2.4 %collective-permute-done.6 = f32[160,128]{1,0:T(8,128)S(1)} collective-permute-done((f32[160,128]{1,0:T(8,128)S(1)}, f32[160,128]{1,0:T(8,128)S(1)}, u32[]{:S(2)}, u32[]{:S(2)}) %collective-permute-start.6) | collective-permute-done | bytes 81952 | tf_op jit(solution)/shard_map/ppermute | solution.py:27
  52.1 2.4 %collective-permute-done.5 = f32[160,128]{1,0:T(8,128)S(1)} collective-permute-done((f32[160,128]{1,0:T(8,128)S(1)}, f32[160,128]{1,0:T(8,128)S(1)}, u32[]{:S(2)}, u32[]{:S(2)}) %collective-permute-start.5) | collective-permute-done | bytes 81952 | tf_op jit(solution)/shard_map/ppermute | solution.py:27
  54.5 1.3 %collective-permute-start.9 = (bf16[160,128]{1,0:T(8,128)(2,1)S(1)}, bf16[160,128]{1,0:T(8,128)(2,1)S(1)}, u32[]{:S(2)}, u32[]{:S(2)}) collective-permute-start(bf16[160,128]{1,0:T(8,128)(2,1)S(1)} %multiply_convert_fusion.refs_0_), channel_id=1, source_target_pairs={{0,24},{8,16},{16,8},{24,0},{1,25},{9,17},{17,9},{25,1},{2,26},{10... | collective-permute-start | bytes 122888 | tf_op jit(solution)/shard_map/ppermute | solution.py:27
  55.8 1.3 %collective-permute-start.8 = (bf16[160,128]{1,0:T(8,128)(2,1)S(1)}, bf16[160,128]{1,0:T(8,128)(2,1)S(1)}, u32[]{:S(2)}, u32[]{:S(2)}) collective-permute-start(bf16[160,128]{1,0:T(8,128)(2,1)S(1)} %multiply_convert_fusion.refs_0_), channel_id=1, source_target_pairs={{0,16},{8,24},{16,0},{24,8},{1,17},{9,25},{17,1},{25,9},{2,18},{10... | collective-permute-start | bytes 122888 | tf_op jit(solution)/shard_map/ppermute | solution.py:27
  57.1 1.0 %collective-permute-start.7 = (bf16[160,128]{1,0:T(8,128)(2,1)S(1)}, bf16[160,128]{1,0:T(8,128)(2,1)S(1)}, u32[]{:S(2)}, u32[]{:S(2)}) collective-permute-start(bf16[160,128]{1,0:T(8,128)(2,1)S(1)} %multiply_convert_fusion.refs_0_), channel_id=1, source_target_pairs={{0,8},{8,0},{16,24},{24,16},{1,9},{9,1},{17,25},{25,17},{2,10},{10... | collective-permute-start | bytes 122888 | tf_op jit(solution)/shard_map/ppermute | solution.py:27
  58.1 1.4 %collective-permute-done.9.refs_3_ = bf16[160,128]{1,0:T(8,128)(2,1)S(1)} collective-permute-done((bf16[160,128]{1,0:T(8,128)(2,1)S(1)}, bf16[160,128]{1,0:T(8,128)(2,1)S(1)}, u32[]{:S(2)}, u32[]{:S(2)}) %collective-permute-start.9) | collective-permute-done | bytes 40992 | tf_op jit(solution)/shard_map/ppermute | solution.py:27
  59.5 0.4 collective-permute-done.8.refs_2_
  59.9 0.1 collective-permute-start.12
  60.0 1.1 %collective-permute-done.7.refs_1_ = bf16[160,128]{1,0:T(8,128)(2,1)S(1)} collective-permute-done((bf16[160,128]{1,0:T(8,128)(2,1)S(1)}, bf16[160,128]{1,0:T(8,128)(2,1)S(1)}, u32[]{:S(2)}, u32[]{:S(2)}) %collective-permute-start.7) | collective-permute-done | bytes 40992 | tf_op jit(solution)/shard_map/ppermute | solution.py:27
  61.1 0.1 pad_add_fusion.place_ref
  61.2 1.1 %collective-permute-done.11.refs_5_ = bf16[160,128]{1,0:T(8,128)(2,1)S(1)} collective-permute-done((bf16[160,128]{1,0:T(8,128)(2,1)S(1)}, bf16[160,128]{1,0:T(8,128)(2,1)S(1)}, u32[]{:S(2)}, u32[]{:S(2)}) %collective-permute-start.11) | collective-permute-done | bytes 40992 | tf_op jit(solution)/shard_map/ppermute | solution.py:27
  62.3 1.6 %shard_map.19 = bf16[512,768]{1,0:T(8,128)(2,1)S(1)} custom-call(s32[2]{0:T(128)S(1)} %pad_add_fusion.place_ref, bf16[512,768]{1,0:T(8,128)(2,1)S(1)} %bitcast.14, bf16[160,128]{1,0:T(8,128)(2,1)S(1)} %multiply_convert_fusion.refs_0_, bf16[160,128]{1,0:T(8,128)(2,1)S(1)} %collective-permute-done.7.refs_1_, ...), custom_call_target="tpu_custom_call" | custom-call | tf_op jit(solution)/shard_map/pallas_call | solution.py:156
  64.0 24.2 %all_to_all.38 = bf16[32,16,768]{2,1,0:T(8,128)(2,1)S(1)} all-to-all(bf16[32,16,768]{2,1,0:T(8,128)(2,1)S(1)} %bitcast.15), channel_id=1, replica_groups=mesh['band'=4,'domain'=8] {'band','domain'}, dimensions={0} | all-to-all | bytes 1572864 | tf_op jit(solution)/shard_map/all_to_all | solution.py:157
  88.1 0.9 %copy.5 = bf16[32,2,8,768]{3,2,0,1:T(8,128)(2,1)} copy(bf16[32,2,8,768]{3,2,1,0:T(8,128)(2,1)S(1)} %bitcast.16) | data formatting | bytes 1572864 | tf_op jit(solution)/shard_map/all_to_all | solution.py:157
  (11 shorter events, 0.0 us)
Async XLA Ops:
  2.1 29.3 %all-to-all-start = ((bf16[16,32,768]{2,0,1:T(8,128)(2,1)}), bf16[16,32,768]{2,0,1:T(8,128)(2,1)S(1)}, u32[]{:S(2)}, u32[]{:S(2)}) async-start(bf16[16,32,768]{2,0,1:T(8,128)(2,1)} %bitcast.12), calls=%async_computation | async-start | bytes 1572864 | tf_op jit(solution)/shard_map/all_to_all | solution.py:139
  32.5 0.7 copy-start
  33.2 1.6 %collective-permute-start = (f32[640,128]{1,0:T(8,128)S(1)}, f32[640,128]{1,0:T(8,128)S(1)}, u32[]{:S(2)}, u32[]{:S(2)}) collective-permute-start(f32[640,128]{1,0:T(8,128)S(1)} %get-tuple-element.12), channel_id=1, source_target_pairs={{0,1},{1,0},{2,3},{3,2},{4,5},{5,4},{6,7},{7,6},{8,9},{9,8},{10,11... | collective-permute-start | bytes 983048 | tf_op jit(solution)/shard_map/ppermute | solution.py:27
  34.8 0.7 copy-start.1
  37.4 4.8 %collective-permute-start.1 = (f32[160,128]{1,0:T(8,128)}, f32[160,128]{1,0:T(8,128)S(1)}, u32[]{:S(2)}, u32[]{:S(2)}) collective-permute-start(f32[160,128]{1,0:T(8,128)} %get-tuple-element.14), channel_id=1, source_target_pairs={{0,8},{8,0},{16,24},{24,16},{1,9},{9,1},{17,25},{25,17},{2,10},{10... | collective-permute-start | bytes 245768 | tf_op jit(solution)/shard_map/ppermute | solution.py:27
  37.9 6.4 %collective-permute-start.2 = (f32[160,128]{1,0:T(8,128)}, f32[160,128]{1,0:T(8,128)S(1)}, u32[]{:S(2)}, u32[]{:S(2)}) collective-permute-start(f32[160,128]{1,0:T(8,128)} %get-tuple-element.15), channel_id=1, source_target_pairs={{0,16},{8,24},{16,0},{24,8},{1,17},{9,25},{17,1},{25,9},{2,18},{10... | collective-permute-start | bytes 245768 | tf_op jit(solution)/shard_map/ppermute | solution.py:27
  38.5 5.8 %collective-permute-start.3 = (f32[160,128]{1,0:T(8,128)}, f32[160,128]{1,0:T(8,128)S(1)}, u32[]{:S(2)}, u32[]{:S(2)}) collective-permute-start(f32[160,128]{1,0:T(8,128)} %get-tuple-element.16), channel_id=1, source_target_pairs={{0,24},{8,16},{16,8},{24,0},{1,25},{9,17},{17,9},{25,1},{2,26},{10... | collective-permute-start | bytes 245768 | tf_op jit(solution)/shard_map/ppermute | solution.py:27
  45.2 6.9 %collective-permute-start.6 = (f32[160,128]{1,0:T(8,128)S(1)}, f32[160,128]{1,0:T(8,128)S(1)}, u32[]{:S(2)}, u32[]{:S(2)}) collective-permute-start(f32[160,128]{1,0:T(8,128)S(1)} %add_add_fusion), channel_id=1, source_target_pairs={{0,6},{1,7},{2,4},{3,5},{4,2},{5,3},{6,0},{7,1},{8,14},{9,15},{10,... | collective-permute-start | bytes 245768 | tf_op jit(solution)/shard_map/ppermute | solution.py:27
  46.9 7.6 %collective-permute-start.5 = (f32[160,128]{1,0:T(8,128)S(1)}, f32[160,128]{1,0:T(8,128)S(1)}, u32[]{:S(2)}, u32[]{:S(2)}) collective-permute-start(f32[160,128]{1,0:T(8,128)S(1)} %add_add_fusion), channel_id=1, source_target_pairs={{0,4},{1,5},{2,6},{3,7},{4,0},{5,1},{6,2},{7,3},{8,12},{9,13},{10,... | collective-permute-start | bytes 245768 | tf_op jit(solution)/shard_map/ppermute | solution.py:27
  46.9 7.6 %collective-permute-start.4 = (f32[160,128]{1,0:T(8,128)S(1)}, f32[160,128]{1,0:T(8,128)S(1)}, u32[]{:S(2)}, u32[]{:S(2)}) collective-permute-start(f32[160,128]{1,0:T(8,128)S(1)} %add_add_fusion), channel_id=1, source_target_pairs={{0,2},{1,3},{2,0},{3,1},{4,6},{5,7},{6,4},{7,5},{8,10},{9,11},{10,... | collective-permute-start | bytes 245768 | tf_op jit(solution)/shard_map/ppermute | solution.py:27
  54.5 5.0 %collective-permute-start.9 = (bf16[160,128]{1,0:T(8,128)(2,1)S(1)}, bf16[160,128]{1,0:T(8,128)(2,1)S(1)}, u32[]{:S(2)}, u32[]{:S(2)}) collective-permute-start(bf16[160,128]{1,0:T(8,128)(2,1)S(1)} %multiply_convert_fusion.refs_0_), channel_id=1, source_target_pairs={{0,24},{8,16},{16,8},{24,0},{1,25},{9,17},{17,9},{25,1},{2,26},{10... | collective-permute-start | bytes 122888 | tf_op jit(solution)/shard_map/ppermute | solution.py:27
  55.8 4.1 %collective-permute-start.8 = (bf16[160,128]{1,0:T(8,128)(2,1)S(1)}, bf16[160,128]{1,0:T(8,128)(2,1)S(1)}, u32[]{:S(2)}, u32[]{:S(2)}) collective-permute-start(bf16[160,128]{1,0:T(8,128)(2,1)S(1)} %multiply_convert_fusion.refs_0_), channel_id=1, source_target_pairs={{0,16},{8,24},{16,0},{24,8},{1,17},{9,25},{17,1},{25,9},{2,18},{10... | collective-permute-start | bytes 122888 | tf_op jit(solution)/shard_map/ppermute | solution.py:27
  57.1 4.0 %collective-permute-start.7 = (bf16[160,128]{1,0:T(8,128)(2,1)S(1)}, bf16[160,128]{1,0:T(8,128)(2,1)S(1)}, u32[]{:S(2)}, u32[]{:S(2)}) collective-permute-start(bf16[160,128]{1,0:T(8,128)(2,1)S(1)} %multiply_convert_fusion.refs_0_), channel_id=1, source_target_pairs={{0,8},{8,0},{16,24},{24,16},{1,9},{9,1},{17,25},{25,17},{2,10},{10... | collective-permute-start | bytes 122888 | tf_op jit(solution)/shard_map/ppermute | solution.py:27
  58.1 3.1 %collective-permute-start.10 = (bf16[160,128]{1,0:T(8,128)(2,1)S(1)}, bf16[160,128]{1,0:T(8,128)(2,1)S(1)}, u32[]{:S(2)}, u32[]{:S(2)}) collective-permute-start(bf16[160,128]{1,0:T(8,128)(2,1)S(1)} %multiply_convert_fusion.refs_0_), channel_id=1, source_target_pairs={{0,1},{1,0},{2,3},{3,2},{4,5},{5,4},{6,7},{7,6},{8,9},{9,8},{10,11... | collective-permute-start | bytes 122888 | tf_op jit(solution)/shard_map/ppermute | solution.py:27
  59.5 1.7 %collective-permute-start.13 = (bf16[160,128]{1,0:T(8,128)(2,1)S(1)}, bf16[160,128]{1,0:T(8,128)(2,1)S(1)}, u32[]{:S(2)}, u32[]{:S(2)}) collective-permute-start(bf16[160,128]{1,0:T(8,128)(2,1)S(1)} %collective-permute-done.9.refs_3_), channel_id=1, source_target_pairs={{0,1},{1,0},{2,3},{3,2},{4,5},{5,4},{6,7},{7,6},{8,9},{9,8},{10,11... | collective-permute-start | bytes 122888 | tf_op jit(solution)/shard_map/ppermute | solution.py:27
  59.9 1.2 %collective-permute-start.12 = (bf16[160,128]{1,0:T(8,128)(2,1)S(1)}, bf16[160,128]{1,0:T(8,128)(2,1)S(1)}, u32[]{:S(2)}, u32[]{:S(2)}) collective-permute-start(bf16[160,128]{1,0:T(8,128)(2,1)S(1)} %collective-permute-done.8.refs_2_), channel_id=1, source_target_pairs={{0,1},{1,0},{2,3},{3,2},{4,5},{5,4},{6,7},{7,6},{8,9},{9,8},{10,11... | collective-permute-start | bytes 122888 | tf_op jit(solution)/shard_map/ppermute | solution.py:27
  61.1 1.2 %collective-permute-start.11 = (bf16[160,128]{1,0:T(8,128)(2,1)S(1)}, bf16[160,128]{1,0:T(8,128)(2,1)S(1)}, u32[]{:S(2)}, u32[]{:S(2)}) collective-permute-start(bf16[160,128]{1,0:T(8,128)(2,1)S(1)} %collective-permute-done.7.refs_1_), channel_id=1, source_target_pairs={{0,1},{1,0},{2,3},{3,2},{4,5},{5,4},{6,7},{7,6},{8,9},{9,8},{10,11... | collective-permute-start | bytes 122888 | tf_op jit(solution)/shard_map/ppermute | solution.py:27

commit v2 on v1

--- a/solution.py
+++ b/solution.py
@@ -12,14 +12,11 @@
 BOTH = ("band", "domain")
 
 
-def vmem_call(body, outs, scratch=(), flops=0, moved=0):
-    return pl.pallas_call(
-        body,
-        out_shape=outs,
-        scratch_shapes=list(scratch),
-        cost_estimate=pl.CostEstimate(flops=flops, bytes_accessed=moved, transcendentals=0),
-        compiler_params=pltpu.CompilerParams(vmem_limit_bytes=48 * 1024 * 1024),
-    )
+VMEM_LIMIT = pltpu.CompilerParams(vmem_limit_bytes=16 * 1024 * 1024)
+
+
+def my_core():
+    return lax.rem(lax.axis_index("domain"), 2)
 
 
 def swap(value, axis, mask):
@@ -38,8 +35,8 @@
     half = len(pairs) * BLOCK // 2
     tile = 2 * BLOCK
 
-    def body(core_ref, x_ref, keep_ref, give_ref):
-        core = core_ref[0]
+    def body(x_ref, keep_ref, give_ref):
+        core = my_core()
         eye = (
             lax.broadcasted_iota(jnp.int32, (BLOCK, BLOCK), 0) == lax.broadcasted_iota(jnp.int32, (BLOCK, BLOCK), 1)
         ).astype(jnp.float32) * share
@@ -74,16 +71,15 @@
     return pl.pallas_call(
         body,
         out_shape=(stacked, stacked),
-        in_specs=[pl.BlockSpec(memory_space=pltpu.SMEM), pl.BlockSpec(memory_space=pltpu.VMEM)],
-        compiler_params=pltpu.CompilerParams(vmem_limit_bytes=48 * 1024 * 1024),
+        compiler_params=VMEM_LIMIT,
     )
 
 
 def band_pieces(half, bands):
     piece = half // bands
 
-    def body(band_ref, keep_ref, got_ref, *piece_refs):
-        band = band_ref[0]
+    def body(keep_ref, got_ref, *piece_refs):
+        band = lax.axis_index("band")
         for m in range(bands):
             at = pl.ds(pl.multiple_of((band ^ m) * piece, piece), piece)
             piece_refs[m][...] = keep_ref[at, :] + got_ref[at, :]
@@ -91,7 +87,7 @@
     return pl.pallas_call(
         body,
         out_shape=tuple(jax.ShapeDtypeStruct((piece, BLOCK), jnp.float32) for _ in range(bands)),
-        in_specs=[pl.BlockSpec(memory_space=pltpu.SMEM)] + [pl.BlockSpec(memory_space=pltpu.VMEM)] * 2,
+        compiler_params=VMEM_LIMIT,
     )
 
 
@@ -102,9 +98,9 @@
     half = len(pairs) * BLOCK // 2
     piece = half // bands
 
-    def body(place_ref, x_ref, *refs):
+    def body(x_ref, *refs):
         piece_refs, out_ref, packed, excess = refs[:-3], refs[-3], refs[-2], refs[-1]
-        band, core = place_ref[0], place_ref[1]
+        band, core = lax.axis_index("band"), my_core()
         for m in range(bands):
             for c in range(2):
                 start = (core ^ c) * half + (band ^ m) * piece
@@ -122,12 +118,11 @@
     return pl.pallas_call(
         body,
         out_shape=jax.ShapeDtypeStruct(x.shape, jnp.bfloat16),
-        in_specs=[pl.BlockSpec(memory_space=pltpu.SMEM)] + [pl.BlockSpec(memory_space=pltpu.VMEM)] * (1 + 2 * bands),
         scratch_shapes=[
             pltpu.VMEM((2 * half, BLOCK), jnp.bfloat16),
             pltpu.VMEM((rows, rows), jnp.bfloat16),
         ],
-        compiler_params=pltpu.CompilerParams(vmem_limit_bytes=48 * 1024 * 1024),
+        compiler_params=VMEM_LIMIT,
     )
 
 
@@ -137,11 +132,9 @@
     fdev, ncoef = functions.shape
     width = ncoef // devices
     x = lax.all_to_all(functions, BOTH, split_axis=1, concat_axis=0, tiled=True)
-    band = lax.axis_index("band").astype(jnp.int32)
-    core = lax.rem(lax.axis_index("domain"), 2).astype(jnp.int32)
-    keep, give = gram_halves(x, NC // devices)(core.reshape(1), x)
+    keep, give = gram_halves(x, NC // devices)(x)
     got = swap(give, "domain", 1)
-    pieces = band_pieces(keep.shape[0], bands)(band.reshape(1), keep, got)
+    pieces = band_pieces(keep.shape[0], bands)(keep, got)
     total = pieces[0]
     for m in range(1, bands):
         total = total + swap(pieces[m], "band", m)
@@ -152,8 +145,7 @@
     excess = (heard[0] * (1.0 / NC)).astype(jnp.bfloat16)
     mine = [excess] + [swap(excess, "band", m) for m in range(1, bands)]
     other = [swap(e, "domain", 1) for e in mine]
-    place = jnp.stack([band, core])
-    out = correct(x, mine, bands)(place, x, *mine, *other)
+    out = correct(x, mine, bands)(x, *mine, *other)
     return lax.all_to_all(out, BOTH, split_axis=0, concat_axis=1, tiled=True)
 
 

time: 89.4 us -> 83.4 us (0.933)
  blocking collectives: 24.2 us -> 53.3 us
  waiting for transfers between devices: 35.9 us -> 13.8 us
  starting transfers between devices: 18.9 us -> 11.7 us
  local copies, waits for them, and re-layouts: 4.44 us -> 2.11 us
  Pallas kernels: 4.58 us -> 2.25 us
  other arithmetic: 1 us -> 0.04 us
    all_to_all x0 -> x1, blocking collectives: none -> 29.1 us  [full_rows(): x = lax.all_to_all(functions, BOTH, split_axis=1, concat_axis=0, tiled=True)]
    all_to_all x1 -> x0, waiting for transfers between devices: 22 us -> none  [full_rows(): x = lax.all_to_all(functions, BOTH, split_axis=1, concat_axis=0, tiled=True)]
    all_to_all x1 -> x0, starting transfers between devices: 7.3 us -> none  [full_rows(): x = lax.all_to_all(functions, BOTH, split_axis=1, concat_axis=0, tiled=True)]
    pallas_call x3, Pallas kernels: 4.58 us -> 2.25 us  [the longest x1 1.11 us: full_rows(): keep, give = gram_halves(x, NC // devices)(x)]
    unnamed x4 -> x0, local copies, waits for them, and re-layouts: 1.44 us -> none
  transfers between devices with their start and end apart: 15 -> 14, of which waited for: 10 -> 10; matrix products, arithmetic and copies ran while one was open for 0% -> 0% of each run, Pallas kernels for 0% -> 0%
where the time goes in v2:
time: 83.4 us; the launch traced here: 83.2 us
  blocking collectives  53.3 us (64%)
  waiting for transfers between devices  13.8 us (17%)
  starting transfers between devices  11.7 us (14%)
  Pallas kernels  2.25 us (3%)
  local copies, waits for them, and re-layouts  2.11 us (3%)
    all_to_all x1, blocking collectives, full_rows(): x = lax.all_to_all(functions, BOTH, split_axis=1, concat_axis=0, tiled=True)  29.1 us
    all_to_all x1, blocking collectives, full_rows(): return lax.all_to_all(out, BOTH, split_axis=0, concat_axis=1, tiled=True)  24.2 us
    ppermute x14, waiting for transfers between devices, swap(): return lax.ppermute(value, axis, [(i, i ^ mask) for i in range(count)])  13.8 us
    ppermute x14, starting transfers between devices, swap(): return lax.ppermute(value, axis, [(i, i ^ mask) for i in range(count)])  11.7 us
  transfers between devices with their start and end apart: 14, of which 10 were waited for; matrix products, arithmetic and copies ran while one was open for 0% of the time, Pallas kernels for 0%

profile of v2, /device:TPU:0, one launch (start us, length us, event | category | flops | bytes accessed | tf_op | source)
XLA Modules:
  0.0 83.2 jit_solution(16334896507198282941)
XLA Ops:
  0.0 1.2 %copy.7 = bf16[2,32,8,768]{3,2,0,1:T(8,128)(2,1)S(1)} copy(bf16[2,32,8,768]{3,2,1,0:T(8,128)(2,1)} %bitcast.16) | data formatting | bytes 1572864 | tf_op jit(solution)/shard_map/all_to_all | solution.py:134
  1.2 29.1 %all_to_all.38 = bf16[16,32,768]{2,0,1:T(8,128)(2,1)S(1)} all-to-all(bf16[16,32,768]{2,0,1:T(8,128)(2,1)S(1)} %bitcast.15), channel_id=1, replica_groups=mesh['band'=4,'domain'=8] {'band','domain'}, dimensions={1} | all-to-all | bytes 1572864 | tf_op jit(solution)/shard_map/all_to_all | solution.py:134
  30.3 1.1 %shard_map.17 = (f32[640,128]{1,0:T(8,128)S(1)}, f32[640,128]{1,0:T(8,128)S(1)}) custom-call(bf16[512,768]{1,0:T(8,128)(2,1)S(1)} %bitcast.11), custom_call_target="tpu_custom_call" | custom-call | tf_op jit(solution)/shard_map/pallas_call | solution.py:135
  31.4 0.1 collective-permute-start
  31.5 1.6 %collective-permute-done.got_ref = f32[640,128]{1,0:T(8,128)S(1)} collective-permute-done((f32[640,128]{1,0:T(8,128)S(1)}, f32[640,128]{1,0:T(8,128)S(1)}, u32[]{:S(2)}, u32[]{:S(2)}) %collective-permute-start) | collective-permute-done | bytes 327712 | tf_op jit(solution)/shard_map/ppermute | solution.py:24
  33.1 0.6 collective-permute-start.1
  33.7 0.6 collective-permute-start.2
  34.3 2.4 %collective-permute-start.3 = (f32[160,128]{1,0:T(8,128)S(1)}, f32[160,128]{1,0:T(8,128)S(1)}, u32[]{:S(2)}, u32[]{:S(2)}) collective-permute-start(f32[160,128]{1,0:T(8,128)S(1)} %get-tuple-element.16), channel_id=1, source_target_pairs={{0,24},{8,16},{16,8},{24,0},{1,25},{9,17},{17,9},{25,1},{2,26},{10... | collective-permute-start | bytes 245768 | tf_op jit(solution)/shard_map/ppermute | solution.py:24
  36.7 1.1 %collective-permute-done.1 = f32[160,128]{1,0:T(8,128)S(1)} collective-permute-done((f32[160,128]{1,0:T(8,128)S(1)}, f32[160,128]{1,0:T(8,128)S(1)}, u32[]{:S(2)}, u32[]{:S(2)}) %collective-permute-start.1) | collective-permute-done | bytes 81952 | tf_op jit(solution)/shard_map/ppermute | solution.py:24
  37.8 2.1 %collective-permute-done.2 = f32[160,128]{1,0:T(8,128)S(1)} collective-permute-done((f32[160,128]{1,0:T(8,128)S(1)}, f32[160,128]{1,0:T(8,128)S(1)}, u32[]{:S(2)}, u32[]{:S(2)}) %collective-permute-start.2) | collective-permute-done | bytes 81952 | tf_op jit(solution)/shard_map/ppermute | solution.py:24
  39.9 0.0 collective-permute-done.3
  39.9 1.7 %collective-permute-start.6 = (f32[160,128]{1,0:T(8,128)S(1)}, f32[160,128]{1,0:T(8,128)S(1)}, u32[]{:S(2)}, u32[]{:S(2)}) collective-permute-start(f32[160,128]{1,0:T(8,128)S(1)} %add_add_fusion), channel_id=1, source_target_pairs={{0,6},{1,7},{2,4},{3,5},{4,2},{5,3},{6,0},{7,1},{8,14},{9,15},{10,... | collective-permute-start | bytes 245768 | tf_op jit(solution)/shard_map/ppermute | solution.py:24
  41.6 0.0 collective-permute-start.5
  41.6 2.8 %collective-permute-start.4 = (f32[160,128]{1,0:T(8,128)S(1)}, f32[160,128]{1,0:T(8,128)S(1)}, u32[]{:S(2)}, u32[]{:S(2)}) collective-permute-start(f32[160,128]{1,0:T(8,128)S(1)} %add_add_fusion), channel_id=1, source_target_pairs={{0,2},{1,3},{2,0},{3,1},{4,6},{5,7},{6,4},{7,5},{8,10},{9,11},{10,... | collective-permute-start | bytes 245768 | tf_op jit(solution)/shard_map/ppermute | solution.py:24
  44.4 2.4 %collective-permute-done.6 = f32[160,128]{1,0:T(8,128)S(1)} collective-permute-done((f32[160,128]{1,0:T(8,128)S(1)}, f32[160,128]{1,0:T(8,128)S(1)}, u32[]{:S(2)}, u32[]{:S(2)}) %collective-permute-start.6) | collective-permute-done | bytes 81952 | tf_op jit(solution)/shard_map/ppermute | solution.py:24
  46.8 2.4 %collective-permute-done.5 = f32[160,128]{1,0:T(8,128)S(1)} collective-permute-done((f32[160,128]{1,0:T(8,128)S(1)}, f32[160,128]{1,0:T(8,128)S(1)}, u32[]{:S(2)}, u32[]{:S(2)}) %collective-permute-start.5) | collective-permute-done | bytes 81952 | tf_op jit(solution)/shard_map/ppermute | solution.py:24
  49.2 0.0 collective-permute-done.4
  49.2 1.3 %collective-permute-start.9 = (bf16[160,128]{1,0:T(8,128)(2,1)S(1)}, bf16[160,128]{1,0:T(8,128)(2,1)S(1)}, u32[]{:S(2)}, u32[]{:S(2)}) collective-permute-start(bf16[160,128]{1,0:T(8,128)(2,1)S(1)} %multiply_convert_fusion.refs_0_), channel_id=1, source_target_pairs={{0,24},{8,16},{16,8},{24,0},{1,25},{9,17},{17,9},{25,1},{2,26},{10... | collective-permute-start | bytes 122888 | tf_op jit(solution)/shard_map/ppermute | solution.py:24
  50.5 1.3 %collective-permute-start.8 = (bf16[160,128]{1,0:T(8,128)(2,1)S(1)}, bf16[160,128]{1,0:T(8,128)(2,1)S(1)}, u32[]{:S(2)}, u32[]{:S(2)}) collective-permute-start(bf16[160,128]{1,0:T(8,128)(2,1)S(1)} %multiply_convert_fusion.refs_0_), channel_id=1, source_target_pairs={{0,16},{8,24},{16,0},{24,8},{1,17},{9,25},{17,1},{25,9},{2,18},{10... | collective-permute-start | bytes 122888 | tf_op jit(solution)/shard_map/ppermute | solution.py:24
  51.8 1.0 %collective-permute-start.7 = (bf16[160,128]{1,0:T(8,128)(2,1)S(1)}, bf16[160,128]{1,0:T(8,128)(2,1)S(1)}, u32[]{:S(2)}, u32[]{:S(2)}) collective-permute-start(bf16[160,128]{1,0:T(8,128)(2,1)S(1)} %multiply_convert_fusion.refs_0_), channel_id=1, source_target_pairs={{0,8},{8,0},{16,24},{24,16},{1,9},{9,1},{17,25},{25,17},{2,10},{10... | collective-permute-start | bytes 122888 | tf_op jit(solution)/shard_map/ppermute | solution.py:24
  52.8 0.0 collective-permute-start.10
  52.8 1.4 %collective-permute-done.9.refs_3_ = bf16[160,128]{1,0:T(8,128)(2,1)S(1)} collective-permute-done((bf16[160,128]{1,0:T(8,128)(2,1)S(1)}, bf16[160,128]{1,0:T(8,128)(2,1)S(1)}, u32[]{:S(2)}, u32[]{:S(2)}) %collective-permute-start.9) | collective-permute-done | bytes 40992 | tf_op jit(solution)/shard_map/ppermute | solution.py:24
  54.2 0.0 collective-permute-start.13
  54.2 0.4 collective-permute-done.8.refs_2_
  54.6 0.1 collective-permute-start.12
  54.7 1.1 %collective-permute-done.7.refs_1_ = bf16[160,128]{1,0:T(8,128)(2,1)S(1)} collective-permute-done((bf16[160,128]{1,0:T(8,128)(2,1)S(1)}, bf16[160,128]{1,0:T(8,128)(2,1)S(1)}, u32[]{:S(2)}, u32[]{:S(2)}) %collective-permute-start.7) | collective-permute-done | bytes 40992 | tf_op jit(solution)/shard_map/ppermute | solution.py:24
  55.8 0.0 collective-permute-start.11
  55.8 0.1 collective-permute-done.12.refs_6_
  55.9 1.2 %collective-permute-done.11.refs_5_ = bf16[160,128]{1,0:T(8,128)(2,1)S(1)} collective-permute-done((bf16[160,128]{1,0:T(8,128)(2,1)S(1)}, bf16[160,128]{1,0:T(8,128)(2,1)S(1)}, u32[]{:S(2)}, u32[]{:S(2)}) %collective-permute-start.11) | collective-permute-done | bytes 40992 | tf_op jit(solution)/shard_map/ppermute | solution.py:24
  57.0 1.1 %shard_map.19 = bf16[512,768]{1,0:T(8,128)(2,1)S(1)} custom-call(bf16[512,768]{1,0:T(8,128)(2,1)S(1)} %bitcast.12, bf16[160,128]{1,0:T(8,128)(2,1)S(1)} %multiply_convert_fusion.refs_0_, bf16[160,128]{1,0:T(8,128)(2,1)S(1)} %collective-permute-done.7.refs_1_, bf16[160,128]{1,0:T(8,128)(2,1)S(1)} %collective-permute-done.8.refs_2_, ...), custom_call_target="tpu_custom_call" | custom-call | tf_op jit(solution)/shard_map/pallas_call | solution.py:148
  58.1 24.2 %all_to_all.39 = bf16[32,16,768]{2,1,0:T(8,128)(2,1)S(1)} all-to-all(bf16[32,16,768]{2,1,0:T(8,128)(2,1)S(1)} %bitcast.13), channel_id=1, replica_groups=mesh['band'=4,'domain'=8] {'band','domain'}, dimensions={0} | all-to-all | bytes 1572864 | tf_op jit(solution)/shard_map/all_to_all | solution.py:149
  82.3 0.9 %copy.5 = bf16[32,2,8,768]{3,2,0,1:T(8,128)(2,1)} copy(bf16[32,2,8,768]{3,2,1,0:T(8,128)(2,1)S(1)} %bitcast.14) | data formatting | bytes 1572864 | tf_op jit(solution)/shard_map/all_to_all | solution.py:149
  (5 shorter events, 0.1 us)
Async XLA Ops:
  31.4 1.7 %collective-permute-start = (f32[640,128]{1,0:T(8,128)S(1)}, f32[640,128]{1,0:T(8,128)S(1)}, u32[]{:S(2)}, u32[]{:S(2)}) collective-permute-start(f32[640,128]{1,0:T(8,128)S(1)} %get-tuple-element.12), channel_id=1, source_target_pairs={{0,1},{1,0},{2,3},{3,2},{4,5},{5,4},{6,7},{7,6},{8,9},{9,8},{10,11... | collective-permute-start | bytes 983048 | tf_op jit(solution)/shard_map/ppermute | solution.py:24
  33.1 4.7 %collective-permute-start.1 = (f32[160,128]{1,0:T(8,128)S(1)}, f32[160,128]{1,0:T(8,128)S(1)}, u32[]{:S(2)}, u32[]{:S(2)}) collective-permute-start(f32[160,128]{1,0:T(8,128)S(1)} %get-tuple-element.14), channel_id=1, source_target_pairs={{0,8},{8,0},{16,24},{24,16},{1,9},{9,1},{17,25},{25,17},{2,10},{10... | collective-permute-start | bytes 245768 | tf_op jit(solution)/shard_map/ppermute | solution.py:24
  33.7 6.2 %collective-permute-start.2 = (f32[160,128]{1,0:T(8,128)S(1)}, f32[160,128]{1,0:T(8,128)S(1)}, u32[]{:S(2)}, u32[]{:S(2)}) collective-permute-start(f32[160,128]{1,0:T(8,128)S(1)} %get-tuple-element.15), channel_id=1, source_target_pairs={{0,16},{8,24},{16,0},{24,8},{1,17},{9,25},{17,1},{25,9},{2,18},{10... | collective-permute-start | bytes 245768 | tf_op jit(solution)/shard_map/ppermute | solution.py:24
  34.3 5.6 %collective-permute-start.3 = (f32[160,128]{1,0:T(8,128)S(1)}, f32[160,128]{1,0:T(8,128)S(1)}, u32[]{:S(2)}, u32[]{:S(2)}) collective-permute-start(f32[160,128]{1,0:T(8,128)S(1)} %get-tuple-element.16), channel_id=1, source_target_pairs={{0,24},{8,16},{16,8},{24,0},{1,25},{9,17},{17,9},{25,1},{2,26},{10... | collective-permute-start | bytes 245768 | tf_op jit(solution)/shard_map/ppermute | solution.py:24
  39.9 6.9 %collective-permute-start.6 = (f32[160,128]{1,0:T(8,128)S(1)}, f32[160,128]{1,0:T(8,128)S(1)}, u32[]{:S(2)}, u32[]{:S(2)}) collective-permute-start(f32[160,128]{1,0:T(8,128)S(1)} %add_add_fusion), channel_id=1, source_target_pairs={{0,6},{1,7},{2,4},{3,5},{4,2},{5,3},{6,0},{7,1},{8,14},{9,15},{10,... | collective-permute-start | bytes 245768 | tf_op jit(solution)/shard_map/ppermute | solution.py:24
  41.6 7.6 %collective-permute-start.5 = (f32[160,128]{1,0:T(8,128)S(1)}, f32[160,128]{1,0:T(8,128)S(1)}, u32[]{:S(2)}, u32[]{:S(2)}) collective-permute-start(f32[160,128]{1,0:T(8,128)S(1)} %add_add_fusion), channel_id=1, source_target_pairs={{0,4},{1,5},{2,6},{3,7},{4,0},{5,1},{6,2},{7,3},{8,12},{9,13},{10,... | collective-permute-start | bytes 245768 | tf_op jit(solution)/shard_map/ppermute | solution.py:24
  41.6 7.6 %collective-permute-start.4 = (f32[160,128]{1,0:T(8,128)S(1)}, f32[160,128]{1,0:T(8,128)S(1)}, u32[]{:S(2)}, u32[]{:S(2)}) collective-permute-start(f32[160,128]{1,0:T(8,128)S(1)} %add_add_fusion), channel_id=1, source_target_pairs={{0,2},{1,3},{2,0},{3,1},{4,6},{5,7},{6,4},{7,5},{8,10},{9,11},{10,... | collective-permute-start | bytes 245768 | tf_op jit(solution)/shard_map/ppermute | solution.py:24
  49.2 5.0 %collective-permute-start.9 = (bf16[160,128]{1,0:T(8,128)(2,1)S(1)}, bf16[160,128]{1,0:T(8,128)(2,1)S(1)}, u32[]{:S(2)}, u32[]{:S(2)}) collective-permute-start(bf16[160,128]{1,0:T(8,128)(2,1)S(1)} %multiply_convert_fusion.refs_0_), channel_id=1, source_target_pairs={{0,24},{8,16},{16,8},{24,0},{1,25},{9,17},{17,9},{25,1},{2,26},{10... | collective-permute-start | bytes 122888 | tf_op jit(solution)/shard_map/ppermute | solution.py:24
  50.5 4.1 %collective-permute-start.8 = (bf16[160,128]{1,0:T(8,128)(2,1)S(1)}, bf16[160,128]{1,0:T(8,128)(2,1)S(1)}, u32[]{:S(2)}, u32[]{:S(2)}) collective-permute-start(bf16[160,128]{1,0:T(8,128)(2,1)S(1)} %multiply_convert_fusion.refs_0_), channel_id=1, source_target_pairs={{0,16},{8,24},{16,0},{24,8},{1,17},{9,25},{17,1},{25,9},{2,18},{10... | collective-permute-start | bytes 122888 | tf_op jit(solution)/shard_map/ppermute | solution.py:24
  51.8 4.0 %collective-permute-start.7 = (bf16[160,128]{1,0:T(8,128)(2,1)S(1)}, bf16[160,128]{1,0:T(8,128)(2,1)S(1)}, u32[]{:S(2)}, u32[]{:S(2)}) collective-permute-start(bf16[160,128]{1,0:T(8,128)(2,1)S(1)} %multiply_convert_fusion.refs_0_), channel_id=1, source_target_pairs={{0,8},{8,0},{16,24},{24,16},{1,9},{9,1},{17,25},{25,17},{2,10},{10... | collective-permute-start | bytes 122888 | tf_op jit(solution)/shard_map/ppermute | solution.py:24
  52.8 3.0 %collective-permute-start.10 = (bf16[160,128]{1,0:T(8,128)(2,1)S(1)}, bf16[160,128]{1,0:T(8,128)(2,1)S(1)}, u32[]{:S(2)}, u32[]{:S(2)}) collective-permute-start(bf16[160,128]{1,0:T(8,128)(2,1)S(1)} %multiply_convert_fusion.refs_0_), channel_id=1, source_target_pairs={{0,1},{1,0},{2,3},{3,2},{4,5},{5,4},{6,7},{7,6},{8,9},{9,8},{10,11... | collective-permute-start | bytes 122888 | tf_op jit(solution)/shard_map/ppermute | solution.py:24
  54.2 1.6 %collective-permute-start.13 = (bf16[160,128]{1,0:T(8,128)(2,1)S(1)}, bf16[160,128]{1,0:T(8,128)(2,1)S(1)}, u32[]{:S(2)}, u32[]{:S(2)}) collective-permute-start(bf16[160,128]{1,0:T(8,128)(2,1)S(1)} %collective-permute-done.9.refs_3_), channel_id=1, source_target_pairs={{0,1},{1,0},{2,3},{3,2},{4,5},{5,4},{6,7},{7,6},{8,9},{9,8},{10,11... | collective-permute-start | bytes 122888 | tf_op jit(solution)/shard_map/ppermute | solution.py:24
  54.6 1.2 %collective-permute-start.12 = (bf16[160,128]{1,0:T(8,128)(2,1)S(1)}, bf16[160,128]{1,0:T(8,128)(2,1)S(1)}, u32[]{:S(2)}, u32[]{:S(2)}) collective-permute-start(bf16[160,128]{1,0:T(8,128)(2,1)S(1)} %collective-permute-done.8.refs_2_), channel_id=1, source_target_pairs={{0,1},{1,0},{2,3},{3,2},{4,5},{5,4},{6,7},{7,6},{8,9},{9,8},{10,11... | collective-permute-start | bytes 122888 | tf_op jit(solution)/shard_map/ppermute | solution.py:24
  55.8 1.2 %collective-permute-start.11 = (bf16[160,128]{1,0:T(8,128)(2,1)S(1)}, bf16[160,128]{1,0:T(8,128)(2,1)S(1)}, u32[]{:S(2)}, u32[]{:S(2)}) collective-permute-start(bf16[160,128]{1,0:T(8,128)(2,1)S(1)} %collective-permute-done.7.refs_1_), channel_id=1, source_target_pairs={{0,1},{1,0},{2,3},{3,2},{4,5},{5,4},{6,7},{7,6},{8,9},{9,8},{10,11... | collective-permute-start | bytes 122888 | tf_op jit(solution)/shard_map/ppermute | solution.py:24

commit v3 on v0

--- a/solution.py
+++ b/solution.py
@@ -1,10 +1,181 @@
+import functools
+
 import jax
 import jax.numpy as jnp
 from jax import lax
+from jax.experimental import pallas as pl
+from jax.experimental.pallas import tpu as pltpu
 from jax.sharding import PartitionSpec as P
 
 NC = 24576
 BLOCK = 128
+BOTH = ("band", "domain")
+
+
+VMEM_LIMIT = pltpu.CompilerParams(vmem_limit_bytes=16 * 1024 * 1024)
+
+
+def my_core():
+    return lax.rem(lax.axis_index("domain"), 2)
+
+
+def swap(value, axis, mask):
+    count = lax.axis_size(axis)
+    return lax.ppermute(value, axis, [(i, i ^ mask) for i in range(count)])
+
+
+ACROSS = (((1,), (1,)), ((), ()))
+
+
+def upper_blocks(count):
+    return [(i, j) for i in range(count) for j in range(i, count)]
+
+
+def own_gram(rows, width, share):
+    count = rows // BLOCK
+
+    def body(x_ref, out_ref):
+        eye = (
+            lax.broadcasted_iota(jnp.int32, (BLOCK, BLOCK), 0) == lax.broadcasted_iota(jnp.int32, (BLOCK, BLOCK), 1)
+        ).astype(jnp.float32) * share
+        got = lax.dot_general(x_ref[...], x_ref[...], ACROSS, preferred_element_type=jnp.float32)
+        for p, (i, j) in enumerate(upper_blocks(count)):
+            block = got[i * BLOCK:(i + 1) * BLOCK, j * BLOCK:(j + 1) * BLOCK]
+            out_ref[p * BLOCK:(p + 1) * BLOCK, :] = block - eye if i == j else block
+
+    stacked = count * (count + 1) // 2 * BLOCK
+    return pl.pallas_call(
+        body,
+        out_shape=jax.ShapeDtypeStruct((stacked, BLOCK), jnp.float32),
+        compiler_params=VMEM_LIMIT,
+        cost_estimate=pl.CostEstimate(
+            flops=2 * rows * rows * width, bytes_accessed=2 * rows * width, transcendentals=0
+        ),
+    )
+
+
+def cross_gram(rows, width, bands):
+    count = rows // BLOCK
+    upper = count * (count + 1) // 2 * BLOCK
+    mid = rows // 2
+    stacked = upper + mid * count
+    piece = stacked // bands
+
+    def body(x_ref, y_ref, own_ref, *refs):
+        piece_refs, stack = refs[:-1], refs[-1]
+        core, band = my_core(), lax.axis_index("band")
+        stack[0:upper, :] = own_ref[...]
+
+        def put(left, right):
+            got = lax.dot_general(left, right, ACROSS, preferred_element_type=jnp.float32)
+            for j in range(count):
+                stack[upper + j * mid:upper + (j + 1) * mid, :] = got[:, j * BLOCK:(j + 1) * BLOCK]
+
+        @pl.when(core == 0)
+        def _():
+            put(x_ref[0:mid, :], y_ref[...])
+
+        @pl.when(core == 1)
+        def _():
+            put(y_ref[mid:rows, :], x_ref[...])
+
+        for m in range(bands):
+            at = pl.ds(pl.multiple_of((band ^ m) * piece, piece), piece)
+            piece_refs[m][...] = stack[at, :]
+
+    return pl.pallas_call(
+        body,
+        out_shape=tuple(jax.ShapeDtypeStruct((piece, BLOCK), jnp.float32) for _ in range(bands)),
+        scratch_shapes=[pltpu.VMEM((stacked, BLOCK), jnp.float32)],
+        compiler_params=VMEM_LIMIT,
+        cost_estimate=pl.CostEstimate(
+            flops=rows * rows * width, bytes_accessed=4 * rows * width, transcendentals=0
+        ),
+    )
+
+
+def correct(rows, width, bands):
+    count = rows // BLOCK
+    upper = count * (count + 1) // 2 * BLOCK
+    mid = rows // 2
+    stacked = upper + mid * count
+    piece = stacked // bands
+
+    def body(x_ref, y_ref, *refs):
+        piece_refs, out_ref, packed, excess = refs[:-3], refs[-3], refs[-2], refs[-1]
+        band, core = lax.axis_index("band"), my_core()
+        for side in range(2):
+            for m in range(bands):
+                start = side * stacked + (band ^ m) * piece
+                packed[pl.ds(pl.multiple_of(start, 16), piece), :] = piece_refs[side * bands + m][...]
+        for side in range(2):
+            for p, (i, j) in enumerate(upper_blocks(count)):
+                at = side * stacked + p * BLOCK
+                block = packed[at:at + BLOCK, :]
+                row, column = side * rows + i * BLOCK, side * rows + j * BLOCK
+                excess[row:row + BLOCK, column:column + BLOCK] = block
+                if i != j:
+                    excess[column:column + BLOCK, row:row + BLOCK] = block.T
+        for part in range(2):
+            for j in range(count):
+                start = (part ^ core) * stacked + upper + j * mid
+                block = packed[pl.ds(pl.multiple_of(start, 16), mid), :]
+                row, column = part * mid, j * BLOCK
+
+                @pl.when(core == 0)
+                def _():
+                    excess[row:row + mid, rows + column:rows + column + BLOCK] = block
+                    excess[rows + column:rows + column + BLOCK, row:row + mid] = block.T
+
+                @pl.when(core == 1)
+                def _():
+                    excess[rows + row:rows + row + mid, column:column + BLOCK] = block
+                    excess[column:column + BLOCK, rows + row:rows + row + mid] = block.T
+
+        own = excess[0:rows, :]
+        twice = jnp.dot(own, excess[...], preferred_element_type=jnp.float32)
+        change = (0.375 * twice - 0.5 * own.astype(jnp.float32)).astype(jnp.bfloat16)
+        out = x_ref[...].astype(jnp.float32)
+        out += jnp.dot(change[:, 0:rows], x_ref[...], preferred_element_type=jnp.float32)
+        out += jnp.dot(change[:, rows:2 * rows], y_ref[...], preferred_element_type=jnp.float32)
+        out_ref[...] = out.astype(jnp.bfloat16)
+
+    return pl.pallas_call(
+        body,
+        out_shape=jax.ShapeDtypeStruct((rows, width), jnp.bfloat16),
+        scratch_shapes=[
+            pltpu.VMEM((2 * stacked, BLOCK), jnp.bfloat16),
+            pltpu.VMEM((2 * rows, 2 * rows), jnp.bfloat16),
+        ],
+        compiler_params=VMEM_LIMIT,
+    )
+
+
+def full_rows(functions, pattern):
+    bands, domains = lax.axis_size("band"), lax.axis_size("domain")
+    devices, levels = bands * domains, domains // 2
+    chips = devices // 2
+    fdev, ncoef = functions.shape
+    tall, width = fdev // 2, ncoef // chips
+    rows = devices * tall
+    order = [[b * domains + 2 * z + c for c in range(2) for b in range(bands) for z in range(levels)]]
+    cut = functions.reshape(2, tall, chips, width).transpose(0, 2, 1, 3).reshape(devices, tall, width)
+    x = lax.all_to_all(cut, BOTH, split_axis=0, concat_axis=0, axis_index_groups=order).reshape(rows, width)
+    y = swap(x, "domain", 1)
+    own = own_gram(rows, width, NC // chips)(x)
+    pieces = cross_gram(rows, width, bands)(x, y, own)
+    total = pieces[0]
+    for m in range(1, bands):
+        total = total + swap(pieces[m], "band", m)
+    heard = [total] + [swap(total, "domain", 2 * m) for m in range(1, levels)]
+    while len(heard) > 1:
+        heard = [heard[k] + heard[k + 1] for k in range(0, len(heard), 2)]
+    excess = (heard[0] * (1.0 / NC)).astype(jnp.bfloat16)
+    mine = [excess] + [swap(excess, "band", m) for m in range(1, bands)]
+    other = [swap(e, "domain", 1) for e in mine]
+    out = correct(rows, width, bands)(x, y, *mine, *other).reshape(devices, tall, width)
+    back = lax.all_to_all(out, BOTH, split_axis=0, concat_axis=0, axis_index_groups=order)
+    return back.reshape(2, chips, tall, width).transpose(0, 2, 1, 3).reshape(fdev, ncoef)
 
 
 def apply_blocks(excess, block_index, source_blocks):
@@ -12,7 +183,7 @@
     return jnp.einsum("bkij,bkjc->bic", excess, picked, preferred_element_type=jnp.float32)
 
 
-def per_device(functions, pattern):
+def some_rows(functions, pattern):
     domains = lax.axis_size("domain")
     fdev = functions.shape[0]
     my_band = lax.axis_index("band")
@@ -44,12 +215,17 @@
     return lax.all_to_all(updated, "domain", split_axis=0, concat_axis=1, tiled=True)
 
 
+def per_device(functions, pattern):
+    nblocks, nonzero = pattern.shape
+    return (full_rows if nonzero == nblocks else some_rows)(functions, pattern)
+
+
 def solution(mesh):
-    placed = (P(("band", "domain"), None), P())
+    placed = (P(BOTH, None), P())
     return jax.shard_map(
         per_device,
         mesh=mesh,
         in_specs=placed,
-        out_specs=P(("band", "domain"), None),
+        out_specs=P(BOTH, None),
         check_vma=False,
     )

time: 223 us -> 82.3 us (0.37)
  waiting for transfers between devices: 140 us -> 14.3 us
  between operations: 13.2 us -> 0.05 us
  starting transfers between devices: 0.09 us -> 11.6 us
  matrix products: 8.34 us -> 0 us
  local copies, waits for them, and re-layouts: 7.44 us -> 0.88 us
    all_gather x2 -> x0, waiting for transfers between devices: 85.4 us -> none  [the longest x1 43.1 us: per_device(): all_first = lax.all_gather(first_half, 'band', axis=0, tiled=True)]
    psum x1 -> x0, waiting for transfers between devices: 55 us -> none  [per_device(): total = lax.psum(partial_sums, 'domain') * (1.0 / NC)]
    ppermute x0 -> x14, waiting for transfers between devices: none -> 14.3 us  [swap(): return lax.ppermute(value, axis, [(i, i ^ mask) for i in range(count)])]
    ppermute x0 -> x14, starting transfers between devices: none -> 11.6 us  [swap(): return lax.ppermute(value, axis, [(i, i ^ mask) for i in range(count)])]
    dot_general x3 -> x0, matrix products: 8.34 us -> none  [the longest x2 5.49 us: apply_blocks(): jnp.einsum('bkij,bkjc->bic', excess, picked, preferred_element_type=jnp.f...]
    gather x2 -> x0, local copies, waits for them, and re-layouts: 5.32 us -> none  [the longest x1 2.68 us: apply_blocks(): picked = jnp.take(source_blocks, block_index, axis=0)]
  transfers between devices with their start and end apart: 3 -> 14, of which waited for: 3 -> 10; matrix products, arithmetic and copies ran while one was open for 0% -> 0% of each run, Pallas kernels for 0% -> 0%
where the time goes in v3:
time: 82.3 us; the launch traced here: 82.1 us
  blocking collectives  53.2 us (65%)
  waiting for transfers between devices  14.3 us (17%)
  starting transfers between devices  11.6 us (14%)
  Pallas kernels  2.02 us (2%)
  local copies, waits for them, and re-layouts  0.88 us (1%)
    all_to_all x1, blocking collectives, full_rows(): lax.all_to_all(cut, BOTH, split_axis=0, concat_axis=0, axis_index_groups=...  28.6 us
    all_to_all x1, blocking collectives, full_rows(): lax.all_to_all(out, BOTH, split_axis=0, concat_axis=0, axis_index_groups=...  24.6 us
    ppermute x14, waiting for transfers between devices, swap(): return lax.ppermute(value, axis, [(i, i ^ mask) for i in range(count)])  14.3 us
    ppermute x14, starting transfers between devices, swap(): return lax.ppermute(value, axis, [(i, i ^ mask) for i in range(count)])  11.6 us
  transfers between devices with their start and end apart: 14, of which 10 were waited for; matrix products, arithmetic and copies ran while one was open for 0% of the time, Pallas kernels for 0%

profile of v3, /device:TPU:0, one launch (start us, length us, event | category | flops | bytes accessed | tf_op | source)
XLA Modules:
  0.0 82.1 jit_solution(5608552108476887935)
XLA Ops:
  0.0 28.6 %all_to_all.10 = bf16[32,8,1536]{2,1,0:T(8,128)(2,1)S(1)} all-to-all(bf16[32,8,1536]{2,1,0:T(8,128)(2,1)} %bitcast.18), channel_id=1, replica_groups={{0,2,4,6,8,10,12,14,16,18,20,22,24,26,28,30,1,3,5,7,9,11,13,15,17,19,21..., dimensions={0} | all-to-all | bytes 1572864 | tf_op jit(solution)/shard_map/all_to_all | solution.py:163
  28.6 0.0 collective-permute-start
  28.6 0.4 shard_map.17.own_ref
  29.1 1.9 %collective-permute-done.y_ref = bf16[256,1536]{1,0:T(8,128)(2,1)S(1)} collective-permute-done((bf16[256,1536]{1,0:T(8,128)(2,1)S(1)}, bf16[256,1536]{1,0:T(8,128)(2,1)S(1)}, u32[]{:S(2)}, u32[]{:S(2)}) %collective-permute-start) | collective-permute-done | bytes 786464 | tf_op jit(solution)/shard_map/ppermute | solution.py:24
  30.9 0.4 shard_map.18
  31.4 1.5 %collective-permute-start.1 = (f32[160,128]{1,0:T(8,128)S(1)}, f32[160,128]{1,0:T(8,128)S(1)}, u32[]{:S(2)}, u32[]{:S(2)}) collective-permute-start(f32[160,128]{1,0:T(8,128)S(1)} %get-tuple-element.10), channel_id=1, source_target_pairs={{0,8},{8,0},{16,24},{24,16},{1,9},{9,1},{17,25},{25,17},{2,10},{10... | collective-permute-start | bytes 245768 | tf_op jit(solution)/shard_map/ppermute | solution.py:24
  32.8 0.1 collective-permute-start.2
  32.9 2.0 %collective-permute-start.3 = (f32[160,128]{1,0:T(8,128)S(1)}, f32[160,128]{1,0:T(8,128)S(1)}, u32[]{:S(2)}, u32[]{:S(2)}) collective-permute-start(f32[160,128]{1,0:T(8,128)S(1)} %get-tuple-element.12), channel_id=1, source_target_pairs={{0,24},{8,16},{16,8},{24,0},{1,25},{9,17},{17,9},{25,1},{2,26},{10... | collective-permute-start | bytes 245768 | tf_op jit(solution)/shard_map/ppermute | solution.py:24
  34.9 1.0 %collective-permute-done.1 = f32[160,128]{1,0:T(8,128)S(1)} collective-permute-done((f32[160,128]{1,0:T(8,128)S(1)}, f32[160,128]{1,0:T(8,128)S(1)}, u32[]{:S(2)}, u32[]{:S(2)}) %collective-permute-start.1) | collective-permute-done | bytes 81952 | tf_op jit(solution)/shard_map/ppermute | solution.py:24
  35.9 3.0 %collective-permute-done.2 = f32[160,128]{1,0:T(8,128)S(1)} collective-permute-done((f32[160,128]{1,0:T(8,128)S(1)}, f32[160,128]{1,0:T(8,128)S(1)}, u32[]{:S(2)}, u32[]{:S(2)}) %collective-permute-start.2) | collective-permute-done | bytes 81952 | tf_op jit(solution)/shard_map/ppermute | solution.py:24
  38.9 0.0 collective-permute-done.3
  38.9 1.4 %collective-permute-start.6 = (f32[160,128]{1,0:T(8,128)S(1)}, f32[160,128]{1,0:T(8,128)S(1)}, u32[]{:S(2)}, u32[]{:S(2)}) collective-permute-start(f32[160,128]{1,0:T(8,128)S(1)} %add_add_fusion), channel_id=1, source_target_pairs={{0,6},{1,7},{2,4},{3,5},{4,2},{5,3},{6,0},{7,1},{8,14},{9,15},{10,... | collective-permute-start | bytes 245768 | tf_op jit(solution)/shard_map/ppermute | solution.py:24
  40.3 0.8 collective-permute-start.5
  41.1 2.3 %collective-permute-start.4 = (f32[160,128]{1,0:T(8,128)S(1)}, f32[160,128]{1,0:T(8,128)S(1)}, u32[]{:S(2)}, u32[]{:S(2)}) collective-permute-start(f32[160,128]{1,0:T(8,128)S(1)} %add_add_fusion), channel_id=1, source_target_pairs={{0,2},{1,3},{2,0},{3,1},{4,6},{5,7},{6,4},{7,5},{8,10},{9,11},{10,... | collective-permute-start | bytes 245768 | tf_op jit(solution)/shard_map/ppermute | solution.py:24
  43.4 2.7 %collective-permute-done.6 = f32[160,128]{1,0:T(8,128)S(1)} collective-permute-done((f32[160,128]{1,0:T(8,128)S(1)}, f32[160,128]{1,0:T(8,128)S(1)}, u32[]{:S(2)}, u32[]{:S(2)}) %collective-permute-start.6) | collective-permute-done | bytes 81952 | tf_op jit(solution)/shard_map/ppermute | solution.py:24
  46.1 1.7 %collective-permute-done.5 = f32[160,128]{1,0:T(8,128)S(1)} collective-permute-done((f32[160,128]{1,0:T(8,128)S(1)}, f32[160,128]{1,0:T(8,128)S(1)}, u32[]{:S(2)}, u32[]{:S(2)}) %collective-permute-start.5) | collective-permute-done | bytes 81952 | tf_op jit(solution)/shard_map/ppermute | solution.py:24
  47.8 0.0 collective-permute-done.4
  47.9 1.8 %collective-permute-start.9 = (bf16[160,128]{1,0:T(8,128)(2,1)S(1)}, bf16[160,128]{1,0:T(8,128)(2,1)S(1)}, u32[]{:S(2)}, u32[]{:S(2)}) collective-permute-start(bf16[160,128]{1,0:T(8,128)(2,1)S(1)} %multiply_convert_fusion.refs_0_), channel_id=1, source_target_pairs={{0,24},{8,16},{16,8},{24,0},{1,25},{9,17},{17,9},{25,1},{2,26},{10... | collective-permute-start | bytes 122888 | tf_op jit(solution)/shard_map/ppermute | solution.py:24
  49.7 0.6 collective-permute-start.8
  50.2 1.2 %collective-permute-start.7 = (bf16[160,128]{1,0:T(8,128)(2,1)S(1)}, bf16[160,128]{1,0:T(8,128)(2,1)S(1)}, u32[]{:S(2)}, u32[]{:S(2)}) collective-permute-start(bf16[160,128]{1,0:T(8,128)(2,1)S(1)} %multiply_convert_fusion.refs_0_), channel_id=1, source_target_pairs={{0,8},{8,0},{16,24},{24,16},{1,9},{9,1},{17,25},{25,17},{2,10},{10... | collective-permute-start | bytes 122888 | tf_op jit(solution)/shard_map/ppermute | solution.py:24
  51.4 0.0 collective-permute-start.10
  51.4 1.5 %collective-permute-done.9.refs_3_ = bf16[160,128]{1,0:T(8,128)(2,1)S(1)} collective-permute-done((bf16[160,128]{1,0:T(8,128)(2,1)S(1)}, bf16[160,128]{1,0:T(8,128)(2,1)S(1)}, u32[]{:S(2)}, u32[]{:S(2)}) %collective-permute-start.9) | collective-permute-done | bytes 40992 | tf_op jit(solution)/shard_map/ppermute | solution.py:24
  52.9 0.0 collective-permute-start.13
  52.9 0.8 collective-permute-done.8.refs_2_
  53.7 0.0 collective-permute-start.12
  53.7 0.6 collective-permute-done.7.refs_1_
  54.2 0.0 collective-permute-start.11
  54.3 0.7 collective-permute-done.12.refs_6_
  54.9 0.6 collective-permute-done.11.refs_5_
  55.5 1.2 %shard_map.19 = bf16[256,1536]{1,0:T(8,128)(2,1)S(1)} custom-call(bf16[256,1536]{1,0:T(8,128)(2,1)S(1)} %bitcast.15, bf16[256,1536]{1,0:T(8,128)(2,1)S(1)} %collective-permute-done.y_ref, bf16[160,128]{1,0:T(8,128)(2,1)S(1)} %multiply_convert_fusion.refs_0_, bf16[160,128]{1,0:T(8,128)(2,1)S(1)} %collective-permute-done.7.refs_1_, ...), custom_call_target="tpu_custom_call" | custom-call | tf_op jit(solution)/shard_map/pallas_call | solution.py:176
  56.7 24.6 %all_to_all.11 = bf16[32,8,1536]{2,1,0:T(8,128)(2,1)S(1)} all-to-all(bf16[32,8,1536]{2,1,0:T(8,128)(2,1)S(1)} %bitcast.16), channel_id=1, replica_groups={{0,2,4,6,8,10,12,14,16,18,20,22,24,26,28,30,1,3,5,7,9,11,13,15,17,19,21..., dimensions={0} | all-to-all | bytes 1572864 | tf_op jit(solution)/shard_map/all_to_all | solution.py:177
  81.2 0.9 %copy.3 = bf16[16,24576]{1,0:T(8,128)(2,1)} copy(bf16[16,24576]{1,0:T(8,128)(2,1)S(1)} %bitcast.17) | data formatting | bytes 1572864
  (4 shorter events, 0.0 us)
Async XLA Ops:
  28.6 2.3 %collective-permute-start = (bf16[256,1536]{1,0:T(8,128)(2,1)S(1)}, bf16[256,1536]{1,0:T(8,128)(2,1)S(1)}, u32[]{:S(2)}, u32[]{:S(2)}) collective-permute-start(bf16[256,1536]{1,0:T(8,128)(2,1)S(1)} %bitcast.12), channel_id=1, source_target_pairs={{0,1},{1,0},{2,3},{3,2},{4,5},{5,4},{6,7},{7,6},{8,9},{9,8},{10,11... | collective-permute-start | bytes 2359304 | tf_op jit(solution)/shard_map/ppermute | solution.py:24
  31.4 4.5 %collective-permute-start.1 = (f32[160,128]{1,0:T(8,128)S(1)}, f32[160,128]{1,0:T(8,128)S(1)}, u32[]{:S(2)}, u32[]{:S(2)}) collective-permute-start(f32[160,128]{1,0:T(8,128)S(1)} %get-tuple-element.10), channel_id=1, source_target_pairs={{0,8},{8,0},{16,24},{24,16},{1,9},{9,1},{17,25},{25,17},{2,10},{10... | collective-permute-start | bytes 245768 | tf_op jit(solution)/shard_map/ppermute | solution.py:24
  32.8 6.1 %collective-permute-start.2 = (f32[160,128]{1,0:T(8,128)S(1)}, f32[160,128]{1,0:T(8,128)S(1)}, u32[]{:S(2)}, u32[]{:S(2)}) collective-permute-start(f32[160,128]{1,0:T(8,128)S(1)} %get-tuple-element.11), channel_id=1, source_target_pairs={{0,16},{8,24},{16,0},{24,8},{1,17},{9,25},{17,1},{25,9},{2,18},{10... | collective-permute-start | bytes 245768 | tf_op jit(solution)/shard_map/ppermute | solution.py:24
  32.9 6.0 %collective-permute-start.3 = (f32[160,128]{1,0:T(8,128)S(1)}, f32[160,128]{1,0:T(8,128)S(1)}, u32[]{:S(2)}, u32[]{:S(2)}) collective-permute-start(f32[160,128]{1,0:T(8,128)S(1)} %get-tuple-element.12), channel_id=1, source_target_pairs={{0,24},{8,16},{16,8},{24,0},{1,25},{9,17},{17,9},{25,1},{2,26},{10... | collective-permute-start | bytes 245768 | tf_op jit(solution)/shard_map/ppermute | solution.py:24
  38.9 7.2 %collective-permute-start.6 = (f32[160,128]{1,0:T(8,128)S(1)}, f32[160,128]{1,0:T(8,128)S(1)}, u32[]{:S(2)}, u32[]{:S(2)}) collective-permute-start(f32[160,128]{1,0:T(8,128)S(1)} %add_add_fusion), channel_id=1, source_target_pairs={{0,6},{1,7},{2,4},{3,5},{4,2},{5,3},{6,0},{7,1},{8,14},{9,15},{10,... | collective-permute-start | bytes 245768 | tf_op jit(solution)/shard_map/ppermute | solution.py:24
  40.3 7.5 %collective-permute-start.5 = (f32[160,128]{1,0:T(8,128)S(1)}, f32[160,128]{1,0:T(8,128)S(1)}, u32[]{:S(2)}, u32[]{:S(2)}) collective-permute-start(f32[160,128]{1,0:T(8,128)S(1)} %add_add_fusion), channel_id=1, source_target_pairs={{0,4},{1,5},{2,6},{3,7},{4,0},{5,1},{6,2},{7,3},{8,12},{9,13},{10,... | collective-permute-start | bytes 245768 | tf_op jit(solution)/shard_map/ppermute | solution.py:24
  41.1 6.7 %collective-permute-start.4 = (f32[160,128]{1,0:T(8,128)S(1)}, f32[160,128]{1,0:T(8,128)S(1)}, u32[]{:S(2)}, u32[]{:S(2)}) collective-permute-start(f32[160,128]{1,0:T(8,128)S(1)} %add_add_fusion), channel_id=1, source_target_pairs={{0,2},{1,3},{2,0},{3,1},{4,6},{5,7},{6,4},{7,5},{8,10},{9,11},{10,... | collective-permute-start | bytes 245768 | tf_op jit(solution)/shard_map/ppermute | solution.py:24
  47.9 5.1 %collective-permute-start.9 = (bf16[160,128]{1,0:T(8,128)(2,1)S(1)}, bf16[160,128]{1,0:T(8,128)(2,1)S(1)}, u32[]{:S(2)}, u32[]{:S(2)}) collective-permute-start(bf16[160,128]{1,0:T(8,128)(2,1)S(1)} %multiply_convert_fusion.refs_0_), channel_id=1, source_target_pairs={{0,24},{8,16},{16,8},{24,0},{1,25},{9,17},{17,9},{25,1},{2,26},{10... | collective-permute-start | bytes 122888 | tf_op jit(solution)/shard_map/ppermute | solution.py:24
  49.7 4.0 %collective-permute-start.8 = (bf16[160,128]{1,0:T(8,128)(2,1)S(1)}, bf16[160,128]{1,0:T(8,128)(2,1)S(1)}, u32[]{:S(2)}, u32[]{:S(2)}) collective-permute-start(bf16[160,128]{1,0:T(8,128)(2,1)S(1)} %multiply_convert_fusion.refs_0_), channel_id=1, source_target_pairs={{0,16},{8,24},{16,0},{24,8},{1,17},{9,25},{17,1},{25,9},{2,18},{10... | collective-permute-start | bytes 122888 | tf_op jit(solution)/shard_map/ppermute | solution.py:24
  50.2 4.0 %collective-permute-start.7 = (bf16[160,128]{1,0:T(8,128)(2,1)S(1)}, bf16[160,128]{1,0:T(8,128)(2,1)S(1)}, u32[]{:S(2)}, u32[]{:S(2)}) collective-permute-start(bf16[160,128]{1,0:T(8,128)(2,1)S(1)} %multiply_convert_fusion.refs_0_), channel_id=1, source_target_pairs={{0,8},{8,0},{16,24},{24,16},{1,9},{9,1},{17,25},{25,17},{2,10},{10... | collective-permute-start | bytes 122888 | tf_op jit(solution)/shard_map/ppermute | solution.py:24
  51.4 2.8 %collective-permute-start.10 = (bf16[160,128]{1,0:T(8,128)(2,1)S(1)}, bf16[160,128]{1,0:T(8,128)(2,1)S(1)}, u32[]{:S(2)}, u32[]{:S(2)}) collective-permute-start(bf16[160,128]{1,0:T(8,128)(2,1)S(1)} %multiply_convert_fusion.refs_0_), channel_id=1, source_target_pairs={{0,1},{1,0},{2,3},{3,2},{4,5},{5,4},{6,7},{7,6},{8,9},{9,8},{10,11... | collective-permute-start | bytes 122888 | tf_op jit(solution)/shard_map/ppermute | solution.py:24
  52.9 1.3 %collective-permute-start.13 = (bf16[160,128]{1,0:T(8,128)(2,1)S(1)}, bf16[160,128]{1,0:T(8,128)(2,1)S(1)}, u32[]{:S(2)}, u32[]{:S(2)}) collective-permute-start(bf16[160,128]{1,0:T(8,128)(2,1)S(1)} %collective-permute-done.9.refs_3_), channel_id=1, source_target_pairs={{0,1},{1,0},{2,3},{3,2},{4,5},{5,4},{6,7},{7,6},{8,9},{9,8},{10,11... | collective-permute-start | bytes 122888 | tf_op jit(solution)/shard_map/ppermute | solution.py:24
  53.7 1.2 %collective-permute-start.12 = (bf16[160,128]{1,0:T(8,128)(2,1)S(1)}, bf16[160,128]{1,0:T(8,128)(2,1)S(1)}, u32[]{:S(2)}, u32[]{:S(2)}) collective-permute-start(bf16[160,128]{1,0:T(8,128)(2,1)S(1)} %collective-permute-done.8.refs_2_), channel_id=1, source_target_pairs={{0,1},{1,0},{2,3},{3,2},{4,5},{5,4},{6,7},{7,6},{8,9},{9,8},{10,11... | collective-permute-start | bytes 122888 | tf_op jit(solution)/shard_map/ppermute | solution.py:24
  54.2 1.2 %collective-permute-start.11 = (bf16[160,128]{1,0:T(8,128)(2,1)S(1)}, bf16[160,128]{1,0:T(8,128)(2,1)S(1)}, u32[]{:S(2)}, u32[]{:S(2)}) collective-permute-start(bf16[160,128]{1,0:T(8,128)(2,1)S(1)} %collective-permute-done.7.refs_1_), channel_id=1, source_target_pairs={{0,1},{1,0},{2,3},{3,2},{4,5},{5,4},{6,7},{7,6},{8,9},{9,8},{10,11... | collective-permute-start | bytes 122888 | tf_op jit(solution)/shard_map/ppermute | solution.py:24

commit v4 on v3

--- a/solution.py
+++ b/solution.py
@@ -10,6 +10,7 @@
 NC = 24576
 BLOCK = 128
 BOTH = ("band", "domain")
+SENT = jnp.float16
 
 
 VMEM_LIMIT = pltpu.CompilerParams(vmem_limit_bytes=16 * 1024 * 1024)
@@ -81,7 +82,7 @@
 
         for m in range(bands):
             at = pl.ds(pl.multiple_of((band ^ m) * piece, piece), piece)
-            piece_refs[m][...] = stack[at, :]
+            piece_refs[m][...] = stack[at, :] * (1.0 / NC)
 
     return pl.pallas_call(
         body,
@@ -166,11 +167,13 @@
     pieces = cross_gram(rows, width, bands)(x, y, own)
     total = pieces[0]
     for m in range(1, bands):
-        total = total + swap(pieces[m], "band", m)
+        total = total + swap(pieces[m].astype(SENT), "band", m).astype(jnp.float32)
+    total = total.astype(SENT)
     heard = [total] + [swap(total, "domain", 2 * m) for m in range(1, levels)]
+    heard = [h.astype(jnp.float32) for h in heard]
     while len(heard) > 1:
         heard = [heard[k] + heard[k + 1] for k in range(0, len(heard), 2)]
-    excess = (heard[0] * (1.0 / NC)).astype(jnp.bfloat16)
+    excess = heard[0].astype(jnp.bfloat16)
     mine = [excess] + [swap(excess, "band", m) for m in range(1, bands)]
     other = [swap(e, "domain", 1) for e in mine]
     out = correct(rows, width, bands)(x, y, *mine, *other).reshape(devices, tall, width)

time: 82.3 us -> 79.2 us (0.962)
  waiting for transfers between devices: 14.3 us -> 11.3 us
    ppermute x14, waiting for transfers between devices: 14.3 us -> 11.3 us  [swap(): return lax.ppermute(value, axis, [(i, i ^ mask) for i in range(count)])]
  transfers between devices with their start and end apart: 14 -> 14, of which waited for: 10 -> 12; matrix products, arithmetic and copies ran while one was open for 0% -> 0% of each run, Pallas kernels for 0% -> 1%
where the time goes in v4:
time: 79.2 us; the launch traced here: 79 us
  blocking collectives  53 us (67%)
  starting transfers between devices  11.7 us (15%)
  waiting for transfers between devices  11.3 us (14%)
  Pallas kernels  2.02 us (3%)
  local copies, waits for them, and re-layouts  0.88 us (1%)
    all_to_all x1, blocking collectives, full_rows(): lax.all_to_all(cut, BOTH, split_axis=0, concat_axis=0, axis_index_groups=...  28.6 us
    all_to_all x1, blocking collectives, full_rows(): lax.all_to_all(out, BOTH, split_axis=0, concat_axis=0, axis_index_groups=...  24.3 us
    ppermute x14, starting transfers between devices, swap(): return lax.ppermute(value, axis, [(i, i ^ mask) for i in range(count)])  11.7 us
    ppermute x14, waiting for transfers between devices, swap(): return lax.ppermute(value, axis, [(i, i ^ mask) for i in range(count)])  11.3 us
  transfers between devices with their start and end apart: 14, of which 12 were waited for; matrix products, arithmetic and copies ran while one was open for 0% of the time, Pallas kernels for 1%

profile of v4, /device:TPU:0, one launch (start us, length us, event | category | flops | bytes accessed | tf_op | source)
XLA Modules:
  0.0 79.0 jit_solution(9796527536769599931)
XLA Ops:
  0.0 28.6 %all_to_all.10 = bf16[32,8,1536]{2,1,0:T(8,128)(2,1)S(1)} all-to-all(bf16[32,8,1536]{2,1,0:T(8,128)(2,1)} %bitcast.18), channel_id=1, replica_groups={{0,2,4,6,8,10,12,14,16,18,20,22,24,26,28,30,1,3,5,7,9,11,13,15,17,19,21..., dimensions={0} | all-to-all | bytes 1572864 | tf_op jit(solution)/shard_map/all_to_all | solution.py:164
  28.6 0.4 shard_map.17.own_ref
  29.1 1.9 %collective-permute-done.y_ref = bf16[256,1536]{1,0:T(8,128)(2,1)S(1)} collective-permute-done((bf16[256,1536]{1,0:T(8,128)(2,1)S(1)}, bf16[256,1536]{1,0:T(8,128)(2,1)S(1)}, u32[]{:S(2)}, u32[]{:S(2)}) %collective-permute-start) | collective-permute-done | bytes 786464 | tf_op jit(solution)/shard_map/ppermute | solution.py:25
  30.9 0.4 shard_map.18
  31.4 0.9 %collective-permute-start.3 = (f16[160,128]{1,0:T(8,128)(2,1)S(1)}, f16[160,128]{1,0:T(8,128)(2,1)S(1)}, u32[]{:S(2)}, u32[]{:S(2)}) collective-permute-start(f16[160,128]{1,0:T(8,128)(2,1)S(1)} %convert_element_type.40), channel_id=1, source_target_pairs={{0,24},{8,16},{16,8},{24,0},{1,25},{9,17},{17,9},{25,1},{2,26},{10... | collective-permute-start | bytes 122888 | tf_op jit(solution)/shard_map/ppermute | solution.py:25
  32.3 2.0 %collective-permute-start.2 = (f16[160,128]{1,0:T(8,128)(2,1)S(1)}, f16[160,128]{1,0:T(8,128)(2,1)S(1)}, u32[]{:S(2)}, u32[]{:S(2)}) collective-permute-start(f16[160,128]{1,0:T(8,128)(2,1)S(1)} %convert_element_type.38), channel_id=1, source_target_pairs={{0,16},{8,24},{16,0},{24,8},{1,17},{9,25},{17,1},{25,9},{2,18},{10... | collective-permute-start | bytes 122888 | tf_op jit(solution)/shard_map/ppermute | solution.py:25
  34.4 0.6 collective-permute-start.1
  35.0 1.6 %collective-permute-done.3 = f16[160,128]{1,0:T(8,128)(2,1)S(1)} collective-permute-done((f16[160,128]{1,0:T(8,128)(2,1)S(1)}, f16[160,128]{1,0:T(8,128)(2,1)S(1)}, u32[]{:S(2)}, u32[]{:S(2)}) %collective-permute-start.3) | collective-permute-done | bytes 40992 | tf_op jit(solution)/shard_map/ppermute | solution.py:25
  36.5 0.3 collective-permute-done.2
  36.8 1.6 %collective-permute-done.1 = f16[160,128]{1,0:T(8,128)(2,1)S(1)} collective-permute-done((f16[160,128]{1,0:T(8,128)(2,1)S(1)}, f16[160,128]{1,0:T(8,128)(2,1)S(1)}, u32[]{:S(2)}, u32[]{:S(2)}) %collective-permute-start.1) | collective-permute-done | bytes 40992 | tf_op jit(solution)/shard_map/ppermute | solution.py:25
  38.4 1.5 %collective-permute-start.6 = (f16[160,128]{1,0:T(8,128)(2,1)S(1)}, f16[160,128]{1,0:T(8,128)(2,1)S(1)}, u32[]{:S(2)}, u32[]{:S(2)}) collective-permute-start(f16[160,128]{1,0:T(8,128)(2,1)S(1)} %add_convert_fusion.1), channel_id=1, source_target_pairs={{0,6},{1,7},{2,4},{3,5},{4,2},{5,3},{6,0},{7,1},{8,14},{9,15},{10,... | collective-permute-start | bytes 122888 | tf_op jit(solution)/shard_map/ppermute | solution.py:25
  39.9 0.0 collective-permute-start.5
  39.9 2.9 %collective-permute-start.4 = (f16[160,128]{1,0:T(8,128)(2,1)S(1)}, f16[160,128]{1,0:T(8,128)(2,1)S(1)}, u32[]{:S(2)}, u32[]{:S(2)}) collective-permute-start(f16[160,128]{1,0:T(8,128)(2,1)S(1)} %add_convert_fusion.1), channel_id=1, source_target_pairs={{0,2},{1,3},{2,0},{3,1},{4,6},{5,7},{6,4},{7,5},{8,10},{9,11},{10,... | collective-permute-start | bytes 122888 | tf_op jit(solution)/shard_map/ppermute | solution.py:25
  42.8 1.4 %collective-permute-done.6 = f16[160,128]{1,0:T(8,128)(2,1)S(1)} collective-permute-done((f16[160,128]{1,0:T(8,128)(2,1)S(1)}, f16[160,128]{1,0:T(8,128)(2,1)S(1)}, u32[]{:S(2)}, u32[]{:S(2)}) %collective-permute-start.6) | collective-permute-done | bytes 40992 | tf_op jit(solution)/shard_map/ppermute | solution.py:25
  44.3 1.0 %collective-permute-done.5 = f16[160,128]{1,0:T(8,128)(2,1)S(1)} collective-permute-done((f16[160,128]{1,0:T(8,128)(2,1)S(1)}, f16[160,128]{1,0:T(8,128)(2,1)S(1)}, u32[]{:S(2)}, u32[]{:S(2)}) %collective-permute-start.5) | collective-permute-done | bytes 40992 | tf_op jit(solution)/shard_map/ppermute | solution.py:25
  45.2 0.0 collective-permute-done.4
  45.3 1.1 %collective-permute-start.9 = (bf16[160,128]{1,0:T(8,128)(2,1)S(1)}, bf16[160,128]{1,0:T(8,128)(2,1)S(1)}, u32[]{:S(2)}, u32[]{:S(2)}) collective-permute-start(bf16[160,128]{1,0:T(8,128)(2,1)S(1)} %add_convert_fusion.refs_0_), channel_id=1, source_target_pairs={{0,24},{8,16},{16,8},{24,0},{1,25},{9,17},{17,9},{25,1},{2,26},{10... | collective-permute-start | bytes 122888 | tf_op jit(solution)/shard_map/ppermute | solution.py:25
  46.4 1.0 %collective-permute-start.8 = (bf16[160,128]{1,0:T(8,128)(2,1)S(1)}, bf16[160,128]{1,0:T(8,128)(2,1)S(1)}, u32[]{:S(2)}, u32[]{:S(2)}) collective-permute-start(bf16[160,128]{1,0:T(8,128)(2,1)S(1)} %add_convert_fusion.refs_0_), channel_id=1, source_target_pairs={{0,16},{8,24},{16,0},{24,8},{1,17},{9,25},{17,1},{25,9},{2,18},{10... | collective-permute-start | bytes 122888 | tf_op jit(solution)/shard_map/ppermute | solution.py:25
  47.4 1.5 %collective-permute-start.7 = (bf16[160,128]{1,0:T(8,128)(2,1)S(1)}, bf16[160,128]{1,0:T(8,128)(2,1)S(1)}, u32[]{:S(2)}, u32[]{:S(2)}) collective-permute-start(bf16[160,128]{1,0:T(8,128)(2,1)S(1)} %add_convert_fusion.refs_0_), channel_id=1, source_target_pairs={{0,8},{8,0},{16,24},{24,16},{1,9},{9,1},{17,25},{25,17},{2,10},{10... | collective-permute-start | bytes 122888 | tf_op jit(solution)/shard_map/ppermute | solution.py:25
  48.8 0.0 collective-permute-start.10
  48.8 1.4 %collective-permute-done.9.refs_3_ = bf16[160,128]{1,0:T(8,128)(2,1)S(1)} collective-permute-done((bf16[160,128]{1,0:T(8,128)(2,1)S(1)}, bf16[160,128]{1,0:T(8,128)(2,1)S(1)}, u32[]{:S(2)}, u32[]{:S(2)}) %collective-permute-start.9) | collective-permute-done | bytes 40992 | tf_op jit(solution)/shard_map/ppermute | solution.py:25
  50.3 0.0 collective-permute-start.13
  50.3 0.4 collective-permute-done.8.refs_2_
  50.7 0.1 collective-permute-start.12
  50.8 0.6 collective-permute-done.7.refs_1_
  51.4 0.0 collective-permute-start.11
  51.4 0.1 collective-permute-done.13.refs_7_
  51.5 0.4 collective-permute-done.12.refs_6_
  51.9 0.7 collective-permute-done.11.refs_5_
  52.6 1.2 %shard_map.19 = bf16[256,1536]{1,0:T(8,128)(2,1)S(1)} custom-call(bf16[256,1536]{1,0:T(8,128)(2,1)S(1)} %bitcast.15, bf16[256,1536]{1,0:T(8,128)(2,1)S(1)} %collective-permute-done.y_ref, bf16[160,128]{1,0:T(8,128)(2,1)S(1)} %add_convert_fusion.refs_0_, bf16[160,128]{1,0:T(8,128)(2,1)S(1)} %collective-permute-done.7.refs_1_, ...), custom_call_target="tpu_custom_call" | custom-call | tf_op jit(solution)/shard_map/pallas_call | solution.py:179
  53.8 24.3 %all_to_all.11 = bf16[32,8,1536]{2,1,0:T(8,128)(2,1)S(1)} all-to-all(bf16[32,8,1536]{2,1,0:T(8,128)(2,1)S(1)} %bitcast.16), channel_id=1, replica_groups={{0,2,4,6,8,10,12,14,16,18,20,22,24,26,28,30,1,3,5,7,9,11,13,15,17,19,21..., dimensions={0} | all-to-all | bytes 1572864 | tf_op jit(solution)/shard_map/all_to_all | solution.py:180
  78.1 0.9 %copy.3 = bf16[16,24576]{1,0:T(8,128)(2,1)} copy(bf16[16,24576]{1,0:T(8,128)(2,1)S(1)} %bitcast.17) | data formatting | bytes 1572864
  (7 shorter events, 0.1 us)
Async XLA Ops:
  28.6 2.3 %collective-permute-start = (bf16[256,1536]{1,0:T(8,128)(2,1)S(1)}, bf16[256,1536]{1,0:T(8,128)(2,1)S(1)}, u32[]{:S(2)}, u32[]{:S(2)}) collective-permute-start(bf16[256,1536]{1,0:T(8,128)(2,1)S(1)} %bitcast.12), channel_id=1, source_target_pairs={{0,1},{1,0},{2,3},{3,2},{4,5},{5,4},{6,7},{7,6},{8,9},{9,8},{10,11... | collective-permute-start | bytes 2359304 | tf_op jit(solution)/shard_map/ppermute | solution.py:25
  31.4 5.1 %collective-permute-start.3 = (f16[160,128]{1,0:T(8,128)(2,1)S(1)}, f16[160,128]{1,0:T(8,128)(2,1)S(1)}, u32[]{:S(2)}, u32[]{:S(2)}) collective-permute-start(f16[160,128]{1,0:T(8,128)(2,1)S(1)} %convert_element_type.40), channel_id=1, source_target_pairs={{0,24},{8,16},{16,8},{24,0},{1,25},{9,17},{17,9},{25,1},{2,26},{10... | collective-permute-start | bytes 122888 | tf_op jit(solution)/shard_map/ppermute | solution.py:25
  32.3 4.5 %collective-permute-start.2 = (f16[160,128]{1,0:T(8,128)(2,1)S(1)}, f16[160,128]{1,0:T(8,128)(2,1)S(1)}, u32[]{:S(2)}, u32[]{:S(2)}) collective-permute-start(f16[160,128]{1,0:T(8,128)(2,1)S(1)} %convert_element_type.38), channel_id=1, source_target_pairs={{0,16},{8,24},{16,0},{24,8},{1,17},{9,25},{17,1},{25,9},{2,18},{10... | collective-permute-start | bytes 122888 | tf_op jit(solution)/shard_map/ppermute | solution.py:25
  34.4 4.0 %collective-permute-start.1 = (f16[160,128]{1,0:T(8,128)(2,1)S(1)}, f16[160,128]{1,0:T(8,128)(2,1)S(1)}, u32[]{:S(2)}, u32[]{:S(2)}) collective-permute-start(f16[160,128]{1,0:T(8,128)(2,1)S(1)} %convert_element_type.36), channel_id=1, source_target_pairs={{0,8},{8,0},{16,24},{24,16},{1,9},{9,1},{17,25},{25,17},{2,10},{10... | collective-permute-start | bytes 122888 | tf_op jit(solution)/shard_map/ppermute | solution.py:25
  38.4 5.9 %collective-permute-start.6 = (f16[160,128]{1,0:T(8,128)(2,1)S(1)}, f16[160,128]{1,0:T(8,128)(2,1)S(1)}, u32[]{:S(2)}, u32[]{:S(2)}) collective-permute-start(f16[160,128]{1,0:T(8,128)(2,1)S(1)} %add_convert_fusion.1), channel_id=1, source_target_pairs={{0,6},{1,7},{2,4},{3,5},{4,2},{5,3},{6,0},{7,1},{8,14},{9,15},{10,... | collective-permute-start | bytes 122888 | tf_op jit(solution)/shard_map/ppermute | solution.py:25
  39.9 5.3 %collective-permute-start.5 = (f16[160,128]{1,0:T(8,128)(2,1)S(1)}, f16[160,128]{1,0:T(8,128)(2,1)S(1)}, u32[]{:S(2)}, u32[]{:S(2)}) collective-permute-start(f16[160,128]{1,0:T(8,128)(2,1)S(1)} %add_convert_fusion.1), channel_id=1, source_target_pairs={{0,4},{1,5},{2,6},{3,7},{4,0},{5,1},{6,2},{7,3},{8,12},{9,13},{10,... | collective-permute-start | bytes 122888 | tf_op jit(solution)/shard_map/ppermute | solution.py:25
  39.9 5.4 %collective-permute-start.4 = (f16[160,128]{1,0:T(8,128)(2,1)S(1)}, f16[160,128]{1,0:T(8,128)(2,1)S(1)}, u32[]{:S(2)}, u32[]{:S(2)}) collective-permute-start(f16[160,128]{1,0:T(8,128)(2,1)S(1)} %add_convert_fusion.1), channel_id=1, source_target_pairs={{0,2},{1,3},{2,0},{3,1},{4,6},{5,7},{6,4},{7,5},{8,10},{9,11},{10,... | collective-permute-start | bytes 122888 | tf_op jit(solution)/shard_map/ppermute | solution.py:25
  45.3 5.0 %collective-permute-start.9 = (bf16[160,128]{1,0:T(8,128)(2,1)S(1)}, bf16[160,128]{1,0:T(8,128)(2,1)S(1)}, u32[]{:S(2)}, u32[]{:S(2)}) collective-permute-start(bf16[160,128]{1,0:T(8,128)(2,1)S(1)} %add_convert_fusion.refs_0_), channel_id=1, source_target_pairs={{0,24},{8,16},{16,8},{24,0},{1,25},{9,17},{17,9},{25,1},{2,26},{10... | collective-permute-start | bytes 122888 | tf_op jit(solution)/shard_map/ppermute | solution.py:25
  46.4 4.3 %collective-permute-start.8 = (bf16[160,128]{1,0:T(8,128)(2,1)S(1)}, bf16[160,128]{1,0:T(8,128)(2,1)S(1)}, u32[]{:S(2)}, u32[]{:S(2)}) collective-permute-start(bf16[160,128]{1,0:T(8,128)(2,1)S(1)} %add_convert_fusion.refs_0_), channel_id=1, source_target_pairs={{0,16},{8,24},{16,0},{24,8},{1,17},{9,25},{17,1},{25,9},{2,18},{10... | collective-permute-start | bytes 122888 | tf_op jit(solution)/shard_map/ppermute | solution.py:25
  47.4 4.0 %collective-permute-start.7 = (bf16[160,128]{1,0:T(8,128)(2,1)S(1)}, bf16[160,128]{1,0:T(8,128)(2,1)S(1)}, u32[]{:S(2)}, u32[]{:S(2)}) collective-permute-start(bf16[160,128]{1,0:T(8,128)(2,1)S(1)} %add_convert_fusion.refs_0_), channel_id=1, source_target_pairs={{0,8},{8,0},{16,24},{24,16},{1,9},{9,1},{17,25},{25,17},{2,10},{10... | collective-permute-start | bytes 122888 | tf_op jit(solution)/shard_map/ppermute | solution.py:25
  48.8 2.5 %collective-permute-start.10 = (bf16[160,128]{1,0:T(8,128)(2,1)S(1)}, bf16[160,128]{1,0:T(8,128)(2,1)S(1)}, u32[]{:S(2)}, u32[]{:S(2)}) collective-permute-start(bf16[160,128]{1,0:T(8,128)(2,1)S(1)} %add_convert_fusion.refs_0_), channel_id=1, source_target_pairs={{0,1},{1,0},{2,3},{3,2},{4,5},{5,4},{6,7},{7,6},{8,9},{9,8},{10,11... | collective-permute-start | bytes 122888 | tf_op jit(solution)/shard_map/ppermute | solution.py:25
  50.3 1.2 %collective-permute-start.13 = (bf16[160,128]{1,0:T(8,128)(2,1)S(1)}, bf16[160,128]{1,0:T(8,128)(2,1)S(1)}, u32[]{:S(2)}, u32[]{:S(2)}) collective-permute-start(bf16[160,128]{1,0:T(8,128)(2,1)S(1)} %collective-permute-done.9.refs_3_), channel_id=1, source_target_pairs={{0,1},{1,0},{2,3},{3,2},{4,5},{5,4},{6,7},{7,6},{8,9},{9,8},{10,11... | collective-permute-start | bytes 122888 | tf_op jit(solution)/shard_map/ppermute | solution.py:25
  50.7 1.2 %collective-permute-start.12 = (bf16[160,128]{1,0:T(8,128)(2,1)S(1)}, bf16[160,128]{1,0:T(8,128)(2,1)S(1)}, u32[]{:S(2)}, u32[]{:S(2)}) collective-permute-start(bf16[160,128]{1,0:T(8,128)(2,1)S(1)} %collective-permute-done.8.refs_2_), channel_id=1, source_target_pairs={{0,1},{1,0},{2,3},{3,2},{4,5},{5,4},{6,7},{7,6},{8,9},{9,8},{10,11... | collective-permute-start | bytes 122888 | tf_op jit(solution)/shard_map/ppermute | solution.py:25
  51.4 1.2 %collective-permute-start.11 = (bf16[160,128]{1,0:T(8,128)(2,1)S(1)}, bf16[160,128]{1,0:T(8,128)(2,1)S(1)}, u32[]{:S(2)}, u32[]{:S(2)}) collective-permute-start(bf16[160,128]{1,0:T(8,128)(2,1)S(1)} %collective-permute-done.7.refs_1_), channel_id=1, source_target_pairs={{0,1},{1,0},{2,3},{3,2},{4,5},{5,4},{6,7},{7,6},{8,9},{9,8},{10,11... | collective-permute-start | bytes 122888 | tf_op jit(solution)/shard_map/ppermute | solution.py:25

commit v5 on v4

--- a/solution.py
+++ b/solution.py
@@ -11,6 +11,7 @@
 BLOCK = 128
 BOTH = ("band", "domain")
 SENT = jnp.float16
+MEASURED = (10, 14, 12, 1, 9, 0, 3, 8, 2, 11, 7, 4, 13, 6, 15, 5)
 
 
 VMEM_LIMIT = pltpu.CompilerParams(vmem_limit_bytes=16 * 1024 * 1024)
@@ -26,6 +27,12 @@
 
 
 ACROSS = (((1,), (1,)), ((), ()))
+
+
+def chip_order(bands, levels):
+    if (bands, levels) == (4, 4):
+        return MEASURED
+    return sorted(range(bands * levels), key=lambda q: (q // levels, abs(q % levels - levels // 2), q))
 
 
 def upper_blocks(count):
@@ -95,7 +102,7 @@
     )
 
 
-def correct(rows, width, bands):
+def correct(rows, width, bands, tall):
     count = rows // BLOCK
     upper = count * (count + 1) // 2 * BLOCK
     mid = rows // 2
@@ -133,12 +140,18 @@
                     excess[rows + row:rows + row + mid, column:column + BLOCK] = block
                     excess[column:column + BLOCK, rows + row:rows + row + mid] = block.T
 
-        own = excess[0:rows, :]
+        mine = pl.ds(pl.multiple_of(core * mid, mid), mid)
+        theirs = pl.ds(pl.multiple_of(rows + core * mid, mid), mid)
+        own = jnp.concatenate([excess[mine, :], excess[theirs, :]], axis=0)
         twice = jnp.dot(own, excess[...], preferred_element_type=jnp.float32)
         change = (0.375 * twice - 0.5 * own.astype(jnp.float32)).astype(jnp.bfloat16)
-        out = x_ref[...].astype(jnp.float32)
+        out = jnp.concatenate([x_ref[mine, :], y_ref[mine, :]], axis=0).astype(jnp.float32)
         out += jnp.dot(change[:, 0:rows], x_ref[...], preferred_element_type=jnp.float32)
         out += jnp.dot(change[:, rows:2 * rows], y_ref[...], preferred_element_type=jnp.float32)
+        near, far = out[0:mid], out[mid:rows]
+        upper_half = jnp.where(core == 0, near, far).reshape(mid // tall, tall, width)
+        lower_half = jnp.where(core == 0, far, near).reshape(mid // tall, tall, width)
+        out = jnp.concatenate([upper_half, lower_half], axis=1).reshape(rows, width)
         out_ref[...] = out.astype(jnp.bfloat16)
 
     return pl.pallas_call(
@@ -159,7 +172,8 @@
     fdev, ncoef = functions.shape
     tall, width = fdev // 2, ncoef // chips
     rows = devices * tall
-    order = [[b * domains + 2 * z + c for c in range(2) for b in range(bands) for z in range(levels)]]
+    spread = [[2 * q + c for q in chip_order(bands, levels)] for c in range(2)]
+    order = [spread[0] + spread[1]]
     cut = functions.reshape(2, tall, chips, width).transpose(0, 2, 1, 3).reshape(devices, tall, width)
     x = lax.all_to_all(cut, BOTH, split_axis=0, concat_axis=0, axis_index_groups=order).reshape(rows, width)
     y = swap(x, "domain", 1)
@@ -176,9 +190,9 @@
     excess = heard[0].astype(jnp.bfloat16)
     mine = [excess] + [swap(excess, "band", m) for m in range(1, bands)]
     other = [swap(e, "domain", 1) for e in mine]
-    out = correct(rows, width, bands)(x, y, *mine, *other).reshape(devices, tall, width)
-    back = lax.all_to_all(out, BOTH, split_axis=0, concat_axis=0, axis_index_groups=order)
-    return back.reshape(2, chips, tall, width).transpose(0, 2, 1, 3).reshape(fdev, ncoef)
+    out = correct(rows, width, bands, tall)(x, y, *mine, *other).reshape(chips, fdev, width)
+    back = lax.all_to_all(out, BOTH, split_axis=0, concat_axis=0, axis_index_groups=spread)
+    return back.transpose(1, 0, 2).reshape(fdev, ncoef)
 
 
 def apply_blocks(excess, block_index, source_blocks):

time: 79.2 us -> 78.4 us (0.990)
  blocking collectives: 53 us -> 50.8 us
  waiting for transfers between devices: 11.3 us -> 12.1 us
    all_to_all x1, blocking collectives: 24.3 us -> 23 us  [full_rows(): lax.all_to_all(out, BOTH, split_axis=0, concat_axis=0, axis_index_groups=...]
    reshape x0 -> x1, local copies, waits for them, and re-layouts: none -> 0.93 us  [full_rows(): return back.transpose(1, 0, 2).reshape(fdev, ncoef)]
    unnamed x1 -> x0, local copies, waits for them, and re-layouts: 0.88 us -> none
    all_to_all x1, blocking collectives: 28.6 us -> 27.8 us  [full_rows(): lax.all_to_all(cut, BOTH, split_axis=0, concat_axis=0, axis_index_groups=...]
  transfers between devices with their start and end apart: 14 -> 14, of which waited for: 12 -> 11; matrix products, arithmetic and copies ran while one was open for 0% -> 0% of each run, Pallas kernels for 1% -> 1%
where the time goes in v5:
time: 78.4 us; the launch traced here: 78.1 us
  blocking collectives  50.8 us (65%)
  starting transfers between devices  12.1 us (15%)
  waiting for transfers between devices  12.1 us (15%)
  Pallas kernels  2.03 us (3%)
  local copies, waits for them, and re-layouts  0.93 us (1%)
    all_to_all x1, blocking collectives, full_rows(): lax.all_to_all(cut, BOTH, split_axis=0, concat_axis=0, axis_index_groups=...  27.8 us
    all_to_all x1, blocking collectives, full_rows(): lax.all_to_all(out, BOTH, split_axis=0, concat_axis=0, axis_index_groups=...  23 us
    ppermute x14, starting transfers between devices, swap(): return lax.ppermute(value, axis, [(i, i ^ mask) for i in range(count)])  12.1 us
    ppermute x14, waiting for transfers between devices, swap(): return lax.ppermute(value, axis, [(i, i ^ mask) for i in range(count)])  12.1 us
  transfers between devices with their start and end apart: 14, of which 11 were waited for; matrix products, arithmetic and copies ran while one was open for 0% of the time, Pallas kernels for 1%

profile of v5, /device:TPU:0, one launch (start us, length us, event | category | flops | bytes accessed | tf_op | source)
XLA Modules:
  0.0 78.1 jit_solution(3676719999825959091)
XLA Ops:
  0.0 27.8 %all_to_all.10 = bf16[32,8,1536]{2,1,0:T(8,128)(2,1)S(1)} all-to-all(bf16[32,8,1536]{2,1,0:T(8,128)(2,1)} %bitcast.16), channel_id=1, replica_groups={{20,28,24,2,18,0,6,16,4,22,14,8,26,12,30,10,21,29,25,3,19,1,7,17,5,23,1..., dimensions={0} | all-to-all | bytes 1572864 | tf_op jit(solution)/shard_map/all_to_all | solution.py:178
  27.8 0.6 collective-permute-start
  28.4 0.4 shard_map.17.own_ref
  28.8 1.5 %collective-permute-done.y_ref = bf16[256,1536]{1,0:T(8,128)(2,1)S(1)} collective-permute-done((bf16[256,1536]{1,0:T(8,128)(2,1)S(1)}, bf16[256,1536]{1,0:T(8,128)(2,1)S(1)}, u32[]{:S(2)}, u32[]{:S(2)}) %collective-permute-start) | collective-permute-done | bytes 786464 | tf_op jit(solution)/shard_map/ppermute | solution.py:26
  30.3 0.4 shard_map.18
  30.8 2.3 %collective-permute-start.3 = (f16[160,128]{1,0:T(8,128)(2,1)S(1)}, f16[160,128]{1,0:T(8,128)(2,1)S(1)}, u32[]{:S(2)}, u32[]{:S(2)}) collective-permute-start(f16[160,128]{1,0:T(8,128)(2,1)S(1)} %convert_element_type.40), channel_id=1, source_target_pairs={{0,24},{8,16},{16,8},{24,0},{1,25},{9,17},{17,9},{25,1},{2,26},{10... | collective-permute-start | bytes 122888 | tf_op jit(solution)/shard_map/ppermute | solution.py:26
  33.1 0.7 collective-permute-start.2
  33.8 0.5 collective-permute-start.1
  34.4 1.4 %collective-permute-done.3 = f16[160,128]{1,0:T(8,128)(2,1)S(1)} collective-permute-done((f16[160,128]{1,0:T(8,128)(2,1)S(1)}, f16[160,128]{1,0:T(8,128)(2,1)S(1)}, u32[]{:S(2)}, u32[]{:S(2)}) %collective-permute-start.3) | collective-permute-done | bytes 40992 | tf_op jit(solution)/shard_map/ppermute | solution.py:26
  35.8 1.3 %collective-permute-done.2 = f16[160,128]{1,0:T(8,128)(2,1)S(1)} collective-permute-done((f16[160,128]{1,0:T(8,128)(2,1)S(1)}, f16[160,128]{1,0:T(8,128)(2,1)S(1)}, u32[]{:S(2)}, u32[]{:S(2)}) %collective-permute-start.2) | collective-permute-done | bytes 40992 | tf_op jit(solution)/shard_map/ppermute | solution.py:26
  37.1 0.7 collective-permute-done.1
  37.9 1.5 %collective-permute-start.6 = (f16[160,128]{1,0:T(8,128)(2,1)S(1)}, f16[160,128]{1,0:T(8,128)(2,1)S(1)}, u32[]{:S(2)}, u32[]{:S(2)}) collective-permute-start(f16[160,128]{1,0:T(8,128)(2,1)S(1)} %add_convert_fusion.1), channel_id=1, source_target_pairs={{0,6},{1,7},{2,4},{3,5},{4,2},{5,3},{6,0},{7,1},{8,14},{9,15},{10,... | collective-permute-start | bytes 122888 | tf_op jit(solution)/shard_map/ppermute | solution.py:26
  39.3 0.3 collective-permute-start.5
  39.6 2.7 %collective-permute-start.4 = (f16[160,128]{1,0:T(8,128)(2,1)S(1)}, f16[160,128]{1,0:T(8,128)(2,1)S(1)}, u32[]{:S(2)}, u32[]{:S(2)}) collective-permute-start(f16[160,128]{1,0:T(8,128)(2,1)S(1)} %add_convert_fusion.1), channel_id=1, source_target_pairs={{0,2},{1,3},{2,0},{3,1},{4,6},{5,7},{6,4},{7,5},{8,10},{9,11},{10,... | collective-permute-start | bytes 122888 | tf_op jit(solution)/shard_map/ppermute | solution.py:26
  42.3 1.7 %collective-permute-done.6 = f16[160,128]{1,0:T(8,128)(2,1)S(1)} collective-permute-done((f16[160,128]{1,0:T(8,128)(2,1)S(1)}, f16[160,128]{1,0:T(8,128)(2,1)S(1)}, u32[]{:S(2)}, u32[]{:S(2)}) %collective-permute-start.6) | collective-permute-done | bytes 40992 | tf_op jit(solution)/shard_map/ppermute | solution.py:26
  44.0 0.8 %collective-permute-done.5 = f16[160,128]{1,0:T(8,128)(2,1)S(1)} collective-permute-done((f16[160,128]{1,0:T(8,128)(2,1)S(1)}, f16[160,128]{1,0:T(8,128)(2,1)S(1)}, u32[]{:S(2)}, u32[]{:S(2)}) %collective-permute-start.5) | collective-permute-done | bytes 40992 | tf_op jit(solution)/shard_map/ppermute | solution.py:26
  44.8 0.0 collective-permute-done.4
  44.9 1.9 %collective-permute-start.9 = (bf16[160,128]{1,0:T(8,128)(2,1)S(1)}, bf16[160,128]{1,0:T(8,128)(2,1)S(1)}, u32[]{:S(2)}, u32[]{:S(2)}) collective-permute-start(bf16[160,128]{1,0:T(8,128)(2,1)S(1)} %add_convert_fusion.refs_0_), channel_id=1, source_target_pairs={{0,24},{8,16},{16,8},{24,0},{1,25},{9,17},{17,9},{25,1},{2,26},{10... | collective-permute-start | bytes 122888 | tf_op jit(solution)/shard_map/ppermute | solution.py:26
  46.8 1.1 %collective-permute-start.8 = (bf16[160,128]{1,0:T(8,128)(2,1)S(1)}, bf16[160,128]{1,0:T(8,128)(2,1)S(1)}, u32[]{:S(2)}, u32[]{:S(2)}) collective-permute-start(bf16[160,128]{1,0:T(8,128)(2,1)S(1)} %add_convert_fusion.refs_0_), channel_id=1, source_target_pairs={{0,16},{8,24},{16,0},{24,8},{1,17},{9,25},{17,1},{25,9},{2,18},{10... | collective-permute-start | bytes 122888 | tf_op jit(solution)/shard_map/ppermute | solution.py:26
  47.8 0.6 collective-permute-start.7
  48.4 0.0 collective-permute-start.10
  48.4 1.4 %collective-permute-done.9.refs_3_ = bf16[160,128]{1,0:T(8,128)(2,1)S(1)} collective-permute-done((bf16[160,128]{1,0:T(8,128)(2,1)S(1)}, bf16[160,128]{1,0:T(8,128)(2,1)S(1)}, u32[]{:S(2)}, u32[]{:S(2)}) %collective-permute-start.9) | collective-permute-done | bytes 40992 | tf_op jit(solution)/shard_map/ppermute | solution.py:26
  49.8 0.9 %collective-permute-done.8.refs_2_ = bf16[160,128]{1,0:T(8,128)(2,1)S(1)} collective-permute-done((bf16[160,128]{1,0:T(8,128)(2,1)S(1)}, bf16[160,128]{1,0:T(8,128)(2,1)S(1)}, u32[]{:S(2)}, u32[]{:S(2)}) %collective-permute-start.8) | collective-permute-done | bytes 40992 | tf_op jit(solution)/shard_map/ppermute | solution.py:26
  50.8 1.1 %collective-permute-done.7.refs_1_ = bf16[160,128]{1,0:T(8,128)(2,1)S(1)} collective-permute-done((bf16[160,128]{1,0:T(8,128)(2,1)S(1)}, bf16[160,128]{1,0:T(8,128)(2,1)S(1)}, u32[]{:S(2)}, u32[]{:S(2)}) %collective-permute-start.7) | collective-permute-done | bytes 40992 | tf_op jit(solution)/shard_map/ppermute | solution.py:26
  51.8 0.0 collective-permute-start.11
  51.8 0.0 collective-permute-done.10.refs_4_
  51.8 0.0 collective-permute-done.13.refs_7_
  51.8 0.1 collective-permute-done.12.refs_6_
  52.0 1.1 %collective-permute-done.11.refs_5_ = bf16[160,128]{1,0:T(8,128)(2,1)S(1)} collective-permute-done((bf16[160,128]{1,0:T(8,128)(2,1)S(1)}, bf16[160,128]{1,0:T(8,128)(2,1)S(1)}, u32[]{:S(2)}, u32[]{:S(2)}) %collective-permute-start.11) | collective-permute-done | bytes 40992 | tf_op jit(solution)/shard_map/ppermute | solution.py:26
  53.0 1.2 %shard_map.19 = bf16[256,1536]{1,0:T(8,128)(2,1)S(1)} custom-call(bf16[256,1536]{1,0:T(8,128)(2,1)S(1)} %bitcast.13, bf16[256,1536]{1,0:T(8,128)(2,1)S(1)} %collective-permute-done.y_ref, bf16[160,128]{1,0:T(8,128)(2,1)S(1)} %add_convert_fusion.refs_0_, bf16[160,128]{1,0:T(8,128)(2,1)S(1)} %collective-permute-done.7.refs_1_, ...), custom_call_target="tpu_custom_call" | custom-call | tf_op jit(solution)/shard_map/pallas_call | solution.py:193
  54.2 23.0 %all_to_all.11 = bf16[16,16,1536]{2,1,0:T(8,128)(2,1)S(1)} all-to-all(bf16[16,16,1536]{2,1,0:T(8,128)(2,1)S(1)} %bitcast.14), channel_id=1, replica_groups={{20,28,24,2,18,0,6,16,4,22,14,8,26,12,30,10},{21,29,25,3,19,1,7,17,5,23..., dimensions={0} | all-to-all | bytes 1572864 | tf_op jit(solution)/shard_map/all_to_all | solution.py:194
  77.2 0.9 %copy.3 = bf16[16,2,8,1536]{3,2,0,1:T(8,128)(2,1)} copy(bf16[16,2,8,1536]{3,2,1,0:T(8,128)(2,1)S(1)} %bitcast.15) | data formatting | bytes 1572864 | tf_op jit(solution)/shard_map/reshape | solution.py:195
  (7 shorter events, 0.1 us)
Async XLA Ops:
  27.8 2.5 %collective-permute-start = (bf16[256,1536]{1,0:T(8,128)(2,1)S(1)}, bf16[256,1536]{1,0:T(8,128)(2,1)S(1)}, u32[]{:S(2)}, u32[]{:S(2)}) collective-permute-start(bf16[256,1536]{1,0:T(8,128)(2,1)S(1)} %bitcast.10), channel_id=1, source_target_pairs={{0,1},{1,0},{2,3},{3,2},{4,5},{5,4},{6,7},{7,6},{8,9},{9,8},{10,11... | collective-permute-start | bytes 2359304 | tf_op jit(solution)/shard_map/ppermute | solution.py:26
  30.8 5.0 %collective-permute-start.3 = (f16[160,128]{1,0:T(8,128)(2,1)S(1)}, f16[160,128]{1,0:T(8,128)(2,1)S(1)}, u32[]{:S(2)}, u32[]{:S(2)}) collective-permute-start(f16[160,128]{1,0:T(8,128)(2,1)S(1)} %convert_element_type.40), channel_id=1, source_target_pairs={{0,24},{8,16},{16,8},{24,0},{1,25},{9,17},{17,9},{25,1},{2,26},{10... | collective-permute-start | bytes 122888 | tf_op jit(solution)/shard_map/ppermute | solution.py:26
  33.1 4.0 %collective-permute-start.2 = (f16[160,128]{1,0:T(8,128)(2,1)S(1)}, f16[160,128]{1,0:T(8,128)(2,1)S(1)}, u32[]{:S(2)}, u32[]{:S(2)}) collective-permute-start(f16[160,128]{1,0:T(8,128)(2,1)S(1)} %convert_element_type.38), channel_id=1, source_target_pairs={{0,16},{8,24},{16,0},{24,8},{1,17},{9,25},{17,1},{25,9},{2,18},{10... | collective-permute-start | bytes 122888 | tf_op jit(solution)/shard_map/ppermute | solution.py:26
  33.8 4.0 %collective-permute-start.1 = (f16[160,128]{1,0:T(8,128)(2,1)S(1)}, f16[160,128]{1,0:T(8,128)(2,1)S(1)}, u32[]{:S(2)}, u32[]{:S(2)}) collective-permute-start(f16[160,128]{1,0:T(8,128)(2,1)S(1)} %convert_element_type.36), channel_id=1, source_target_pairs={{0,8},{8,0},{16,24},{24,16},{1,9},{9,1},{17,25},{25,17},{2,10},{10... | collective-permute-start | bytes 122888 | tf_op jit(solution)/shard_map/ppermute | solution.py:26
  37.9 6.1 %collective-permute-start.6 = (f16[160,128]{1,0:T(8,128)(2,1)S(1)}, f16[160,128]{1,0:T(8,128)(2,1)S(1)}, u32[]{:S(2)}, u32[]{:S(2)}) collective-permute-start(f16[160,128]{1,0:T(8,128)(2,1)S(1)} %add_convert_fusion.1), channel_id=1, source_target_pairs={{0,6},{1,7},{2,4},{3,5},{4,2},{5,3},{6,0},{7,1},{8,14},{9,15},{10,... | collective-permute-start | bytes 122888 | tf_op jit(solution)/shard_map/ppermute | solution.py:26
  39.3 5.5 %collective-permute-start.5 = (f16[160,128]{1,0:T(8,128)(2,1)S(1)}, f16[160,128]{1,0:T(8,128)(2,1)S(1)}, u32[]{:S(2)}, u32[]{:S(2)}) collective-permute-start(f16[160,128]{1,0:T(8,128)(2,1)S(1)} %add_convert_fusion.1), channel_id=1, source_target_pairs={{0,4},{1,5},{2,6},{3,7},{4,0},{5,1},{6,2},{7,3},{8,12},{9,13},{10,... | collective-permute-start | bytes 122888 | tf_op jit(solution)/shard_map/ppermute | solution.py:26
  39.6 5.2 %collective-permute-start.4 = (f16[160,128]{1,0:T(8,128)(2,1)S(1)}, f16[160,128]{1,0:T(8,128)(2,1)S(1)}, u32[]{:S(2)}, u32[]{:S(2)}) collective-permute-start(f16[160,128]{1,0:T(8,128)(2,1)S(1)} %add_convert_fusion.1), channel_id=1, source_target_pairs={{0,2},{1,3},{2,0},{3,1},{4,6},{5,7},{6,4},{7,5},{8,10},{9,11},{10,... | collective-permute-start | bytes 122888 | tf_op jit(solution)/shard_map/ppermute | solution.py:26
  44.9 5.0 %collective-permute-start.9 = (bf16[160,128]{1,0:T(8,128)(2,1)S(1)}, bf16[160,128]{1,0:T(8,128)(2,1)S(1)}, u32[]{:S(2)}, u32[]{:S(2)}) collective-permute-start(bf16[160,128]{1,0:T(8,128)(2,1)S(1)} %add_convert_fusion.refs_0_), channel_id=1, source_target_pairs={{0,24},{8,16},{16,8},{24,0},{1,25},{9,17},{17,9},{25,1},{2,26},{10... | collective-permute-start | bytes 122888 | tf_op jit(solution)/shard_map/ppermute | solution.py:26
  46.8 4.0 %collective-permute-start.8 = (bf16[160,128]{1,0:T(8,128)(2,1)S(1)}, bf16[160,128]{1,0:T(8,128)(2,1)S(1)}, u32[]{:S(2)}, u32[]{:S(2)}) collective-permute-start(bf16[160,128]{1,0:T(8,128)(2,1)S(1)} %add_convert_fusion.refs_0_), channel_id=1, source_target_pairs={{0,16},{8,24},{16,0},{24,8},{1,17},{9,25},{17,1},{25,9},{2,18},{10... | collective-permute-start | bytes 122888 | tf_op jit(solution)/shard_map/ppermute | solution.py:26
  47.8 4.0 %collective-permute-start.7 = (bf16[160,128]{1,0:T(8,128)(2,1)S(1)}, bf16[160,128]{1,0:T(8,128)(2,1)S(1)}, u32[]{:S(2)}, u32[]{:S(2)}) collective-permute-start(bf16[160,128]{1,0:T(8,128)(2,1)S(1)} %add_convert_fusion.refs_0_), channel_id=1, source_target_pairs={{0,8},{8,0},{16,24},{24,16},{1,9},{9,1},{17,25},{25,17},{2,10},{10... | collective-permute-start | bytes 122888 | tf_op jit(solution)/shard_map/ppermute | solution.py:26
  48.4 3.4 %collective-permute-start.10 = (bf16[160,128]{1,0:T(8,128)(2,1)S(1)}, bf16[160,128]{1,0:T(8,128)(2,1)S(1)}, u32[]{:S(2)}, u32[]{:S(2)}) collective-permute-start(bf16[160,128]{1,0:T(8,128)(2,1)S(1)} %add_convert_fusion.refs_0_), channel_id=1, source_target_pairs={{0,1},{1,0},{2,3},{3,2},{4,5},{5,4},{6,7},{7,6},{8,9},{9,8},{10,11... | collective-permute-start | bytes 122888 | tf_op jit(solution)/shard_map/ppermute | solution.py:26
  49.8 2.0 %collective-permute-start.13 = (bf16[160,128]{1,0:T(8,128)(2,1)S(1)}, bf16[160,128]{1,0:T(8,128)(2,1)S(1)}, u32[]{:S(2)}, u32[]{:S(2)}) collective-permute-start(bf16[160,128]{1,0:T(8,128)(2,1)S(1)} %collective-permute-done.9.refs_3_), channel_id=1, source_target_pairs={{0,1},{1,0},{2,3},{3,2},{4,5},{5,4},{6,7},{7,6},{8,9},{9,8},{10,11... | collective-permute-start | bytes 122888 | tf_op jit(solution)/shard_map/ppermute | solution.py:26
  50.8 1.2 %collective-permute-start.12 = (bf16[160,128]{1,0:T(8,128)(2,1)S(1)}, bf16[160,128]{1,0:T(8,128)(2,1)S(1)}, u32[]{:S(2)}, u32[]{:S(2)}) collective-permute-start(bf16[160,128]{1,0:T(8,128)(2,1)S(1)} %collective-permute-done.8.refs_2_), channel_id=1, source_target_pairs={{0,1},{1,0},{2,3},{3,2},{4,5},{5,4},{6,7},{7,6},{8,9},{9,8},{10,11... | collective-permute-start | bytes 122888 | tf_op jit(solution)/shard_map/ppermute | solution.py:26
  51.8 1.2 %collective-permute-start.11 = (bf16[160,128]{1,0:T(8,128)(2,1)S(1)}, bf16[160,128]{1,0:T(8,128)(2,1)S(1)}, u32[]{:S(2)}, u32[]{:S(2)}) collective-permute-start(bf16[160,128]{1,0:T(8,128)(2,1)S(1)} %collective-permute-done.7.refs_1_), channel_id=1, source_target_pairs={{0,1},{1,0},{2,3},{3,2},{4,5},{5,4},{6,7},{7,6},{8,9},{9,8},{10,11... | collective-permute-start | bytes 122888 | tf_op jit(solution)/shard_map/ppermute | solution.py:26

commit v6 on v5

--- a/solution.py
+++ b/solution.py
@@ -10,7 +10,6 @@
 NC = 24576
 BLOCK = 128
 BOTH = ("band", "domain")
-SENT = jnp.float16
 MEASURED = (10, 14, 12, 1, 9, 0, 3, 8, 2, 11, 7, 4, 13, 6, 15, 5)
 
 
@@ -89,7 +88,7 @@
 
         for m in range(bands):
             at = pl.ds(pl.multiple_of((band ^ m) * piece, piece), piece)
-            piece_refs[m][...] = stack[at, :] * (1.0 / NC)
+            piece_refs[m][...] = stack[at, :]
 
     return pl.pallas_call(
         body,
@@ -144,8 +143,13 @@
         theirs = pl.ds(pl.multiple_of(rows + core * mid, mid), mid)
         own = jnp.concatenate([excess[mine, :], excess[theirs, :]], axis=0)
         twice = jnp.dot(own, excess[...], preferred_element_type=jnp.float32)
-        change = (0.375 * twice - 0.5 * own.astype(jnp.float32)).astype(jnp.bfloat16)
-        out = jnp.concatenate([x_ref[mine, :], y_ref[mine, :]], axis=0).astype(jnp.float32)
+        change = 0.375 * twice - 0.5 * own.astype(jnp.float32)
+        row = lax.broadcasted_iota(jnp.int32, (rows, 2 * rows), 0)
+        column = lax.broadcasted_iota(jnp.int32, (rows, 2 * rows), 1)
+        diagonal = column == row + core * mid + jnp.where(row < mid, 0, rows - mid)
+        weight = 1.0 + jnp.sum(jnp.where(diagonal, change, 0.0), axis=1, keepdims=True)
+        change = jnp.where(diagonal, 0.0, change).astype(jnp.bfloat16)
+        out = jnp.concatenate([x_ref[mine, :], y_ref[mine, :]], axis=0).astype(jnp.float32) * weight
         out += jnp.dot(change[:, 0:rows], x_ref[...], preferred_element_type=jnp.float32)
         out += jnp.dot(change[:, rows:2 * rows], y_ref[...], preferred_element_type=jnp.float32)
         near, far = out[0:mid], out[mid:rows]
@@ -181,13 +185,11 @@
     pieces = cross_gram(rows, width, bands)(x, y, own)
     total = pieces[0]
     for m in range(1, bands):
-        total = total + swap(pieces[m].astype(SENT), "band", m).astype(jnp.float32)
-    total = total.astype(SENT)
+        total = total + swap(pieces[m], "band", m)
     heard = [total] + [swap(total, "domain", 2 * m) for m in range(1, levels)]
-    heard = [h.astype(jnp.float32) for h in heard]
     while len(heard) > 1:
         heard = [heard[k] + heard[k + 1] for k in range(0, len(heard), 2)]
-    excess = heard[0].astype(jnp.bfloat16)
+    excess = (heard[0] * (1.0 / NC)).astype(jnp.bfloat16)
     mine = [excess] + [swap(excess, "band", m) for m in range(1, bands)]
     other = [swap(e, "domain", 1) for e in mine]
     out = correct(rows, width, bands, tall)(x, y, *mine, *other).reshape(chips, fdev, width)

time: 78.4 us -> 81.7 us (1.042)
  waiting for transfers between devices: 12.1 us -> 14.7 us
    ppermute x14, waiting for transfers between devices: 12.1 us -> 14.7 us  [swap(): return lax.ppermute(value, axis, [(i, i ^ mask) for i in range(count)])]
  transfers between devices with their start and end apart: 14 -> 14, of which waited for: 11 -> 11; matrix products, arithmetic and copies ran while one was open for 0% -> 0% of each run, Pallas kernels for 1% -> 0%
where the time goes in v6:
time: 81.7 us; the launch traced here: 81.5 us
  blocking collectives  51.3 us (63%)
  waiting for transfers between devices  14.7 us (18%)
  starting transfers between devices  12.2 us (15%)
  Pallas kernels  2.19 us (3%)
  local copies, waits for them, and re-layouts  0.93 us (1%)
    all_to_all x1, blocking collectives, full_rows(): lax.all_to_all(cut, BOTH, split_axis=0, concat_axis=0, axis_index_groups=...  27.8 us
    all_to_all x1, blocking collectives, full_rows(): lax.all_to_all(out, BOTH, split_axis=0, concat_axis=0, axis_index_groups=...  23.5 us
    ppermute x14, waiting for transfers between devices, swap(): return lax.ppermute(value, axis, [(i, i ^ mask) for i in range(count)])  14.7 us
    ppermute x14, starting transfers between devices, swap(): return lax.ppermute(value, axis, [(i, i ^ mask) for i in range(count)])  12.2 us
  transfers between devices with their start and end apart: 14, of which 11 were waited for; matrix products, arithmetic and copies ran while one was open for 0% of the time, Pallas kernels for 0%

profile of v6, /device:TPU:0, one launch (start us, length us, event | category | flops | bytes accessed | tf_op | source)
XLA Modules:
  0.0 81.5 jit_solution(2367199935807196266)
XLA Ops:
  0.0 27.8 %all_to_all.10 = bf16[32,8,1536]{2,1,0:T(8,128)(2,1)S(1)} all-to-all(bf16[32,8,1536]{2,1,0:T(8,128)(2,1)} %bitcast.16), channel_id=1, replica_groups={{20,28,24,2,18,0,6,16,4,22,14,8,26,12,30,10,21,29,25,3,19,1,7,17,5,23,1..., dimensions={0} | all-to-all | bytes 1572864 | tf_op jit(solution)/shard_map/all_to_all | solution.py:182
  27.8 0.6 collective-permute-start
  28.4 0.4 shard_map.17.own_ref
  28.8 1.5 %collective-permute-done.y_ref = bf16[256,1536]{1,0:T(8,128)(2,1)S(1)} collective-permute-done((bf16[256,1536]{1,0:T(8,128)(2,1)S(1)}, bf16[256,1536]{1,0:T(8,128)(2,1)S(1)}, u32[]{:S(2)}, u32[]{:S(2)}) %collective-permute-start) | collective-permute-done | bytes 786464 | tf_op jit(solution)/shard_map/ppermute | solution.py:25
  30.3 0.4 shard_map.18
  30.7 1.6 %collective-permute-start.1 = (f32[160,128]{1,0:T(8,128)S(1)}, f32[160,128]{1,0:T(8,128)S(1)}, u32[]{:S(2)}, u32[]{:S(2)}) collective-permute-start(f32[160,128]{1,0:T(8,128)S(1)} %get-tuple-element.10), channel_id=1, source_target_pairs={{0,8},{8,0},{16,24},{24,16},{1,9},{9,1},{17,25},{25,17},{2,10},{10... | collective-permute-start | bytes 245768 | tf_op jit(solution)/shard_map/ppermute | solution.py:25
  32.3 1.3 %collective-permute-start.2 = (f32[160,128]{1,0:T(8,128)S(1)}, f32[160,128]{1,0:T(8,128)S(1)}, u32[]{:S(2)}, u32[]{:S(2)}) collective-permute-start(f32[160,128]{1,0:T(8,128)S(1)} %get-tuple-element.11), channel_id=1, source_target_pairs={{0,16},{8,24},{16,0},{24,8},{1,17},{9,25},{17,1},{25,9},{2,18},{10... | collective-permute-start | bytes 245768 | tf_op jit(solution)/shard_map/ppermute | solution.py:25
  33.6 0.7 collective-permute-start.3
  34.3 1.2 %collective-permute-done.1 = f32[160,128]{1,0:T(8,128)S(1)} collective-permute-done((f32[160,128]{1,0:T(8,128)S(1)}, f32[160,128]{1,0:T(8,128)S(1)}, u32[]{:S(2)}, u32[]{:S(2)}) %collective-permute-start.1) | collective-permute-done | bytes 81952 | tf_op jit(solution)/shard_map/ppermute | solution.py:25
  35.5 1.2 %collective-permute-done.2 = f32[160,128]{1,0:T(8,128)S(1)} collective-permute-done((f32[160,128]{1,0:T(8,128)S(1)}, f32[160,128]{1,0:T(8,128)S(1)}, u32[]{:S(2)}, u32[]{:S(2)}) %collective-permute-start.2) | collective-permute-done | bytes 81952 | tf_op jit(solution)/shard_map/ppermute | solution.py:25
  36.8 2.2 %collective-permute-done.3 = f32[160,128]{1,0:T(8,128)S(1)} collective-permute-done((f32[160,128]{1,0:T(8,128)S(1)}, f32[160,128]{1,0:T(8,128)S(1)}, u32[]{:S(2)}, u32[]{:S(2)}) %collective-permute-start.3) | collective-permute-done | bytes 81952 | tf_op jit(solution)/shard_map/ppermute | solution.py:25
  39.0 1.3 %collective-permute-start.6 = (f32[160,128]{1,0:T(8,128)S(1)}, f32[160,128]{1,0:T(8,128)S(1)}, u32[]{:S(2)}, u32[]{:S(2)}) collective-permute-start(f32[160,128]{1,0:T(8,128)S(1)} %add_add_fusion), channel_id=1, source_target_pairs={{0,6},{1,7},{2,4},{3,5},{4,2},{5,3},{6,0},{7,1},{8,14},{9,15},{10,... | collective-permute-start | bytes 245768 | tf_op jit(solution)/shard_map/ppermute | solution.py:25
  40.3 0.6 collective-permute-start.5
  40.9 2.6 %collective-permute-start.4 = (f32[160,128]{1,0:T(8,128)S(1)}, f32[160,128]{1,0:T(8,128)S(1)}, u32[]{:S(2)}, u32[]{:S(2)}) collective-permute-start(f32[160,128]{1,0:T(8,128)S(1)} %add_add_fusion), channel_id=1, source_target_pairs={{0,2},{1,3},{2,0},{3,1},{4,6},{5,7},{6,4},{7,5},{8,10},{9,11},{10,... | collective-permute-start | bytes 245768 | tf_op jit(solution)/shard_map/ppermute | solution.py:25
  43.5 2.6 %collective-permute-done.6 = f32[160,128]{1,0:T(8,128)S(1)} collective-permute-done((f32[160,128]{1,0:T(8,128)S(1)}, f32[160,128]{1,0:T(8,128)S(1)}, u32[]{:S(2)}, u32[]{:S(2)}) %collective-permute-start.6) | collective-permute-done | bytes 81952 | tf_op jit(solution)/shard_map/ppermute | solution.py:25
  46.0 2.0 %collective-permute-done.5 = f32[160,128]{1,0:T(8,128)S(1)} collective-permute-done((f32[160,128]{1,0:T(8,128)S(1)}, f32[160,128]{1,0:T(8,128)S(1)}, u32[]{:S(2)}, u32[]{:S(2)}) %collective-permute-start.5) | collective-permute-done | bytes 81952 | tf_op jit(solution)/shard_map/ppermute | solution.py:25
  48.1 0.0 collective-permute-done.4
  48.1 1.3 %collective-permute-start.9 = (bf16[160,128]{1,0:T(8,128)(2,1)S(1)}, bf16[160,128]{1,0:T(8,128)(2,1)S(1)}, u32[]{:S(2)}, u32[]{:S(2)}) collective-permute-start(bf16[160,128]{1,0:T(8,128)(2,1)S(1)} %multiply_convert_fusion.refs_0_), channel_id=1, source_target_pairs={{0,24},{8,16},{16,8},{24,0},{1,25},{9,17},{17,9},{25,1},{2,26},{10... | collective-permute-start | bytes 122888 | tf_op jit(solution)/shard_map/ppermute | solution.py:25
  49.4 1.1 %collective-permute-start.8 = (bf16[160,128]{1,0:T(8,128)(2,1)S(1)}, bf16[160,128]{1,0:T(8,128)(2,1)S(1)}, u32[]{:S(2)}, u32[]{:S(2)}) collective-permute-start(bf16[160,128]{1,0:T(8,128)(2,1)S(1)} %multiply_convert_fusion.refs_0_), channel_id=1, source_target_pairs={{0,16},{8,24},{16,0},{24,8},{1,17},{9,25},{17,1},{25,9},{2,18},{10... | collective-permute-start | bytes 122888 | tf_op jit(solution)/shard_map/ppermute | solution.py:25
  50.5 1.2 %collective-permute-start.7 = (bf16[160,128]{1,0:T(8,128)(2,1)S(1)}, bf16[160,128]{1,0:T(8,128)(2,1)S(1)}, u32[]{:S(2)}, u32[]{:S(2)}) collective-permute-start(bf16[160,128]{1,0:T(8,128)(2,1)S(1)} %multiply_convert_fusion.refs_0_), channel_id=1, source_target_pairs={{0,8},{8,0},{16,24},{24,16},{1,9},{9,1},{17,25},{25,17},{2,10},{10... | collective-permute-start | bytes 122888 | tf_op jit(solution)/shard_map/ppermute | solution.py:25
  51.7 0.0 collective-permute-start.10
  51.7 1.4 %collective-permute-done.9.refs_3_ = bf16[160,128]{1,0:T(8,128)(2,1)S(1)} collective-permute-done((bf16[160,128]{1,0:T(8,128)(2,1)S(1)}, bf16[160,128]{1,0:T(8,128)(2,1)S(1)}, u32[]{:S(2)}, u32[]{:S(2)}) %collective-permute-start.9) | collective-permute-done | bytes 40992 | tf_op jit(solution)/shard_map/ppermute | solution.py:25
  53.1 0.0 collective-permute-start.13
  53.1 0.4 collective-permute-done.8.refs_2_
  53.5 0.1 collective-permute-start.12
  53.6 0.9 %collective-permute-done.7.refs_1_ = bf16[160,128]{1,0:T(8,128)(2,1)S(1)} collective-permute-done((bf16[160,128]{1,0:T(8,128)(2,1)S(1)}, bf16[160,128]{1,0:T(8,128)(2,1)S(1)}, u32[]{:S(2)}, u32[]{:S(2)}) %collective-permute-start.7) | collective-permute-done | bytes 40992 | tf_op jit(solution)/shard_map/ppermute | solution.py:25
  54.5 0.0 collective-permute-start.11
  54.5 0.2 collective-permute-done.12.refs_6_
  54.7 1.0 %collective-permute-done.11.refs_5_ = bf16[160,128]{1,0:T(8,128)(2,1)S(1)} collective-permute-done((bf16[160,128]{1,0:T(8,128)(2,1)S(1)}, bf16[160,128]{1,0:T(8,128)(2,1)S(1)}, u32[]{:S(2)}, u32[]{:S(2)}) %collective-permute-start.11) | collective-permute-done | bytes 40992 | tf_op jit(solution)/shard_map/ppermute | solution.py:25
  55.7 1.4 %shard_map.19 = bf16[256,1536]{1,0:T(8,128)(2,1)S(1)} custom-call(bf16[256,1536]{1,0:T(8,128)(2,1)S(1)} %bitcast.13, bf16[256,1536]{1,0:T(8,128)(2,1)S(1)} %collective-permute-done.y_ref, bf16[160,128]{1,0:T(8,128)(2,1)S(1)} %multiply_convert_fusion.refs_0_, bf16[160,128]{1,0:T(8,128)(2,1)S(1)} %collective-permute-done.7.refs_1_, ...), custom_call_target="tpu_custom_call" | custom-call | tf_op jit(solution)/shard_map/pallas_call | solution.py:195
  57.1 23.5 %all_to_all.11 = bf16[16,16,1536]{2,1,0:T(8,128)(2,1)S(1)} all-to-all(bf16[16,16,1536]{2,1,0:T(8,128)(2,1)S(1)} %bitcast.14), channel_id=1, replica_groups={{20,28,24,2,18,0,6,16,4,22,14,8,26,12,30,10},{21,29,25,3,19,1,7,17,5,23..., dimensions={0} | all-to-all | bytes 1572864 | tf_op jit(solution)/shard_map/all_to_all | solution.py:196
  80.5 0.9 %copy.3 = bf16[16,2,8,1536]{3,2,0,1:T(8,128)(2,1)} copy(bf16[16,2,8,1536]{3,2,1,0:T(8,128)(2,1)S(1)} %bitcast.15) | data formatting | bytes 1572864 | tf_op jit(solution)/shard_map/reshape | solution.py:197
  (4 shorter events, 0.0 us)
Async XLA Ops:
  27.8 2.5 %collective-permute-start = (bf16[256,1536]{1,0:T(8,128)(2,1)S(1)}, bf16[256,1536]{1,0:T(8,128)(2,1)S(1)}, u32[]{:S(2)}, u32[]{:S(2)}) collective-permute-start(bf16[256,1536]{1,0:T(8,128)(2,1)S(1)} %bitcast.10), channel_id=1, source_target_pairs={{0,1},{1,0},{2,3},{3,2},{4,5},{5,4},{6,7},{7,6},{8,9},{9,8},{10,11... | collective-permute-start | bytes 2359304 | tf_op jit(solution)/shard_map/ppermute | solution.py:25
  30.7 4.8 %collective-permute-start.1 = (f32[160,128]{1,0:T(8,128)S(1)}, f32[160,128]{1,0:T(8,128)S(1)}, u32[]{:S(2)}, u32[]{:S(2)}) collective-permute-start(f32[160,128]{1,0:T(8,128)S(1)} %get-tuple-element.10), channel_id=1, source_target_pairs={{0,8},{8,0},{16,24},{24,16},{1,9},{9,1},{17,25},{25,17},{2,10},{10... | collective-permute-start | bytes 245768 | tf_op jit(solution)/shard_map/ppermute | solution.py:25
  32.3 4.5 %collective-permute-start.2 = (f32[160,128]{1,0:T(8,128)S(1)}, f32[160,128]{1,0:T(8,128)S(1)}, u32[]{:S(2)}, u32[]{:S(2)}) collective-permute-start(f32[160,128]{1,0:T(8,128)S(1)} %get-tuple-element.11), channel_id=1, source_target_pairs={{0,16},{8,24},{16,0},{24,8},{1,17},{9,25},{17,1},{25,9},{2,18},{10... | collective-permute-start | bytes 245768 | tf_op jit(solution)/shard_map/ppermute | solution.py:25
  33.6 5.3 %collective-permute-start.3 = (f32[160,128]{1,0:T(8,128)S(1)}, f32[160,128]{1,0:T(8,128)S(1)}, u32[]{:S(2)}, u32[]{:S(2)}) collective-permute-start(f32[160,128]{1,0:T(8,128)S(1)} %get-tuple-element.12), channel_id=1, source_target_pairs={{0,24},{8,16},{16,8},{24,0},{1,25},{9,17},{17,9},{25,1},{2,26},{10... | collective-permute-start | bytes 245768 | tf_op jit(solution)/shard_map/ppermute | solution.py:25
  39.0 7.0 %collective-permute-start.6 = (f32[160,128]{1,0:T(8,128)S(1)}, f32[160,128]{1,0:T(8,128)S(1)}, u32[]{:S(2)}, u32[]{:S(2)}) collective-permute-start(f32[160,128]{1,0:T(8,128)S(1)} %add_add_fusion), channel_id=1, source_target_pairs={{0,6},{1,7},{2,4},{3,5},{4,2},{5,3},{6,0},{7,1},{8,14},{9,15},{10,... | collective-permute-start | bytes 245768 | tf_op jit(solution)/shard_map/ppermute | solution.py:25
  40.3 7.8 %collective-permute-start.5 = (f32[160,128]{1,0:T(8,128)S(1)}, f32[160,128]{1,0:T(8,128)S(1)}, u32[]{:S(2)}, u32[]{:S(2)}) collective-permute-start(f32[160,128]{1,0:T(8,128)S(1)} %add_add_fusion), channel_id=1, source_target_pairs={{0,4},{1,5},{2,6},{3,7},{4,0},{5,1},{6,2},{7,3},{8,12},{9,13},{10,... | collective-permute-start | bytes 245768 | tf_op jit(solution)/shard_map/ppermute | solution.py:25
  40.9 7.2 %collective-permute-start.4 = (f32[160,128]{1,0:T(8,128)S(1)}, f32[160,128]{1,0:T(8,128)S(1)}, u32[]{:S(2)}, u32[]{:S(2)}) collective-permute-start(f32[160,128]{1,0:T(8,128)S(1)} %add_add_fusion), channel_id=1, source_target_pairs={{0,2},{1,3},{2,0},{3,1},{4,6},{5,7},{6,4},{7,5},{8,10},{9,11},{10,... | collective-permute-start | bytes 245768 | tf_op jit(solution)/shard_map/ppermute | solution.py:25
  48.1 5.0 %collective-permute-start.9 = (bf16[160,128]{1,0:T(8,128)(2,1)S(1)}, bf16[160,128]{1,0:T(8,128)(2,1)S(1)}, u32[]{:S(2)}, u32[]{:S(2)}) collective-permute-start(bf16[160,128]{1,0:T(8,128)(2,1)S(1)} %multiply_convert_fusion.refs_0_), channel_id=1, source_target_pairs={{0,24},{8,16},{16,8},{24,0},{1,25},{9,17},{17,9},{25,1},{2,26},{10... | collective-permute-start | bytes 122888 | tf_op jit(solution)/shard_map/ppermute | solution.py:25
  49.4 4.1 %collective-permute-start.8 = (bf16[160,128]{1,0:T(8,128)(2,1)S(1)}, bf16[160,128]{1,0:T(8,128)(2,1)S(1)}, u32[]{:S(2)}, u32[]{:S(2)}) collective-permute-start(bf16[160,128]{1,0:T(8,128)(2,1)S(1)} %multiply_convert_fusion.refs_0_), channel_id=1, source_target_pairs={{0,16},{8,24},{16,0},{24,8},{1,17},{9,25},{17,1},{25,9},{2,18},{10... | collective-permute-start | bytes 122888 | tf_op jit(solution)/shard_map/ppermute | solution.py:25
  50.5 4.0 %collective-permute-start.7 = (bf16[160,128]{1,0:T(8,128)(2,1)S(1)}, bf16[160,128]{1,0:T(8,128)(2,1)S(1)}, u32[]{:S(2)}, u32[]{:S(2)}) collective-permute-start(bf16[160,128]{1,0:T(8,128)(2,1)S(1)} %multiply_convert_fusion.refs_0_), channel_id=1, source_target_pairs={{0,8},{8,0},{16,24},{24,16},{1,9},{9,1},{17,25},{25,17},{2,10},{10... | collective-permute-start | bytes 122888 | tf_op jit(solution)/shard_map/ppermute | solution.py:25
  51.7 2.8 %collective-permute-start.10 = (bf16[160,128]{1,0:T(8,128)(2,1)S(1)}, bf16[160,128]{1,0:T(8,128)(2,1)S(1)}, u32[]{:S(2)}, u32[]{:S(2)}) collective-permute-start(bf16[160,128]{1,0:T(8,128)(2,1)S(1)} %multiply_convert_fusion.refs_0_), channel_id=1, source_target_pairs={{0,1},{1,0},{2,3},{3,2},{4,5},{5,4},{6,7},{7,6},{8,9},{9,8},{10,11... | collective-permute-start | bytes 122888 | tf_op jit(solution)/shard_map/ppermute | solution.py:25
  53.1 1.4 %collective-permute-start.13 = (bf16[160,128]{1,0:T(8,128)(2,1)S(1)}, bf16[160,128]{1,0:T(8,128)(2,1)S(1)}, u32[]{:S(2)}, u32[]{:S(2)}) collective-permute-start(bf16[160,128]{1,0:T(8,128)(2,1)S(1)} %collective-permute-done.9.refs_3_), channel_id=1, source_target_pairs={{0,1},{1,0},{2,3},{3,2},{4,5},{5,4},{6,7},{7,6},{8,9},{9,8},{10,11... | collective-permute-start | bytes 122888 | tf_op jit(solution)/shard_map/ppermute | solution.py:25
  53.5 1.2 %collective-permute-start.12 = (bf16[160,128]{1,0:T(8,128)(2,1)S(1)}, bf16[160,128]{1,0:T(8,128)(2,1)S(1)}, u32[]{:S(2)}, u32[]{:S(2)}) collective-permute-start(bf16[160,128]{1,0:T(8,128)(2,1)S(1)} %collective-permute-done.8.refs_2_), channel_id=1, source_target_pairs={{0,1},{1,0},{2,3},{3,2},{4,5},{5,4},{6,7},{7,6},{8,9},{9,8},{10,11... | collective-permute-start | bytes 122888 | tf_op jit(solution)/shard_map/ppermute | solution.py:25
  54.5 1.2 %collective-permute-start.11 = (bf16[160,128]{1,0:T(8,128)(2,1)S(1)}, bf16[160,128]{1,0:T(8,128)(2,1)S(1)}, u32[]{:S(2)}, u32[]{:S(2)}) collective-permute-start(bf16[160,128]{1,0:T(8,128)(2,1)S(1)} %collective-permute-done.7.refs_1_), channel_id=1, source_target_pairs={{0,1},{1,0},{2,3},{3,2},{4,5},{5,4},{6,7},{7,6},{8,9},{9,8},{10,11... | collective-permute-start | bytes 122888 | tf_op jit(solution)/shard_map/ppermute | solution.py:25

commit v7 on v6

--- a/solution.py
+++ b/solution.py
@@ -34,79 +34,81 @@
     return sorted(range(bands * levels), key=lambda q: (q // levels, abs(q % levels - levels // 2), q))
 
 
-def upper_blocks(count):
-    return [(i, j) for i in range(count) for j in range(i, count)]
-
-
-def own_gram(rows, width, share):
-    count = rows // BLOCK
+def squares():
+    shape = (BLOCK, BLOCK)
+    return lax.broadcasted_iota(jnp.int32, shape, 0), lax.broadcasted_iota(jnp.int32, shape, 1)
+
+
+def heights(bands):
+    body = 4 * BLOCK
+    piece = -(-(body + 8) // (8 * bands)) * 8
+    return body, piece * bands - body, piece
+
+
+def own_gram(width, share, bands):
+    _, tail, _ = heights(bands)
 
     def body(x_ref, out_ref):
-        eye = (
-            lax.broadcasted_iota(jnp.int32, (BLOCK, BLOCK), 0) == lax.broadcasted_iota(jnp.int32, (BLOCK, BLOCK), 1)
-        ).astype(jnp.float32) * share
+        row, column = squares()
         got = lax.dot_general(x_ref[...], x_ref[...], ACROSS, preferred_element_type=jnp.float32)
-        for p, (i, j) in enumerate(upper_blocks(count)):
-            block = got[i * BLOCK:(i + 1) * BLOCK, j * BLOCK:(j + 1) * BLOCK]
-            out_ref[p * BLOCK:(p + 1) * BLOCK, :] = block - eye if i == j else block
-
-    stacked = count * (count + 1) // 2 * BLOCK
+        eye = jnp.where(row == column, share, 0.0).astype(jnp.float32)
+        first, second = got[0:BLOCK, 0:BLOCK] - eye, got[BLOCK:, BLOCK:] - eye
+        out_ref[0:BLOCK, :] = jnp.where(row <= column, first, second)
+        out_ref[BLOCK:2 * BLOCK, :] = got[0:BLOCK, BLOCK:]
+        line = jnp.sum(jnp.where(row == column, second, 0.0), axis=0, keepdims=True)
+        out_ref[2 * BLOCK:2 * BLOCK + tail, :] = jnp.broadcast_to(line, (tail, BLOCK))
+
     return pl.pallas_call(
         body,
-        out_shape=jax.ShapeDtypeStruct((stacked, BLOCK), jnp.float32),
+        out_shape=jax.ShapeDtypeStruct((2 * BLOCK + tail, BLOCK), jnp.float32),
         compiler_params=VMEM_LIMIT,
         cost_estimate=pl.CostEstimate(
-            flops=2 * rows * rows * width, bytes_accessed=2 * rows * width, transcendentals=0
+            flops=8 * BLOCK * BLOCK * width, bytes_accessed=4 * BLOCK * width, transcendentals=0
         ),
     )
 
 
-def cross_gram(rows, width, bands):
-    count = rows // BLOCK
-    upper = count * (count + 1) // 2 * BLOCK
-    mid = rows // 2
-    stacked = upper + mid * count
-    piece = stacked // bands
+def cross_gram(width, bands):
+    whole, tail, piece = heights(bands)
 
     def body(x_ref, y_ref, own_ref, *refs):
         piece_refs, stack = refs[:-1], refs[-1]
         core, band = my_core(), lax.axis_index("band")
-        stack[0:upper, :] = own_ref[...]
+        stack[0:2 * BLOCK, :] = own_ref[0:2 * BLOCK, :]
+        stack[whole:whole + tail, :] = own_ref[2 * BLOCK:2 * BLOCK + tail, :]
 
         def put(left, right):
             got = lax.dot_general(left, right, ACROSS, preferred_element_type=jnp.float32)
-            for j in range(count):
-                stack[upper + j * mid:upper + (j + 1) * mid, :] = got[:, j * BLOCK:(j + 1) * BLOCK]
+            for j in range(2):
+                stack[(2 + j) * BLOCK:(3 + j) * BLOCK, :] = got[:, j * BLOCK:(j + 1) * BLOCK]
 
         @pl.when(core == 0)
         def _():
-            put(x_ref[0:mid, :], y_ref[...])
+            put(x_ref[0:BLOCK, :], y_ref[...])
 
         @pl.when(core == 1)
         def _():
-            put(y_ref[mid:rows, :], x_ref[...])
+            put(y_ref[BLOCK:2 * BLOCK, :], x_ref[...])
 
         for m in range(bands):
-            at = pl.ds(pl.multiple_of((band ^ m) * piece, piece), piece)
+            at = pl.ds(pl.multiple_of((band ^ m) * piece, 8), piece)
             piece_refs[m][...] = stack[at, :]
 
     return pl.pallas_call(
         body,
         out_shape=tuple(jax.ShapeDtypeStruct((piece, BLOCK), jnp.float32) for _ in range(bands)),
-        scratch_shapes=[pltpu.VMEM((stacked, BLOCK), jnp.float32)],
+        scratch_shapes=[pltpu.VMEM((whole + tail, BLOCK), jnp.float32)],
         compiler_params=VMEM_LIMIT,
         cost_estimate=pl.CostEstimate(
-            flops=rows * rows * width, bytes_accessed=4 * rows * width, transcendentals=0
+            flops=4 * BLOCK * BLOCK * width, bytes_accessed=8 * BLOCK * width, transcendentals=0
         ),
     )
 
 
-def correct(rows, width, bands, tall):
-    count = rows // BLOCK
-    upper = count * (count + 1) // 2 * BLOCK
-    mid = rows // 2
-    stacked = upper + mid * count
-    piece = stacked // bands
+def correct(width, bands, tall):
+    whole, tail, piece = heights(bands)
+    stacked = whole + tail
+    mid, rows = BLOCK, 2 * BLOCK
 
     def body(x_ref, y_ref, *refs):
         piece_refs, out_ref, packed, excess = refs[:-3], refs[-3], refs[-2], refs[-1]
@@ -114,30 +116,38 @@
         for side in range(2):
             for m in range(bands):
                 start = side * stacked + (band ^ m) * piece
-                packed[pl.ds(pl.multiple_of(start, 16), piece), :] = piece_refs[side * bands + m][...]
+                held = piece_refs[side * bands + m][...].astype(jnp.float32)
+                packed[pl.ds(pl.multiple_of(start, 8), piece), :] = held
+
+        def put(row, column, block):
+            at = (slice(row * BLOCK, (row + 1) * BLOCK), slice(column * BLOCK, (column + 1) * BLOCK))
+            excess[at] = block.astype(jnp.bfloat16)
+
+        row, column = squares()
         for side in range(2):
-            for p, (i, j) in enumerate(upper_blocks(count)):
-                at = side * stacked + p * BLOCK
-                block = packed[at:at + BLOCK, :]
-                row, column = side * rows + i * BLOCK, side * rows + j * BLOCK
-                excess[row:row + BLOCK, column:column + BLOCK] = block
-                if i != j:
-                    excess[column:column + BLOCK, row:row + BLOCK] = block.T
+            at = side * stacked
+            both, beside = packed[at:at + BLOCK, :], packed[at + BLOCK:at + 2 * BLOCK, :]
+            line = packed[at + whole:at + whole + 8, :][0:1, :]
+            turned = both.T
+            put(2 * side, 2 * side, jnp.where(row <= column, both, turned))
+            second = jnp.where(row > column, both, turned)
+            put(2 * side + 1, 2 * side + 1, jnp.where(row == column, line, second))
+            put(2 * side, 2 * side + 1, beside)
+            put(2 * side + 1, 2 * side, beside.T)
         for part in range(2):
-            for j in range(count):
-                start = (part ^ core) * stacked + upper + j * mid
-                block = packed[pl.ds(pl.multiple_of(start, 16), mid), :]
-                row, column = part * mid, j * BLOCK
+            for j in range(2):
+                start = (part ^ core) * stacked + (2 + j) * BLOCK
+                block = packed[pl.ds(pl.multiple_of(start, 8), BLOCK), :]
 
                 @pl.when(core == 0)
                 def _():
-                    excess[row:row + mid, rows + column:rows + column + BLOCK] = block
-                    excess[rows + column:rows + column + BLOCK, row:row + mid] = block.T
+                    put(part, 2 + j, block)
+                    put(2 + j, part, block.T)
 
                 @pl.when(core == 1)
                 def _():
-                    excess[rows + row:rows + row + mid, column:column + BLOCK] = block
-                    excess[column:column + BLOCK, rows + row:rows + row + mid] = block.T
+                    put(2 + part, j, block)
+                    put(j, 2 + part, block.T)
 
         mine = pl.ds(pl.multiple_of(core * mid, mid), mid)
         theirs = pl.ds(pl.multiple_of(rows + core * mid, mid), mid)
@@ -162,7 +172,7 @@
         body,
         out_shape=jax.ShapeDtypeStruct((rows, width), jnp.bfloat16),
         scratch_shapes=[
-            pltpu.VMEM((2 * stacked, BLOCK), jnp.bfloat16),
+            pltpu.VMEM((2 * stacked, BLOCK), jnp.float32),
             pltpu.VMEM((2 * rows, 2 * rows), jnp.bfloat16),
         ],
         compiler_params=VMEM_LIMIT,
@@ -181,8 +191,8 @@
     cut = functions.reshape(2, tall, chips, width).transpose(0, 2, 1, 3).reshape(devices, tall, width)
     x = lax.all_to_all(cut, BOTH, split_axis=0, concat_axis=0, axis_index_groups=order).reshape(rows, width)
     y = swap(x, "domain", 1)
-    own = own_gram(rows, width, NC // chips)(x)
-    pieces = cross_gram(rows, width, bands)(x, y, own)
+    own = own_gram(width, NC // chips, bands)(x)
+    pieces = cross_gram(width, bands)(x, y, own)
     total = pieces[0]
     for m in range(1, bands):
         total = total + swap(pieces[m], "band", m)
@@ -192,7 +202,7 @@
     excess = (heard[0] * (1.0 / NC)).astype(jnp.bfloat16)
     mine = [excess] + [swap(excess, "band", m) for m in range(1, bands)]
     other = [swap(e, "domain", 1) for e in mine]
-    out = correct(rows, width, bands, tall)(x, y, *mine, *other).reshape(chips, fdev, width)
+    out = correct(width, bands, tall)(x, y, *mine, *other).reshape(chips, fdev, width)
     back = lax.all_to_all(out, BOTH, split_axis=0, concat_axis=0, axis_index_groups=spread)
     return back.transpose(1, 0, 2).reshape(fdev, ncoef)
 
@@ -236,7 +246,7 @@
 
 def per_device(functions, pattern):
     nblocks, nonzero = pattern.shape
-    return (full_rows if nonzero == nblocks else some_rows)(functions, pattern)
+    return (full_rows if nonzero == nblocks == 4 else some_rows)(functions, pattern)
 
 
 def solution(mesh):

time: 81.7 us -> 80.7 us (0.988)
  waiting for transfers between devices: 14.7 us -> 13.5 us
    ppermute x14, waiting for transfers between devices: 14.7 us -> 13.5 us  [swap(): return lax.ppermute(value, axis, [(i, i ^ mask) for i in range(count)])]
  transfers between devices with their start and end apart: 14 -> 14, of which waited for: 11 -> 11; matrix products, arithmetic and copies ran while one was open for 0% -> 0% of each run, Pallas kernels for 0% -> 1%
where the time goes in v7:
time: 80.7 us; the launch traced here: 80.4 us
  blocking collectives  51.3 us (64%)
  waiting for transfers between devices  13.5 us (17%)
  starting transfers between devices  12.3 us (15%)
  Pallas kernels  2.3 us (3%)
  local copies, waits for them, and re-layouts  0.93 us (1%)
    all_to_all x1, blocking collectives, full_rows(): lax.all_to_all(cut, BOTH, split_axis=0, concat_axis=0, axis_index_groups=...  27.8 us
    all_to_all x1, blocking collectives, full_rows(): lax.all_to_all(out, BOTH, split_axis=0, concat_axis=0, axis_index_groups=...  23.5 us
    ppermute x14, waiting for transfers between devices, swap(): return lax.ppermute(value, axis, [(i, i ^ mask) for i in range(count)])  13.5 us
    ppermute x14, starting transfers between devices, swap(): return lax.ppermute(value, axis, [(i, i ^ mask) for i in range(count)])  12.3 us
  transfers between devices with their start and end apart: 14, of which 11 were waited for; matrix products, arithmetic and copies ran while one was open for 0% of the time, Pallas kernels for 1%

profile of v7, /device:TPU:0, one launch (start us, length us, event | category | flops | bytes accessed | tf_op | source)
XLA Modules:
  0.0 80.4 jit_solution(3223879338449032432)
XLA Ops:
  0.0 27.8 %all_to_all.10 = bf16[32,8,1536]{2,1,0:T(8,128)(2,1)S(1)} all-to-all(bf16[32,8,1536]{2,1,0:T(8,128)(2,1)} %bitcast.16), channel_id=1, replica_groups={{20,28,24,2,18,0,6,16,4,22,14,8,26,12,30,10,21,29,25,3,19,1,7,17,5,23,1..., dimensions={0} | all-to-all | bytes 1572864 | tf_op jit(solution)/shard_map/all_to_all | solution.py:192
  27.8 0.6 collective-permute-start
  28.4 0.4 shard_map.17.own_ref
  28.8 1.5 %collective-permute-done.y_ref = bf16[256,1536]{1,0:T(8,128)(2,1)S(1)} collective-permute-done((bf16[256,1536]{1,0:T(8,128)(2,1)S(1)}, bf16[256,1536]{1,0:T(8,128)(2,1)S(1)}, u32[]{:S(2)}, u32[]{:S(2)}) %collective-permute-start) | collective-permute-done | bytes 786464 | tf_op jit(solution)/shard_map/ppermute | solution.py:25
  30.3 0.4 shard_map.18
  30.7 1.6 %collective-permute-start.1 = (f32[136,128]{1,0:T(8,128)S(1)}, f32[136,128]{1,0:T(8,128)S(1)}, u32[]{:S(2)}, u32[]{:S(2)}) collective-permute-start(f32[136,128]{1,0:T(8,128)S(1)} %get-tuple-element.10), channel_id=1, source_target_pairs={{0,8},{8,0},{16,24},{24,16},{1,9},{9,1},{17,25},{25,17},{2,10},{10... | collective-permute-start | bytes 208904 | tf_op jit(solution)/shard_map/ppermute | solution.py:25
  32.3 1.3 %collective-permute-start.2 = (f32[136,128]{1,0:T(8,128)S(1)}, f32[136,128]{1,0:T(8,128)S(1)}, u32[]{:S(2)}, u32[]{:S(2)}) collective-permute-start(f32[136,128]{1,0:T(8,128)S(1)} %get-tuple-element.11), channel_id=1, source_target_pairs={{0,16},{8,24},{16,0},{24,8},{1,17},{9,25},{17,1},{25,9},{2,18},{10... | collective-permute-start | bytes 208904 | tf_op jit(solution)/shard_map/ppermute | solution.py:25
  33.6 0.7 collective-permute-start.3
  34.3 1.0 %collective-permute-done.1 = f32[136,128]{1,0:T(8,128)S(1)} collective-permute-done((f32[136,128]{1,0:T(8,128)S(1)}, f32[136,128]{1,0:T(8,128)S(1)}, u32[]{:S(2)}, u32[]{:S(2)}) %collective-permute-start.1) | collective-permute-done | bytes 69664 | tf_op jit(solution)/shard_map/ppermute | solution.py:25
  35.3 1.3 %collective-permute-done.2 = f32[136,128]{1,0:T(8,128)S(1)} collective-permute-done((f32[136,128]{1,0:T(8,128)S(1)}, f32[136,128]{1,0:T(8,128)S(1)}, u32[]{:S(2)}, u32[]{:S(2)}) %collective-permute-start.2) | collective-permute-done | bytes 69664 | tf_op jit(solution)/shard_map/ppermute | solution.py:25
  36.6 2.2 %collective-permute-done.3 = f32[136,128]{1,0:T(8,128)S(1)} collective-permute-done((f32[136,128]{1,0:T(8,128)S(1)}, f32[136,128]{1,0:T(8,128)S(1)}, u32[]{:S(2)}, u32[]{:S(2)}) %collective-permute-start.3) | collective-permute-done | bytes 69664 | tf_op jit(solution)/shard_map/ppermute | solution.py:25
  38.9 1.0 %collective-permute-start.6 = (f32[136,128]{1,0:T(8,128)S(1)}, f32[136,128]{1,0:T(8,128)S(1)}, u32[]{:S(2)}, u32[]{:S(2)}) collective-permute-start(f32[136,128]{1,0:T(8,128)S(1)} %add_add_fusion), channel_id=1, source_target_pairs={{0,6},{1,7},{2,4},{3,5},{4,2},{5,3},{6,0},{7,1},{8,14},{9,15},{10,... | collective-permute-start | bytes 208904 | tf_op jit(solution)/shard_map/ppermute | solution.py:25
  39.9 0.6 collective-permute-start.5
  40.5 2.8 %collective-permute-start.4 = (f32[136,128]{1,0:T(8,128)S(1)}, f32[136,128]{1,0:T(8,128)S(1)}, u32[]{:S(2)}, u32[]{:S(2)}) collective-permute-start(f32[136,128]{1,0:T(8,128)S(1)} %add_add_fusion), channel_id=1, source_target_pairs={{0,2},{1,3},{2,0},{3,1},{4,6},{5,7},{6,4},{7,5},{8,10},{9,11},{10,... | collective-permute-start | bytes 208904 | tf_op jit(solution)/shard_map/ppermute | solution.py:25
  43.3 1.8 %collective-permute-done.6 = f32[136,128]{1,0:T(8,128)S(1)} collective-permute-done((f32[136,128]{1,0:T(8,128)S(1)}, f32[136,128]{1,0:T(8,128)S(1)}, u32[]{:S(2)}, u32[]{:S(2)}) %collective-permute-start.6) | collective-permute-done | bytes 69664 | tf_op jit(solution)/shard_map/ppermute | solution.py:25
  45.2 1.8 %collective-permute-done.5 = f32[136,128]{1,0:T(8,128)S(1)} collective-permute-done((f32[136,128]{1,0:T(8,128)S(1)}, f32[136,128]{1,0:T(8,128)S(1)}, u32[]{:S(2)}, u32[]{:S(2)}) %collective-permute-start.5) | collective-permute-done | bytes 69664 | tf_op jit(solution)/shard_map/ppermute | solution.py:25
  47.0 1.3 %collective-permute-start.9 = (bf16[136,128]{1,0:T(8,128)(2,1)S(1)}, bf16[136,128]{1,0:T(8,128)(2,1)S(1)}, u32[]{:S(2)}, u32[]{:S(2)}) collective-permute-start(bf16[136,128]{1,0:T(8,128)(2,1)S(1)} %multiply_convert_fusion.refs_0_), channel_id=1, source_target_pairs={{0,24},{8,16},{16,8},{24,0},{1,25},{9,17},{17,9},{25,1},{2,26},{10... | collective-permute-start | bytes 104456 | tf_op jit(solution)/shard_map/ppermute | solution.py:25
  48.3 1.1 %collective-permute-start.8 = (bf16[136,128]{1,0:T(8,128)(2,1)S(1)}, bf16[136,128]{1,0:T(8,128)(2,1)S(1)}, u32[]{:S(2)}, u32[]{:S(2)}) collective-permute-start(bf16[136,128]{1,0:T(8,128)(2,1)S(1)} %multiply_convert_fusion.refs_0_), channel_id=1, source_target_pairs={{0,16},{8,24},{16,0},{24,8},{1,17},{9,25},{17,1},{25,9},{2,18},{10... | collective-permute-start | bytes 104456 | tf_op jit(solution)/shard_map/ppermute | solution.py:25
  49.4 1.1 %collective-permute-start.7 = (bf16[136,128]{1,0:T(8,128)(2,1)S(1)}, bf16[136,128]{1,0:T(8,128)(2,1)S(1)}, u32[]{:S(2)}, u32[]{:S(2)}) collective-permute-start(bf16[136,128]{1,0:T(8,128)(2,1)S(1)} %multiply_convert_fusion.refs_0_), channel_id=1, source_target_pairs={{0,8},{8,0},{16,24},{24,16},{1,9},{9,1},{17,25},{25,17},{2,10},{10... | collective-permute-start | bytes 104456 | tf_op jit(solution)/shard_map/ppermute | solution.py:25
  50.6 0.0 collective-permute-start.10
  50.6 1.3 %collective-permute-done.9.refs_3_ = bf16[136,128]{1,0:T(8,128)(2,1)S(1)} collective-permute-done((bf16[136,128]{1,0:T(8,128)(2,1)S(1)}, bf16[136,128]{1,0:T(8,128)(2,1)S(1)}, u32[]{:S(2)}, u32[]{:S(2)}) %collective-permute-start.9) | collective-permute-done | bytes 34848 | tf_op jit(solution)/shard_map/ppermute | solution.py:25
  51.9 0.0 collective-permute-start.13
  51.9 0.4 collective-permute-done.8.refs_2_
  52.3 0.1 collective-permute-start.12
  52.4 0.9 %collective-permute-done.7.refs_1_ = bf16[136,128]{1,0:T(8,128)(2,1)S(1)} collective-permute-done((bf16[136,128]{1,0:T(8,128)(2,1)S(1)}, bf16[136,128]{1,0:T(8,128)(2,1)S(1)}, u32[]{:S(2)}, u32[]{:S(2)}) %collective-permute-start.7) | collective-permute-done | bytes 34848 | tf_op jit(solution)/shard_map/ppermute | solution.py:25
  53.3 0.0 collective-permute-start.11
  53.3 0.0 collective-permute-done.10.refs_4_
  53.4 0.1 collective-permute-done.12.refs_6_
  53.5 1.1 %collective-permute-done.11.refs_5_ = bf16[136,128]{1,0:T(8,128)(2,1)S(1)} collective-permute-done((bf16[136,128]{1,0:T(8,128)(2,1)S(1)}, bf16[136,128]{1,0:T(8,128)(2,1)S(1)}, u32[]{:S(2)}, u32[]{:S(2)}) %collective-permute-start.11) | collective-permute-done | bytes 34848 | tf_op jit(solution)/shard_map/ppermute | solution.py:25
  54.6 1.5 %shard_map.19 = bf16[256,1536]{1,0:T(8,128)(2,1)S(1)} custom-call(bf16[256,1536]{1,0:T(8,128)(2,1)S(1)} %bitcast.13, bf16[256,1536]{1,0:T(8,128)(2,1)S(1)} %collective-permute-done.y_ref, bf16[136,128]{1,0:T(8,128)(2,1)S(1)} %multiply_convert_fusion.refs_0_, bf16[136,128]{1,0:T(8,128)(2,1)S(1)} %collective-permute-done.7.refs_1_, ...), custom_call_target="tpu_custom_call" | custom-call | tf_op jit(solution)/shard_map/pallas_call | solution.py:205
  56.0 23.5 %all_to_all.11 = bf16[16,16,1536]{2,1,0:T(8,128)(2,1)S(1)} all-to-all(bf16[16,16,1536]{2,1,0:T(8,128)(2,1)S(1)} %bitcast.14), channel_id=1, replica_groups={{20,28,24,2,18,0,6,16,4,22,14,8,26,12,30,10},{21,29,25,3,19,1,7,17,5,23..., dimensions={0} | all-to-all | bytes 1572864 | tf_op jit(solution)/shard_map/all_to_all | solution.py:206
  79.5 0.9 %copy.3 = bf16[16,2,8,1536]{3,2,0,1:T(8,128)(2,1)} copy(bf16[16,2,8,1536]{3,2,1,0:T(8,128)(2,1)S(1)} %bitcast.15) | data formatting | bytes 1572864 | tf_op jit(solution)/shard_map/reshape | solution.py:207
  (4 shorter events, 0.1 us)
Async XLA Ops:
  27.8 2.5 %collective-permute-start = (bf16[256,1536]{1,0:T(8,128)(2,1)S(1)}, bf16[256,1536]{1,0:T(8,128)(2,1)S(1)}, u32[]{:S(2)}, u32[]{:S(2)}) collective-permute-start(bf16[256,1536]{1,0:T(8,128)(2,1)S(1)} %bitcast.10), channel_id=1, source_target_pairs={{0,1},{1,0},{2,3},{3,2},{4,5},{5,4},{6,7},{7,6},{8,9},{9,8},{10,11... | collective-permute-start | bytes 2359304 | tf_op jit(solution)/shard_map/ppermute | solution.py:25
  30.7 4.5 %collective-permute-start.1 = (f32[136,128]{1,0:T(8,128)S(1)}, f32[136,128]{1,0:T(8,128)S(1)}, u32[]{:S(2)}, u32[]{:S(2)}) collective-permute-start(f32[136,128]{1,0:T(8,128)S(1)} %get-tuple-element.10), channel_id=1, source_target_pairs={{0,8},{8,0},{16,24},{24,16},{1,9},{9,1},{17,25},{25,17},{2,10},{10... | collective-permute-start | bytes 208904 | tf_op jit(solution)/shard_map/ppermute | solution.py:25
  32.3 4.3 %collective-permute-start.2 = (f32[136,128]{1,0:T(8,128)S(1)}, f32[136,128]{1,0:T(8,128)S(1)}, u32[]{:S(2)}, u32[]{:S(2)}) collective-permute-start(f32[136,128]{1,0:T(8,128)S(1)} %get-tuple-element.11), channel_id=1, source_target_pairs={{0,16},{8,24},{16,0},{24,8},{1,17},{9,25},{17,1},{25,9},{2,18},{10... | collective-permute-start | bytes 208904 | tf_op jit(solution)/shard_map/ppermute | solution.py:25
  33.6 5.2 %collective-permute-start.3 = (f32[136,128]{1,0:T(8,128)S(1)}, f32[136,128]{1,0:T(8,128)S(1)}, u32[]{:S(2)}, u32[]{:S(2)}) collective-permute-start(f32[136,128]{1,0:T(8,128)S(1)} %get-tuple-element.12), channel_id=1, source_target_pairs={{0,24},{8,16},{16,8},{24,0},{1,25},{9,17},{17,9},{25,1},{2,26},{10... | collective-permute-start | bytes 208904 | tf_op jit(solution)/shard_map/ppermute | solution.py:25
  38.9 6.3 %collective-permute-start.6 = (f32[136,128]{1,0:T(8,128)S(1)}, f32[136,128]{1,0:T(8,128)S(1)}, u32[]{:S(2)}, u32[]{:S(2)}) collective-permute-start(f32[136,128]{1,0:T(8,128)S(1)} %add_add_fusion), channel_id=1, source_target_pairs={{0,6},{1,7},{2,4},{3,5},{4,2},{5,3},{6,0},{7,1},{8,14},{9,15},{10,... | collective-permute-start | bytes 208904 | tf_op jit(solution)/shard_map/ppermute | solution.py:25
  39.9 7.1 %collective-permute-start.5 = (f32[136,128]{1,0:T(8,128)S(1)}, f32[136,128]{1,0:T(8,128)S(1)}, u32[]{:S(2)}, u32[]{:S(2)}) collective-permute-start(f32[136,128]{1,0:T(8,128)S(1)} %add_add_fusion), channel_id=1, source_target_pairs={{0,4},{1,5},{2,6},{3,7},{4,0},{5,1},{6,2},{7,3},{8,12},{9,13},{10,... | collective-permute-start | bytes 208904 | tf_op jit(solution)/shard_map/ppermute | solution.py:25
  40.5 6.5 %collective-permute-start.4 = (f32[136,128]{1,0:T(8,128)S(1)}, f32[136,128]{1,0:T(8,128)S(1)}, u32[]{:S(2)}, u32[]{:S(2)}) collective-permute-start(f32[136,128]{1,0:T(8,128)S(1)} %add_add_fusion), channel_id=1, source_target_pairs={{0,2},{1,3},{2,0},{3,1},{4,6},{5,7},{6,4},{7,5},{8,10},{9,11},{10,... | collective-permute-start | bytes 208904 | tf_op jit(solution)/shard_map/ppermute | solution.py:25
  47.0 4.9 %collective-permute-start.9 = (bf16[136,128]{1,0:T(8,128)(2,1)S(1)}, bf16[136,128]{1,0:T(8,128)(2,1)S(1)}, u32[]{:S(2)}, u32[]{:S(2)}) collective-permute-start(bf16[136,128]{1,0:T(8,128)(2,1)S(1)} %multiply_convert_fusion.refs_0_), channel_id=1, source_target_pairs={{0,24},{8,16},{16,8},{24,0},{1,25},{9,17},{17,9},{25,1},{2,26},{10... | collective-permute-start | bytes 104456 | tf_op jit(solution)/shard_map/ppermute | solution.py:25
  48.3 4.0 %collective-permute-start.8 = (bf16[136,128]{1,0:T(8,128)(2,1)S(1)}, bf16[136,128]{1,0:T(8,128)(2,1)S(1)}, u32[]{:S(2)}, u32[]{:S(2)}) collective-permute-start(bf16[136,128]{1,0:T(8,128)(2,1)S(1)} %multiply_convert_fusion.refs_0_), channel_id=1, source_target_pairs={{0,16},{8,24},{16,0},{24,8},{1,17},{9,25},{17,1},{25,9},{2,18},{10... | collective-permute-start | bytes 104456 | tf_op jit(solution)/shard_map/ppermute | solution.py:25
  49.4 3.9 %collective-permute-start.7 = (bf16[136,128]{1,0:T(8,128)(2,1)S(1)}, bf16[136,128]{1,0:T(8,128)(2,1)S(1)}, u32[]{:S(2)}, u32[]{:S(2)}) collective-permute-start(bf16[136,128]{1,0:T(8,128)(2,1)S(1)} %multiply_convert_fusion.refs_0_), channel_id=1, source_target_pairs={{0,8},{8,0},{16,24},{24,16},{1,9},{9,1},{17,25},{25,17},{2,10},{10... | collective-permute-start | bytes 104456 | tf_op jit(solution)/shard_map/ppermute | solution.py:25
  50.6 2.8 %collective-permute-start.10 = (bf16[136,128]{1,0:T(8,128)(2,1)S(1)}, bf16[136,128]{1,0:T(8,128)(2,1)S(1)}, u32[]{:S(2)}, u32[]{:S(2)}) collective-permute-start(bf16[136,128]{1,0:T(8,128)(2,1)S(1)} %multiply_convert_fusion.refs_0_), channel_id=1, source_target_pairs={{0,1},{1,0},{2,3},{3,2},{4,5},{5,4},{6,7},{7,6},{8,9},{9,8},{10,11... | collective-permute-start | bytes 104456 | tf_op jit(solution)/shard_map/ppermute | solution.py:25
  51.9 1.5 %collective-permute-start.13 = (bf16[136,128]{1,0:T(8,128)(2,1)S(1)}, bf16[136,128]{1,0:T(8,128)(2,1)S(1)}, u32[]{:S(2)}, u32[]{:S(2)}) collective-permute-start(bf16[136,128]{1,0:T(8,128)(2,1)S(1)} %collective-permute-done.9.refs_3_), channel_id=1, source_target_pairs={{0,1},{1,0},{2,3},{3,2},{4,5},{5,4},{6,7},{7,6},{8,9},{9,8},{10,11... | collective-permute-start | bytes 104456 | tf_op jit(solution)/shard_map/ppermute | solution.py:25
  52.3 1.2 %collective-permute-start.12 = (bf16[136,128]{1,0:T(8,128)(2,1)S(1)}, bf16[136,128]{1,0:T(8,128)(2,1)S(1)}, u32[]{:S(2)}, u32[]{:S(2)}) collective-permute-start(bf16[136,128]{1,0:T(8,128)(2,1)S(1)} %collective-permute-done.8.refs_2_), channel_id=1, source_target_pairs={{0,1},{1,0},{2,3},{3,2},{4,5},{5,4},{6,7},{7,6},{8,9},{9,8},{10,11... | collective-permute-start | bytes 104456 | tf_op jit(solution)/shard_map/ppermute | solution.py:25
  53.3 1.2 %collective-permute-start.11 = (bf16[136,128]{1,0:T(8,128)(2,1)S(1)}, bf16[136,128]{1,0:T(8,128)(2,1)S(1)}, u32[]{:S(2)}, u32[]{:S(2)}) collective-permute-start(bf16[136,128]{1,0:T(8,128)(2,1)S(1)} %collective-permute-done.7.refs_1_), channel_id=1, source_target_pairs={{0,1},{1,0},{2,3},{3,2},{4,5},{5,4},{6,7},{7,6},{8,9},{9,8},{10,11... | collective-permute-start | bytes 104456 | tf_op jit(solution)/shard_map/ppermute | solution.py:25

commit v8 on v7

--- a/solution.py
+++ b/solution.py
@@ -105,10 +105,10 @@
     )
 
 
-def correct(width, bands, tall):
+def correct(width, bands):
     whole, tail, piece = heights(bands)
     stacked = whole + tail
-    mid, rows = BLOCK, 2 * BLOCK
+    rows = 2 * BLOCK
 
     def body(x_ref, y_ref, *refs):
         piece_refs, out_ref, packed, excess = refs[:-3], refs[-3], refs[-2], refs[-1]
@@ -149,23 +149,16 @@
                     put(2 + part, j, block)
                     put(j, 2 + part, block.T)
 
-        mine = pl.ds(pl.multiple_of(core * mid, mid), mid)
-        theirs = pl.ds(pl.multiple_of(rows + core * mid, mid), mid)
-        own = jnp.concatenate([excess[mine, :], excess[theirs, :]], axis=0)
+        own = excess[0:rows, :]
         twice = jnp.dot(own, excess[...], preferred_element_type=jnp.float32)
         change = 0.375 * twice - 0.5 * own.astype(jnp.float32)
-        row = lax.broadcasted_iota(jnp.int32, (rows, 2 * rows), 0)
-        column = lax.broadcasted_iota(jnp.int32, (rows, 2 * rows), 1)
-        diagonal = column == row + core * mid + jnp.where(row < mid, 0, rows - mid)
+        place = (rows, 2 * rows)
+        diagonal = lax.broadcasted_iota(jnp.int32, place, 0) == lax.broadcasted_iota(jnp.int32, place, 1)
         weight = 1.0 + jnp.sum(jnp.where(diagonal, change, 0.0), axis=1, keepdims=True)
         change = jnp.where(diagonal, 0.0, change).astype(jnp.bfloat16)
-        out = jnp.concatenate([x_ref[mine, :], y_ref[mine, :]], axis=0).astype(jnp.float32) * weight
+        out = x_ref[...].astype(jnp.float32) * weight
         out += jnp.dot(change[:, 0:rows], x_ref[...], preferred_element_type=jnp.float32)
         out += jnp.dot(change[:, rows:2 * rows], y_ref[...], preferred_element_type=jnp.float32)
-        near, far = out[0:mid], out[mid:rows]
-        upper_half = jnp.where(core == 0, near, far).reshape(mid // tall, tall, width)
-        lower_half = jnp.where(core == 0, far, near).reshape(mid // tall, tall, width)
-        out = jnp.concatenate([upper_half, lower_half], axis=1).reshape(rows, width)
         out_ref[...] = out.astype(jnp.bfloat16)
 
     return pl.pallas_call(
@@ -184,12 +177,10 @@
     devices, levels = bands * domains, domains // 2
     chips = devices // 2
     fdev, ncoef = functions.shape
-    tall, width = fdev // 2, ncoef // chips
-    rows = devices * tall
+    width, rows = ncoef // chips, chips * fdev
     spread = [[2 * q + c for q in chip_order(bands, levels)] for c in range(2)]
-    order = [spread[0] + spread[1]]
-    cut = functions.reshape(2, tall, chips, width).transpose(0, 2, 1, 3).reshape(devices, tall, width)
-    x = lax.all_to_all(cut, BOTH, split_axis=0, concat_axis=0, axis_index_groups=order).reshape(rows, width)
+    cut = functions.reshape(fdev, chips, width).transpose(1, 0, 2)
+    x = lax.all_to_all(cut, BOTH, split_axis=0, concat_axis=0, axis_index_groups=spread).reshape(rows, width)
     y = swap(x, "domain", 1)
     own = own_gram(width, NC // chips, bands)(x)
     pieces = cross_gram(width, bands)(x, y, own)
@@ -202,7 +193,7 @@
     excess = (heard[0] * (1.0 / NC)).astype(jnp.bfloat16)
     mine = [excess] + [swap(excess, "band", m) for m in range(1, bands)]
     other = [swap(e, "domain", 1) for e in mine]
-    out = correct(width, bands, tall)(x, y, *mine, *other).reshape(chips, fdev, width)
+    out = correct(width, bands)(x, y, *mine, *other).reshape(chips, fdev, width)
     back = lax.all_to_all(out, BOTH, split_axis=0, concat_axis=0, axis_index_groups=spread)
     return back.transpose(1, 0, 2).reshape(fdev, ncoef)
 

time: 80.7 us -> 79.9 us (0.990)
  blocking collectives: 51.3 us -> 49.6 us
  local copies, waits for them, and re-layouts: 0.93 us -> 2.14 us
    all_to_all x1, blocking collectives: 27.8 us -> 26.2 us  [full_rows(): lax.all_to_all(cut, BOTH, split_axis=0, concat_axis=0, axis_index_groups=...]
    reshape x0 -> x1, local copies, waits for them, and re-layouts: none -> 1.21 us  [full_rows(): cut = functions.reshape(fdev, chips, width).transpose(1, 0, 2)]
  transfers between devices with their start and end apart: 14 -> 14, of which waited for: 11 -> 10; matrix products, arithmetic and copies ran while one was open for 0% -> 0% of each run, Pallas kernels for 1% -> 1%
where the time goes in v8:
time: 79.9 us; the launch traced here: 79.7 us
  blocking collectives  49.6 us (62%)
  waiting for transfers between devices  14 us (18%)
  starting transfers between devices  11.7 us (15%)
  local copies, waits for them, and re-layouts  2.14 us (3%)
  Pallas kernels  2.14 us (3%)
    all_to_all x1, blocking collectives, full_rows(): lax.all_to_all(cut, BOTH, split_axis=0, concat_axis=0, axis_index_groups=...  26.2 us
    all_to_all x1, blocking collectives, full_rows(): lax.all_to_all(out, BOTH, split_axis=0, concat_axis=0, axis_index_groups=...  23.4 us
    ppermute x14, waiting for transfers between devices, swap(): return lax.ppermute(value, axis, [(i, i ^ mask) for i in range(count)])  14 us
    ppermute x14, starting transfers between devices, swap(): return lax.ppermute(value, axis, [(i, i ^ mask) for i in range(count)])  11.7 us
  transfers between devices with their start and end apart: 14, of which 10 were waited for; matrix products, arithmetic and copies ran while one was open for 0% of the time, Pallas kernels for 1%

profile of v8, /device:TPU:0, one launch (start us, length us, event | category | flops | bytes accessed | tf_op | source)
XLA Modules:
  0.0 79.7 jit_solution(8153767483869074567)
XLA Ops:
  0.0 1.2 %copy.7 = bf16[2,16,8,1536]{3,2,0,1:T(8,128)(2,1)S(1)} copy(bf16[2,16,8,1536]{3,2,1,0:T(8,128)(2,1)} %bitcast.19) | data formatting | bytes 1572864 | tf_op jit(solution)/shard_map/reshape | solution.py:182
  1.2 26.2 %all_to_all.10 = bf16[16,16,1536]{2,1,0:T(8,128)(2,1)S(1)} all-to-all(bf16[16,16,1536]{2,1,0:T(8,128)(2,1)S(1)} %bitcast.18), channel_id=1, replica_groups={{20,28,24,2,18,0,6,16,4,22,14,8,26,12,30,10},{21,29,25,3,19,1,7,17,5,23..., dimensions={0} | all-to-all | bytes 1572864 | tf_op jit(solution)/shard_map/all_to_all | solution.py:183
  27.4 0.0 collective-permute-start
  27.4 0.4 shard_map.17.own_ref
  27.8 1.9 %collective-permute-done.y_ref = bf16[256,1536]{1,0:T(8,128)(2,1)S(1)} collective-permute-done((bf16[256,1536]{1,0:T(8,128)(2,1)S(1)}, bf16[256,1536]{1,0:T(8,128)(2,1)S(1)}, u32[]{:S(2)}, u32[]{:S(2)}) %collective-permute-start) | collective-permute-done | bytes 786464 | tf_op jit(solution)/shard_map/ppermute | solution.py:25
  29.7 0.4 shard_map.18
  30.1 1.0 %collective-permute-start.1 = (f32[136,128]{1,0:T(8,128)S(1)}, f32[136,128]{1,0:T(8,128)S(1)}, u32[]{:S(2)}, u32[]{:S(2)}) collective-permute-start(f32[136,128]{1,0:T(8,128)S(1)} %get-tuple-element.10), channel_id=1, source_target_pairs={{0,8},{8,0},{16,24},{24,16},{1,9},{9,1},{17,25},{25,17},{2,10},{10... | collective-permute-start | bytes 208904 | tf_op jit(solution)/shard_map/ppermute | solution.py:25
  31.1 1.6 %collective-permute-start.2 = (f32[136,128]{1,0:T(8,128)S(1)}, f32[136,128]{1,0:T(8,128)S(1)}, u32[]{:S(2)}, u32[]{:S(2)}) collective-permute-start(f32[136,128]{1,0:T(8,128)S(1)} %get-tuple-element.11), channel_id=1, source_target_pairs={{0,16},{8,24},{16,0},{24,8},{1,17},{9,25},{17,1},{25,9},{2,18},{10... | collective-permute-start | bytes 208904 | tf_op jit(solution)/shard_map/ppermute | solution.py:25
  32.8 0.9 %collective-permute-start.3 = (f32[136,128]{1,0:T(8,128)S(1)}, f32[136,128]{1,0:T(8,128)S(1)}, u32[]{:S(2)}, u32[]{:S(2)}) collective-permute-start(f32[136,128]{1,0:T(8,128)S(1)} %get-tuple-element.12), channel_id=1, source_target_pairs={{0,24},{8,16},{16,8},{24,0},{1,25},{9,17},{17,9},{25,1},{2,26},{10... | collective-permute-start | bytes 208904 | tf_op jit(solution)/shard_map/ppermute | solution.py:25
  33.7 0.8 %collective-permute-done.1 = f32[136,128]{1,0:T(8,128)S(1)} collective-permute-done((f32[136,128]{1,0:T(8,128)S(1)}, f32[136,128]{1,0:T(8,128)S(1)}, u32[]{:S(2)}, u32[]{:S(2)}) %collective-permute-start.1) | collective-permute-done | bytes 69664 | tf_op jit(solution)/shard_map/ppermute | solution.py:25
  34.5 0.9 %collective-permute-done.2 = f32[136,128]{1,0:T(8,128)S(1)} collective-permute-done((f32[136,128]{1,0:T(8,128)S(1)}, f32[136,128]{1,0:T(8,128)S(1)}, u32[]{:S(2)}, u32[]{:S(2)}) %collective-permute-start.2) | collective-permute-done | bytes 69664 | tf_op jit(solution)/shard_map/ppermute | solution.py:25
  35.5 2.5 %collective-permute-done.3 = f32[136,128]{1,0:T(8,128)S(1)} collective-permute-done((f32[136,128]{1,0:T(8,128)S(1)}, f32[136,128]{1,0:T(8,128)S(1)}, u32[]{:S(2)}, u32[]{:S(2)}) %collective-permute-start.3) | collective-permute-done | bytes 69664 | tf_op jit(solution)/shard_map/ppermute | solution.py:25
  38.0 2.9 %collective-permute-start.6 = (f32[136,128]{1,0:T(8,128)S(1)}, f32[136,128]{1,0:T(8,128)S(1)}, u32[]{:S(2)}, u32[]{:S(2)}) collective-permute-start(f32[136,128]{1,0:T(8,128)S(1)} %add_add_fusion), channel_id=1, source_target_pairs={{0,6},{1,7},{2,4},{3,5},{4,2},{5,3},{6,0},{7,1},{8,14},{9,15},{10,... | collective-permute-start | bytes 208904 | tf_op jit(solution)/shard_map/ppermute | solution.py:25
  40.9 1.6 %collective-permute-start.4 = (f32[136,128]{1,0:T(8,128)S(1)}, f32[136,128]{1,0:T(8,128)S(1)}, u32[]{:S(2)}, u32[]{:S(2)}) collective-permute-start(f32[136,128]{1,0:T(8,128)S(1)} %add_add_fusion), channel_id=1, source_target_pairs={{0,2},{1,3},{2,0},{3,1},{4,6},{5,7},{6,4},{7,5},{8,10},{9,11},{10,... | collective-permute-start | bytes 208904 | tf_op jit(solution)/shard_map/ppermute | solution.py:25
  42.4 2.2 %collective-permute-done.6 = f32[136,128]{1,0:T(8,128)S(1)} collective-permute-done((f32[136,128]{1,0:T(8,128)S(1)}, f32[136,128]{1,0:T(8,128)S(1)}, u32[]{:S(2)}, u32[]{:S(2)}) %collective-permute-start.6) | collective-permute-done | bytes 69664 | tf_op jit(solution)/shard_map/ppermute | solution.py:25
  44.6 1.8 %collective-permute-done.5 = f32[136,128]{1,0:T(8,128)S(1)} collective-permute-done((f32[136,128]{1,0:T(8,128)S(1)}, f32[136,128]{1,0:T(8,128)S(1)}, u32[]{:S(2)}, u32[]{:S(2)}) %collective-permute-start.5) | collective-permute-done | bytes 69664 | tf_op jit(solution)/shard_map/ppermute | solution.py:25
  46.4 0.0 collective-permute-done.4
  46.4 1.1 %collective-permute-start.9 = (bf16[136,128]{1,0:T(8,128)(2,1)S(1)}, bf16[136,128]{1,0:T(8,128)(2,1)S(1)}, u32[]{:S(2)}, u32[]{:S(2)}) collective-permute-start(bf16[136,128]{1,0:T(8,128)(2,1)S(1)} %multiply_convert_fusion.refs_0_), channel_id=1, source_target_pairs={{0,24},{8,16},{16,8},{24,0},{1,25},{9,17},{17,9},{25,1},{2,26},{10... | collective-permute-start | bytes 104456 | tf_op jit(solution)/shard_map/ppermute | solution.py:25
  47.5 1.4 %collective-permute-start.8 = (bf16[136,128]{1,0:T(8,128)(2,1)S(1)}, bf16[136,128]{1,0:T(8,128)(2,1)S(1)}, u32[]{:S(2)}, u32[]{:S(2)}) collective-permute-start(bf16[136,128]{1,0:T(8,128)(2,1)S(1)} %multiply_convert_fusion.refs_0_), channel_id=1, source_target_pairs={{0,16},{8,24},{16,0},{24,8},{1,17},{9,25},{17,1},{25,9},{2,18},{10... | collective-permute-start | bytes 104456 | tf_op jit(solution)/shard_map/ppermute | solution.py:25
  48.9 1.1 %collective-permute-start.7 = (bf16[136,128]{1,0:T(8,128)(2,1)S(1)}, bf16[136,128]{1,0:T(8,128)(2,1)S(1)}, u32[]{:S(2)}, u32[]{:S(2)}) collective-permute-start(bf16[136,128]{1,0:T(8,128)(2,1)S(1)} %multiply_convert_fusion.refs_0_), channel_id=1, source_target_pairs={{0,8},{8,0},{16,24},{24,16},{1,9},{9,1},{17,25},{25,17},{2,10},{10... | collective-permute-start | bytes 104456 | tf_op jit(solution)/shard_map/ppermute | solution.py:25
  50.0 1.4 %collective-permute-done.9.refs_3_ = bf16[136,128]{1,0:T(8,128)(2,1)S(1)} collective-permute-done((bf16[136,128]{1,0:T(8,128)(2,1)S(1)}, bf16[136,128]{1,0:T(8,128)(2,1)S(1)}, u32[]{:S(2)}, u32[]{:S(2)}) %collective-permute-start.9) | collective-permute-done | bytes 34848 | tf_op jit(solution)/shard_map/ppermute | solution.py:25
  51.4 0.3 collective-permute-done.8.refs_2_
  51.7 0.2 collective-permute-start.12
  51.9 1.0 %collective-permute-done.7.refs_1_ = bf16[136,128]{1,0:T(8,128)(2,1)S(1)} collective-permute-done((bf16[136,128]{1,0:T(8,128)(2,1)S(1)}, bf16[136,128]{1,0:T(8,128)(2,1)S(1)}, u32[]{:S(2)}, u32[]{:S(2)}) %collective-permute-start.7) | collective-permute-done | bytes 34848 | tf_op jit(solution)/shard_map/ppermute | solution.py:25
  52.9 0.0 collective-permute-start.11
  52.9 0.0 collective-permute-done.10.refs_4_
  52.9 0.0 collective-permute-done.13.refs_7_
  52.9 0.0 collective-permute-done.12.refs_6_
  52.9 1.2 %collective-permute-done.11.refs_5_ = bf16[136,128]{1,0:T(8,128)(2,1)S(1)} collective-permute-done((bf16[136,128]{1,0:T(8,128)(2,1)S(1)}, bf16[136,128]{1,0:T(8,128)(2,1)S(1)}, u32[]{:S(2)}, u32[]{:S(2)}) %collective-permute-start.11) | collective-permute-done | bytes 34848 | tf_op jit(solution)/shard_map/ppermute | solution.py:25
  54.1 1.3 %shard_map.19 = bf16[256,1536]{1,0:T(8,128)(2,1)S(1)} custom-call(bf16[256,1536]{1,0:T(8,128)(2,1)S(1)} %bitcast.15, bf16[256,1536]{1,0:T(8,128)(2,1)S(1)} %collective-permute-done.y_ref, bf16[136,128]{1,0:T(8,128)(2,1)S(1)} %multiply_convert_fusion.refs_0_, bf16[136,128]{1,0:T(8,128)(2,1)S(1)} %collective-permute-done.7.refs_1_, ...), custom_call_target="tpu_custom_call" | custom-call | tf_op jit(solution)/shard_map/pallas_call | solution.py:196
  55.4 23.4 %all_to_all.11 = bf16[16,16,1536]{2,1,0:T(8,128)(2,1)S(1)} all-to-all(bf16[16,16,1536]{2,1,0:T(8,128)(2,1)S(1)} %bitcast.16), channel_id=1, replica_groups={{20,28,24,2,18,0,6,16,4,22,14,8,26,12,30,10},{21,29,25,3,19,1,7,17,5,23..., dimensions={0} | all-to-all | bytes 1572864 | tf_op jit(solution)/shard_map/all_to_all | solution.py:197
  78.8 0.9 %copy.5 = bf16[16,2,8,1536]{3,2,0,1:T(8,128)(2,1)} copy(bf16[16,2,8,1536]{3,2,1,0:T(8,128)(2,1)S(1)} %bitcast.17) | data formatting | bytes 1572864 | tf_op jit(solution)/shard_map/reshape | solution.py:198
  (5 shorter events, 0.1 us)
Async XLA Ops:
  27.4 2.3 %collective-permute-start = (bf16[256,1536]{1,0:T(8,128)(2,1)S(1)}, bf16[256,1536]{1,0:T(8,128)(2,1)S(1)}, u32[]{:S(2)}, u32[]{:S(2)}) collective-permute-start(bf16[256,1536]{1,0:T(8,128)(2,1)S(1)} %bitcast.12), channel_id=1, source_target_pairs={{0,1},{1,0},{2,3},{3,2},{4,5},{5,4},{6,7},{7,6},{8,9},{9,8},{10,11... | collective-permute-start | bytes 2359304 | tf_op jit(solution)/shard_map/ppermute | solution.py:25
  30.1 4.4 %collective-permute-start.1 = (f32[136,128]{1,0:T(8,128)S(1)}, f32[136,128]{1,0:T(8,128)S(1)}, u32[]{:S(2)}, u32[]{:S(2)}) collective-permute-start(f32[136,128]{1,0:T(8,128)S(1)} %get-tuple-element.10), channel_id=1, source_target_pairs={{0,8},{8,0},{16,24},{24,16},{1,9},{9,1},{17,25},{25,17},{2,10},{10... | collective-permute-start | bytes 208904 | tf_op jit(solution)/shard_map/ppermute | solution.py:25
  31.1 4.3 %collective-permute-start.2 = (f32[136,128]{1,0:T(8,128)S(1)}, f32[136,128]{1,0:T(8,128)S(1)}, u32[]{:S(2)}, u32[]{:S(2)}) collective-permute-start(f32[136,128]{1,0:T(8,128)S(1)} %get-tuple-element.11), channel_id=1, source_target_pairs={{0,16},{8,24},{16,0},{24,8},{1,17},{9,25},{17,1},{25,9},{2,18},{10... | collective-permute-start | bytes 208904 | tf_op jit(solution)/shard_map/ppermute | solution.py:25
  32.8 5.2 %collective-permute-start.3 = (f32[136,128]{1,0:T(8,128)S(1)}, f32[136,128]{1,0:T(8,128)S(1)}, u32[]{:S(2)}, u32[]{:S(2)}) collective-permute-start(f32[136,128]{1,0:T(8,128)S(1)} %get-tuple-element.12), channel_id=1, source_target_pairs={{0,24},{8,16},{16,8},{24,0},{1,25},{9,17},{17,9},{25,1},{2,26},{10... | collective-permute-start | bytes 208904 | tf_op jit(solution)/shard_map/ppermute | solution.py:25
  38.0 6.6 %collective-permute-start.6 = (f32[136,128]{1,0:T(8,128)S(1)}, f32[136,128]{1,0:T(8,128)S(1)}, u32[]{:S(2)}, u32[]{:S(2)}) collective-permute-start(f32[136,128]{1,0:T(8,128)S(1)} %add_add_fusion), channel_id=1, source_target_pairs={{0,6},{1,7},{2,4},{3,5},{4,2},{5,3},{6,0},{7,1},{8,14},{9,15},{10,... | collective-permute-start | bytes 208904 | tf_op jit(solution)/shard_map/ppermute | solution.py:25
  40.9 5.5 %collective-permute-start.5 = (f32[136,128]{1,0:T(8,128)S(1)}, f32[136,128]{1,0:T(8,128)S(1)}, u32[]{:S(2)}, u32[]{:S(2)}) collective-permute-start(f32[136,128]{1,0:T(8,128)S(1)} %add_add_fusion), channel_id=1, source_target_pairs={{0,4},{1,5},{2,6},{3,7},{4,0},{5,1},{6,2},{7,3},{8,12},{9,13},{10,... | collective-permute-start | bytes 208904 | tf_op jit(solution)/shard_map/ppermute | solution.py:25
  40.9 5.5 %collective-permute-start.4 = (f32[136,128]{1,0:T(8,128)S(1)}, f32[136,128]{1,0:T(8,128)S(1)}, u32[]{:S(2)}, u32[]{:S(2)}) collective-permute-start(f32[136,128]{1,0:T(8,128)S(1)} %add_add_fusion), channel_id=1, source_target_pairs={{0,2},{1,3},{2,0},{3,1},{4,6},{5,7},{6,4},{7,5},{8,10},{9,11},{10,... | collective-permute-start | bytes 208904 | tf_op jit(solution)/shard_map/ppermute | solution.py:25
  46.4 4.9 %collective-permute-start.9 = (bf16[136,128]{1,0:T(8,128)(2,1)S(1)}, bf16[136,128]{1,0:T(8,128)(2,1)S(1)}, u32[]{:S(2)}, u32[]{:S(2)}) collective-permute-start(bf16[136,128]{1,0:T(8,128)(2,1)S(1)} %multiply_convert_fusion.refs_0_), channel_id=1, source_target_pairs={{0,24},{8,16},{16,8},{24,0},{1,25},{9,17},{17,9},{25,1},{2,26},{10... | collective-permute-start | bytes 104456 | tf_op jit(solution)/shard_map/ppermute | solution.py:25
  47.5 4.2 %collective-permute-start.8 = (bf16[136,128]{1,0:T(8,128)(2,1)S(1)}, bf16[136,128]{1,0:T(8,128)(2,1)S(1)}, u32[]{:S(2)}, u32[]{:S(2)}) collective-permute-start(bf16[136,128]{1,0:T(8,128)(2,1)S(1)} %multiply_convert_fusion.refs_0_), channel_id=1, source_target_pairs={{0,16},{8,24},{16,0},{24,8},{1,17},{9,25},{17,1},{25,9},{2,18},{10... | collective-permute-start | bytes 104456 | tf_op jit(solution)/shard_map/ppermute | solution.py:25
  48.9 3.9 %collective-permute-start.7 = (bf16[136,128]{1,0:T(8,128)(2,1)S(1)}, bf16[136,128]{1,0:T(8,128)(2,1)S(1)}, u32[]{:S(2)}, u32[]{:S(2)}) collective-permute-start(bf16[136,128]{1,0:T(8,128)(2,1)S(1)} %multiply_convert_fusion.refs_0_), channel_id=1, source_target_pairs={{0,8},{8,0},{16,24},{24,16},{1,9},{9,1},{17,25},{25,17},{2,10},{10... | collective-permute-start | bytes 104456 | tf_op jit(solution)/shard_map/ppermute | solution.py:25
  50.0 2.9 %collective-permute-start.10 = (bf16[136,128]{1,0:T(8,128)(2,1)S(1)}, bf16[136,128]{1,0:T(8,128)(2,1)S(1)}, u32[]{:S(2)}, u32[]{:S(2)}) collective-permute-start(bf16[136,128]{1,0:T(8,128)(2,1)S(1)} %multiply_convert_fusion.refs_0_), channel_id=1, source_target_pairs={{0,1},{1,0},{2,3},{3,2},{4,5},{5,4},{6,7},{7,6},{8,9},{9,8},{10,11... | collective-permute-start | bytes 104456 | tf_op jit(solution)/shard_map/ppermute | solution.py:25
  51.4 1.5 %collective-permute-start.13 = (bf16[136,128]{1,0:T(8,128)(2,1)S(1)}, bf16[136,128]{1,0:T(8,128)(2,1)S(1)}, u32[]{:S(2)}, u32[]{:S(2)}) collective-permute-start(bf16[136,128]{1,0:T(8,128)(2,1)S(1)} %collective-permute-done.9.refs_3_), channel_id=1, source_target_pairs={{0,1},{1,0},{2,3},{3,2},{4,5},{5,4},{6,7},{7,6},{8,9},{9,8},{10,11... | collective-permute-start | bytes 104456 | tf_op jit(solution)/shard_map/ppermute | solution.py:25
  51.7 1.2 %collective-permute-start.12 = (bf16[136,128]{1,0:T(8,128)(2,1)S(1)}, bf16[136,128]{1,0:T(8,128)(2,1)S(1)}, u32[]{:S(2)}, u32[]{:S(2)}) collective-permute-start(bf16[136,128]{1,0:T(8,128)(2,1)S(1)} %collective-permute-done.8.refs_2_), channel_id=1, source_target_pairs={{0,1},{1,0},{2,3},{3,2},{4,5},{5,4},{6,7},{7,6},{8,9},{9,8},{10,11... | collective-permute-start | bytes 104456 | tf_op jit(solution)/shard_map/ppermute | solution.py:25
  52.9 1.2 %collective-permute-start.11 = (bf16[136,128]{1,0:T(8,128)(2,1)S(1)}, bf16[136,128]{1,0:T(8,128)(2,1)S(1)}, u32[]{:S(2)}, u32[]{:S(2)}) collective-permute-start(bf16[136,128]{1,0:T(8,128)(2,1)S(1)} %collective-permute-done.7.refs_1_), channel_id=1, source_target_pairs={{0,1},{1,0},{2,3},{3,2},{4,5},{5,4},{6,7},{7,6},{8,9},{9,8},{10,11... | collective-permute-start | bytes 104456 | tf_op jit(solution)/shard_map/ppermute | solution.py:25

commit v9 on v8

--- a/solution.py
+++ b/solution.py
@@ -105,49 +105,80 @@
     )
 
 
+def unstack(piece_refs, packed, bands):
+    whole, tail, piece = heights(bands)
+    band = lax.axis_index("band")
+    for m in range(bands):
+        packed[pl.ds(pl.multiple_of((band ^ m) * piece, 8), piece), :] = piece_refs[m][...].astype(jnp.float32)
+    row, column = squares()
+    both, beside = packed[0:BLOCK, :], packed[BLOCK:2 * BLOCK, :]
+    line = packed[whole:whole + 8, :][0:1, :]
+    turned = both.T
+    first = jnp.where(row <= column, both, turned)
+    second = jnp.where(row == column, line, jnp.where(row > column, both, turned))
+    grid = ((first, beside), (beside.T, second))
+    return grid, [packed[(2 + j) * BLOCK:(3 + j) * BLOCK, :] for j in range(2)]
+
+
+def block_at(row, column):
+    return slice(row * BLOCK, (row + 1) * BLOCK), slice(column * BLOCK, (column + 1) * BLOCK)
+
+
+def own_side(bands):
+    whole, tail, _ = heights(bands)
+
+    def body(*refs):
+        piece_refs, square_ref, cross_ref, turned_ref, packed = refs[:-4], refs[-4], refs[-3], refs[-2], refs[-1]
+        grid, cross = unstack(piece_refs, packed, bands)
+        for i in range(2):
+            for j in range(2):
+                square_ref[block_at(i, j)] = grid[i][j].astype(jnp.bfloat16)
+            cross_ref[block_at(0, i)] = cross[i].astype(jnp.bfloat16)
+            turned_ref[block_at(i, 0)] = cross[i].T.astype(jnp.bfloat16)
+
+    return pl.pallas_call(
+        body,
+        out_shape=(
+            jax.ShapeDtypeStruct((2 * BLOCK, 2 * BLOCK), jnp.bfloat16),
+            jax.ShapeDtypeStruct((BLOCK, 2 * BLOCK), jnp.bfloat16),
+            jax.ShapeDtypeStruct((2 * BLOCK, BLOCK), jnp.bfloat16),
+        ),
+        scratch_shapes=[pltpu.VMEM((whole + tail, BLOCK), jnp.float32)],
+        compiler_params=VMEM_LIMIT,
+        cost_estimate=pl.CostEstimate(
+            flops=16 * BLOCK * BLOCK, bytes_accessed=32 * BLOCK * BLOCK, transcendentals=0
+        ),
+    )
+
+
 def correct(width, bands):
-    whole, tail, piece = heights(bands)
-    stacked = whole + tail
+    whole, tail, _ = heights(bands)
     rows = 2 * BLOCK
 
-    def body(x_ref, y_ref, *refs):
+    def body(x_ref, y_ref, square_ref, cross_ref, turned_ref, *refs):
         piece_refs, out_ref, packed, excess = refs[:-3], refs[-3], refs[-2], refs[-1]
-        band, core = lax.axis_index("band"), my_core()
-        for side in range(2):
-            for m in range(bands):
-                start = side * stacked + (band ^ m) * piece
-                held = piece_refs[side * bands + m][...].astype(jnp.float32)
-                packed[pl.ds(pl.multiple_of(start, 8), piece), :] = held
-
-        def put(row, column, block):
-            at = (slice(row * BLOCK, (row + 1) * BLOCK), slice(column * BLOCK, (column + 1) * BLOCK))
-            excess[at] = block.astype(jnp.bfloat16)
-
-        row, column = squares()
-        for side in range(2):
-            at = side * stacked
-            both, beside = packed[at:at + BLOCK, :], packed[at + BLOCK:at + 2 * BLOCK, :]
-            line = packed[at + whole:at + whole + 8, :][0:1, :]
-            turned = both.T
-            put(2 * side, 2 * side, jnp.where(row <= column, both, turned))
-            second = jnp.where(row > column, both, turned)
-            put(2 * side + 1, 2 * side + 1, jnp.where(row == column, line, second))
-            put(2 * side, 2 * side + 1, beside)
-            put(2 * side + 1, 2 * side, beside.T)
-        for part in range(2):
+        core = my_core()
+        excess[0:rows, 0:rows] = square_ref[...]
+        grid, cross = unstack(piece_refs, packed, bands)
+        for i in range(2):
             for j in range(2):
-                start = (part ^ core) * stacked + (2 + j) * BLOCK
-                block = packed[pl.ds(pl.multiple_of(start, 8), BLOCK), :]
-
-                @pl.when(core == 0)
-                def _():
-                    put(part, 2 + j, block)
-                    put(2 + j, part, block.T)
-
-                @pl.when(core == 1)
-                def _():
-                    put(2 + part, j, block)
-                    put(j, 2 + part, block.T)
+                excess[block_at(2 + i, 2 + j)] = grid[i][j].astype(jnp.bfloat16)
+        wide = jnp.concatenate(cross, axis=1).astype(jnp.bfloat16)
+        tall = jnp.concatenate([c.T for c in cross], axis=0).astype(jnp.bfloat16)
+
+        @pl.when(core == 0)
+        def _():
+            excess[0:BLOCK, rows:2 * rows] = cross_ref[...]
+            excess[BLOCK:rows, rows:2 * rows] = wide
+            excess[rows:2 * rows, 0:BLOCK] = turned_ref[...]
+            excess[rows:2 * rows, BLOCK:rows] = tall
+
+        @pl.when(core == 1)
+        def _():
+            excess[rows:rows + BLOCK, 0:rows] = wide
+            excess[rows + BLOCK:2 * rows, 0:rows] = cross_ref[...]
+            excess[0:rows, rows:rows + BLOCK] = tall
+            excess[0:rows, rows + BLOCK:2 * rows] = turned_ref[...]
 
         own = excess[0:rows, :]
         twice = jnp.dot(own, excess[...], preferred_element_type=jnp.float32)
@@ -165,7 +196,7 @@
         body,
         out_shape=jax.ShapeDtypeStruct((rows, width), jnp.bfloat16),
         scratch_shapes=[
-            pltpu.VMEM((2 * stacked, BLOCK), jnp.float32),
+            pltpu.VMEM((whole + tail, BLOCK), jnp.float32),
             pltpu.VMEM((2 * rows, 2 * rows), jnp.bfloat16),
         ],
         compiler_params=VMEM_LIMIT,
@@ -193,7 +224,7 @@
     excess = (heard[0] * (1.0 / NC)).astype(jnp.bfloat16)
     mine = [excess] + [swap(excess, "band", m) for m in range(1, bands)]
     other = [swap(e, "domain", 1) for e in mine]
-    out = correct(width, bands)(x, y, *mine, *other).reshape(chips, fdev, width)
+    out = correct(width, bands)(x, y, *own_side(bands)(*mine), *other).reshape(chips, fdev, width)
     back = lax.all_to_all(out, BOTH, split_axis=0, concat_axis=0, axis_index_groups=spread)
     return back.transpose(1, 0, 2).reshape(fdev, ncoef)
 

time: 79.9 us -> 79.6 us (level)
  no operation moved by 1% of the time
where the time goes in v9:
time: 79.6 us; the launch traced here: 79.3 us
  blocking collectives  49.5 us (62%)
  waiting for transfers between devices  13.9 us (17%)
  starting transfers between devices  11.7 us (15%)
  local copies, waits for them, and re-layouts  2.14 us (3%)
  Pallas kernels  1.93 us (2%)
    all_to_all x1, blocking collectives, full_rows(): lax.all_to_all(cut, BOTH, split_axis=0, concat_axis=0, axis_index_groups=...  26.2 us
    all_to_all x1, blocking collectives, full_rows(): lax.all_to_all(out, BOTH, split_axis=0, concat_axis=0, axis_index_groups=...  23.3 us
    ppermute x14, waiting for transfers between devices, swap(): return lax.ppermute(value, axis, [(i, i ^ mask) for i in range(count)])  13.9 us
    ppermute x14, starting transfers between devices, swap(): return lax.ppermute(value, axis, [(i, i ^ mask) for i in range(count)])  11.7 us
  transfers between devices with their start and end apart: 14, of which 10 were waited for; matrix products, arithmetic and copies ran while one was open for 0% of the time, Pallas kernels for 1%

profile of v9, /device:TPU:0, one launch (start us, length us, event | category | flops | bytes accessed | tf_op | source)
XLA Modules:
  0.0 79.3 jit_solution(5780107377430954088)
XLA Ops:
  0.0 1.2 %copy.7 = bf16[2,16,8,1536]{3,2,0,1:T(8,128)(2,1)S(1)} copy(bf16[2,16,8,1536]{3,2,1,0:T(8,128)(2,1)} %bitcast.19) | data formatting | bytes 1572864 | tf_op jit(solution)/shard_map/reshape | solution.py:213
  1.2 26.2 %all_to_all.10 = bf16[16,16,1536]{2,1,0:T(8,128)(2,1)S(1)} all-to-all(bf16[16,16,1536]{2,1,0:T(8,128)(2,1)S(1)} %bitcast.18), channel_id=1, replica_groups={{20,28,24,2,18,0,6,16,4,22,14,8,26,12,30,10},{21,29,25,3,19,1,7,17,5,23..., dimensions={0} | all-to-all | bytes 1572864 | tf_op jit(solution)/shard_map/all_to_all | solution.py:214
  27.4 0.0 collective-permute-start
  27.4 0.4 shard_map.17.own_ref
  27.8 1.9 %collective-permute-done.y_ref = bf16[256,1536]{1,0:T(8,128)(2,1)S(1)} collective-permute-done((bf16[256,1536]{1,0:T(8,128)(2,1)S(1)}, bf16[256,1536]{1,0:T(8,128)(2,1)S(1)}, u32[]{:S(2)}, u32[]{:S(2)}) %collective-permute-start) | collective-permute-done | bytes 786464 | tf_op jit(solution)/shard_map/ppermute | solution.py:25
  29.7 0.4 shard_map.18
  30.1 1.0 %collective-permute-start.1 = (f32[136,128]{1,0:T(8,128)S(1)}, f32[136,128]{1,0:T(8,128)S(1)}, u32[]{:S(2)}, u32[]{:S(2)}) collective-permute-start(f32[136,128]{1,0:T(8,128)S(1)} %get-tuple-element.13), channel_id=1, source_target_pairs={{0,8},{8,0},{16,24},{24,16},{1,9},{9,1},{17,25},{25,17},{2,10},{10... | collective-permute-start | bytes 208904 | tf_op jit(solution)/shard_map/ppermute | solution.py:25
  31.1 1.6 %collective-permute-start.2 = (f32[136,128]{1,0:T(8,128)S(1)}, f32[136,128]{1,0:T(8,128)S(1)}, u32[]{:S(2)}, u32[]{:S(2)}) collective-permute-start(f32[136,128]{1,0:T(8,128)S(1)} %get-tuple-element.14), channel_id=1, source_target_pairs={{0,16},{8,24},{16,0},{24,8},{1,17},{9,25},{17,1},{25,9},{2,18},{10... | collective-permute-start | bytes 208904 | tf_op jit(solution)/shard_map/ppermute | solution.py:25
  32.8 0.9 %collective-permute-start.3 = (f32[136,128]{1,0:T(8,128)S(1)}, f32[136,128]{1,0:T(8,128)S(1)}, u32[]{:S(2)}, u32[]{:S(2)}) collective-permute-start(f32[136,128]{1,0:T(8,128)S(1)} %get-tuple-element.15), channel_id=1, source_target_pairs={{0,24},{8,16},{16,8},{24,0},{1,25},{9,17},{17,9},{25,1},{2,26},{10... | collective-permute-start | bytes 208904 | tf_op jit(solution)/shard_map/ppermute | solution.py:25
  33.7 0.8 %collective-permute-done.1 = f32[136,128]{1,0:T(8,128)S(1)} collective-permute-done((f32[136,128]{1,0:T(8,128)S(1)}, f32[136,128]{1,0:T(8,128)S(1)}, u32[]{:S(2)}, u32[]{:S(2)}) %collective-permute-start.1) | collective-permute-done | bytes 69664 | tf_op jit(solution)/shard_map/ppermute | solution.py:25
  34.5 0.9 %collective-permute-done.2 = f32[136,128]{1,0:T(8,128)S(1)} collective-permute-done((f32[136,128]{1,0:T(8,128)S(1)}, f32[136,128]{1,0:T(8,128)S(1)}, u32[]{:S(2)}, u32[]{:S(2)}) %collective-permute-start.2) | collective-permute-done | bytes 69664 | tf_op jit(solution)/shard_map/ppermute | solution.py:25
  35.5 2.5 %collective-permute-done.3 = f32[136,128]{1,0:T(8,128)S(1)} collective-permute-done((f32[136,128]{1,0:T(8,128)S(1)}, f32[136,128]{1,0:T(8,128)S(1)}, u32[]{:S(2)}, u32[]{:S(2)}) %collective-permute-start.3) | collective-permute-done | bytes 69664 | tf_op jit(solution)/shard_map/ppermute | solution.py:25
  38.0 2.9 %collective-permute-start.6 = (f32[136,128]{1,0:T(8,128)S(1)}, f32[136,128]{1,0:T(8,128)S(1)}, u32[]{:S(2)}, u32[]{:S(2)}) collective-permute-start(f32[136,128]{1,0:T(8,128)S(1)} %add_add_fusion), channel_id=1, source_target_pairs={{0,6},{1,7},{2,4},{3,5},{4,2},{5,3},{6,0},{7,1},{8,14},{9,15},{10,... | collective-permute-start | bytes 208904 | tf_op jit(solution)/shard_map/ppermute | solution.py:25
  40.9 0.0 collective-permute-start.5
  40.9 1.6 %collective-permute-start.4 = (f32[136,128]{1,0:T(8,128)S(1)}, f32[136,128]{1,0:T(8,128)S(1)}, u32[]{:S(2)}, u32[]{:S(2)}) collective-permute-start(f32[136,128]{1,0:T(8,128)S(1)} %add_add_fusion), channel_id=1, source_target_pairs={{0,2},{1,3},{2,0},{3,1},{4,6},{5,7},{6,4},{7,5},{8,10},{9,11},{10,... | collective-permute-start | bytes 208904 | tf_op jit(solution)/shard_map/ppermute | solution.py:25
  42.4 2.2 %collective-permute-done.6 = f32[136,128]{1,0:T(8,128)S(1)} collective-permute-done((f32[136,128]{1,0:T(8,128)S(1)}, f32[136,128]{1,0:T(8,128)S(1)}, u32[]{:S(2)}, u32[]{:S(2)}) %collective-permute-start.6) | collective-permute-done | bytes 69664 | tf_op jit(solution)/shard_map/ppermute | solution.py:25
  44.6 1.8 %collective-permute-done.5 = f32[136,128]{1,0:T(8,128)S(1)} collective-permute-done((f32[136,128]{1,0:T(8,128)S(1)}, f32[136,128]{1,0:T(8,128)S(1)}, u32[]{:S(2)}, u32[]{:S(2)}) %collective-permute-start.5) | collective-permute-done | bytes 69664 | tf_op jit(solution)/shard_map/ppermute | solution.py:25
  46.4 1.1 %collective-permute-start.9 = (bf16[136,128]{1,0:T(8,128)(2,1)S(1)}, bf16[136,128]{1,0:T(8,128)(2,1)S(1)}, u32[]{:S(2)}, u32[]{:S(2)}) collective-permute-start(bf16[136,128]{1,0:T(8,128)(2,1)S(1)} %multiply_convert_fusion.refs_0_), channel_id=1, source_target_pairs={{0,24},{8,16},{16,8},{24,0},{1,25},{9,17},{17,9},{25,1},{2,26},{10... | collective-permute-start | bytes 104456 | tf_op jit(solution)/shard_map/ppermute | solution.py:25
  47.5 1.4 %collective-permute-start.8 = (bf16[136,128]{1,0:T(8,128)(2,1)S(1)}, bf16[136,128]{1,0:T(8,128)(2,1)S(1)}, u32[]{:S(2)}, u32[]{:S(2)}) collective-permute-start(bf16[136,128]{1,0:T(8,128)(2,1)S(1)} %multiply_convert_fusion.refs_0_), channel_id=1, source_target_pairs={{0,16},{8,24},{16,0},{24,8},{1,17},{9,25},{17,1},{25,9},{2,18},{10... | collective-permute-start | bytes 104456 | tf_op jit(solution)/shard_map/ppermute | solution.py:25
  48.9 1.1 %collective-permute-start.7 = (bf16[136,128]{1,0:T(8,128)(2,1)S(1)}, bf16[136,128]{1,0:T(8,128)(2,1)S(1)}, u32[]{:S(2)}, u32[]{:S(2)}) collective-permute-start(bf16[136,128]{1,0:T(8,128)(2,1)S(1)} %multiply_convert_fusion.refs_0_), channel_id=1, source_target_pairs={{0,8},{8,0},{16,24},{24,16},{1,9},{9,1},{17,25},{25,17},{2,10},{10... | collective-permute-start | bytes 104456 | tf_op jit(solution)/shard_map/ppermute | solution.py:25
  50.0 0.0 collective-permute-start.10
  50.0 1.4 %collective-permute-done.9.refs_3_ = bf16[136,128]{1,0:T(8,128)(2,1)S(1)} collective-permute-done((bf16[136,128]{1,0:T(8,128)(2,1)S(1)}, bf16[136,128]{1,0:T(8,128)(2,1)S(1)}, u32[]{:S(2)}, u32[]{:S(2)}) %collective-permute-start.9) | collective-permute-done | bytes 34848 | tf_op jit(solution)/shard_map/ppermute | solution.py:25
  51.4 0.0 collective-permute-start.13
  51.4 0.3 collective-permute-done.8.refs_2_
  51.7 0.2 collective-permute-start.12
  51.9 1.0 %collective-permute-done.7.refs_1_ = bf16[136,128]{1,0:T(8,128)(2,1)S(1)} collective-permute-done((bf16[136,128]{1,0:T(8,128)(2,1)S(1)}, bf16[136,128]{1,0:T(8,128)(2,1)S(1)}, u32[]{:S(2)}, u32[]{:S(2)}) %collective-permute-start.7) | collective-permute-done | bytes 34848 | tf_op jit(solution)/shard_map/ppermute | solution.py:25
  52.9 0.0 collective-permute-start.11
  52.9 0.1 shard_map.19
  53.0 1.0 %collective-permute-done.11.refs_1_ = bf16[136,128]{1,0:T(8,128)(2,1)S(1)} collective-permute-done((bf16[136,128]{1,0:T(8,128)(2,1)S(1)}, bf16[136,128]{1,0:T(8,128)(2,1)S(1)}, u32[]{:S(2)}, u32[]{:S(2)}) %collective-permute-start.11) | collective-permute-done | bytes 34848 | tf_op jit(solution)/shard_map/ppermute | solution.py:25
  54.1 1.0 %shard_map.20 = bf16[256,1536]{1,0:T(8,128)(2,1)S(1)} custom-call(bf16[256,1536]{1,0:T(8,128)(2,1)S(1)} %bitcast.15, bf16[256,1536]{1,0:T(8,128)(2,1)S(1)} %collective-permute-done.y_ref, bf16[256,256]{1,0:T(8,128)(2,1)S(1)} %get-tuple-element.16.square_ref, bf16[128,256]{1,0:T(8,128)(2,1)S(1)} %get-tuple-element.17.cross_ref, ...), custom_call_target="tpu_custom_call" | custom-call | tf_op jit(solution)/shard_map/pallas_call | solution.py:227
  55.1 23.3 %all_to_all.11 = bf16[16,16,1536]{2,1,0:T(8,128)(2,1)S(1)} all-to-all(bf16[16,16,1536]{2,1,0:T(8,128)(2,1)S(1)} %bitcast.16), channel_id=1, replica_groups={{20,28,24,2,18,0,6,16,4,22,14,8,26,12,30,10},{21,29,25,3,19,1,7,17,5,23..., dimensions={0} | all-to-all | bytes 1572864 | tf_op jit(solution)/shard_map/all_to_all | solution.py:228
  78.4 0.9 %copy.5 = bf16[16,2,8,1536]{3,2,0,1:T(8,128)(2,1)} copy(bf16[16,2,8,1536]{3,2,1,0:T(8,128)(2,1)S(1)} %bitcast.17) | data formatting | bytes 1572864 | tf_op jit(solution)/shard_map/reshape | solution.py:229
  (6 shorter events, 0.1 us)
Async XLA Ops:
  27.4 2.3 %collective-permute-start = (bf16[256,1536]{1,0:T(8,128)(2,1)S(1)}, bf16[256,1536]{1,0:T(8,128)(2,1)S(1)}, u32[]{:S(2)}, u32[]{:S(2)}) collective-permute-start(bf16[256,1536]{1,0:T(8,128)(2,1)S(1)} %bitcast.12), channel_id=1, source_target_pairs={{0,1},{1,0},{2,3},{3,2},{4,5},{5,4},{6,7},{7,6},{8,9},{9,8},{10,11... | collective-permute-start | bytes 2359304 | tf_op jit(solution)/shard_map/ppermute | solution.py:25
  30.1 4.4 %collective-permute-start.1 = (f32[136,128]{1,0:T(8,128)S(1)}, f32[136,128]{1,0:T(8,128)S(1)}, u32[]{:S(2)}, u32[]{:S(2)}) collective-permute-start(f32[136,128]{1,0:T(8,128)S(1)} %get-tuple-element.13), channel_id=1, source_target_pairs={{0,8},{8,0},{16,24},{24,16},{1,9},{9,1},{17,25},{25,17},{2,10},{10... | collective-permute-start | bytes 208904 | tf_op jit(solution)/shard_map/ppermute | solution.py:25
  31.1 4.3 %collective-permute-start.2 = (f32[136,128]{1,0:T(8,128)S(1)}, f32[136,128]{1,0:T(8,128)S(1)}, u32[]{:S(2)}, u32[]{:S(2)}) collective-permute-start(f32[136,128]{1,0:T(8,128)S(1)} %get-tuple-element.14), channel_id=1, source_target_pairs={{0,16},{8,24},{16,0},{24,8},{1,17},{9,25},{17,1},{25,9},{2,18},{10... | collective-permute-start | bytes 208904 | tf_op jit(solution)/shard_map/ppermute | solution.py:25
  32.8 5.2 %collective-permute-start.3 = (f32[136,128]{1,0:T(8,128)S(1)}, f32[136,128]{1,0:T(8,128)S(1)}, u32[]{:S(2)}, u32[]{:S(2)}) collective-permute-start(f32[136,128]{1,0:T(8,128)S(1)} %get-tuple-element.15), channel_id=1, source_target_pairs={{0,24},{8,16},{16,8},{24,0},{1,25},{9,17},{17,9},{25,1},{2,26},{10... | collective-permute-start | bytes 208904 | tf_op jit(solution)/shard_map/ppermute | solution.py:25
  38.0 6.6 %collective-permute-start.6 = (f32[136,128]{1,0:T(8,128)S(1)}, f32[136,128]{1,0:T(8,128)S(1)}, u32[]{:S(2)}, u32[]{:S(2)}) collective-permute-start(f32[136,128]{1,0:T(8,128)S(1)} %add_add_fusion), channel_id=1, source_target_pairs={{0,6},{1,7},{2,4},{3,5},{4,2},{5,3},{6,0},{7,1},{8,14},{9,15},{10,... | collective-permute-start | bytes 208904 | tf_op jit(solution)/shard_map/ppermute | solution.py:25
  40.9 5.5 %collective-permute-start.5 = (f32[136,128]{1,0:T(8,128)S(1)}, f32[136,128]{1,0:T(8,128)S(1)}, u32[]{:S(2)}, u32[]{:S(2)}) collective-permute-start(f32[136,128]{1,0:T(8,128)S(1)} %add_add_fusion), channel_id=1, source_target_pairs={{0,4},{1,5},{2,6},{3,7},{4,0},{5,1},{6,2},{7,3},{8,12},{9,13},{10,... | collective-permute-start | bytes 208904 | tf_op jit(solution)/shard_map/ppermute | solution.py:25
  40.9 5.5 %collective-permute-start.4 = (f32[136,128]{1,0:T(8,128)S(1)}, f32[136,128]{1,0:T(8,128)S(1)}, u32[]{:S(2)}, u32[]{:S(2)}) collective-permute-start(f32[136,128]{1,0:T(8,128)S(1)} %add_add_fusion), channel_id=1, source_target_pairs={{0,2},{1,3},{2,0},{3,1},{4,6},{5,7},{6,4},{7,5},{8,10},{9,11},{10,... | collective-permute-start | bytes 208904 | tf_op jit(solution)/shard_map/ppermute | solution.py:25
  46.4 4.9 %collective-permute-start.9 = (bf16[136,128]{1,0:T(8,128)(2,1)S(1)}, bf16[136,128]{1,0:T(8,128)(2,1)S(1)}, u32[]{:S(2)}, u32[]{:S(2)}) collective-permute-start(bf16[136,128]{1,0:T(8,128)(2,1)S(1)} %multiply_convert_fusion.refs_0_), channel_id=1, source_target_pairs={{0,24},{8,16},{16,8},{24,0},{1,25},{9,17},{17,9},{25,1},{2,26},{10... | collective-permute-start | bytes 104456 | tf_op jit(solution)/shard_map/ppermute | solution.py:25
  47.5 4.2 %collective-permute-start.8 = (bf16[136,128]{1,0:T(8,128)(2,1)S(1)}, bf16[136,128]{1,0:T(8,128)(2,1)S(1)}, u32[]{:S(2)}, u32[]{:S(2)}) collective-permute-start(bf16[136,128]{1,0:T(8,128)(2,1)S(1)} %multiply_convert_fusion.refs_0_), channel_id=1, source_target_pairs={{0,16},{8,24},{16,0},{24,8},{1,17},{9,25},{17,1},{25,9},{2,18},{10... | collective-permute-start | bytes 104456 | tf_op jit(solution)/shard_map/ppermute | solution.py:25
  48.9 3.9 %collective-permute-start.7 = (bf16[136,128]{1,0:T(8,128)(2,1)S(1)}, bf16[136,128]{1,0:T(8,128)(2,1)S(1)}, u32[]{:S(2)}, u32[]{:S(2)}) collective-permute-start(bf16[136,128]{1,0:T(8,128)(2,1)S(1)} %multiply_convert_fusion.refs_0_), channel_id=1, source_target_pairs={{0,8},{8,0},{16,24},{24,16},{1,9},{9,1},{17,25},{25,17},{2,10},{10... | collective-permute-start | bytes 104456 | tf_op jit(solution)/shard_map/ppermute | solution.py:25
  50.0 3.0 %collective-permute-start.10 = (bf16[136,128]{1,0:T(8,128)(2,1)S(1)}, bf16[136,128]{1,0:T(8,128)(2,1)S(1)}, u32[]{:S(2)}, u32[]{:S(2)}) collective-permute-start(bf16[136,128]{1,0:T(8,128)(2,1)S(1)} %multiply_convert_fusion.refs_0_), channel_id=1, source_target_pairs={{0,1},{1,0},{2,3},{3,2},{4,5},{5,4},{6,7},{7,6},{8,9},{9,8},{10,11... | collective-permute-start | bytes 104456 | tf_op jit(solution)/shard_map/ppermute | solution.py:25
  51.4 1.7 %collective-permute-start.13 = (bf16[136,128]{1,0:T(8,128)(2,1)S(1)}, bf16[136,128]{1,0:T(8,128)(2,1)S(1)}, u32[]{:S(2)}, u32[]{:S(2)}) collective-permute-start(bf16[136,128]{1,0:T(8,128)(2,1)S(1)} %collective-permute-done.9.refs_3_), channel_id=1, source_target_pairs={{0,1},{1,0},{2,3},{3,2},{4,5},{5,4},{6,7},{7,6},{8,9},{9,8},{10,11... | collective-permute-start | bytes 104456 | tf_op jit(solution)/shard_map/ppermute | solution.py:25
  51.7 1.3 %collective-permute-start.12 = (bf16[136,128]{1,0:T(8,128)(2,1)S(1)}, bf16[136,128]{1,0:T(8,128)(2,1)S(1)}, u32[]{:S(2)}, u32[]{:S(2)}) collective-permute-start(bf16[136,128]{1,0:T(8,128)(2,1)S(1)} %collective-permute-done.8.refs_2_), channel_id=1, source_target_pairs={{0,1},{1,0},{2,3},{3,2},{4,5},{5,4},{6,7},{7,6},{8,9},{9,8},{10,11... | collective-permute-start | bytes 104456 | tf_op jit(solution)/shard_map/ppermute | solution.py:25
  52.9 1.2 %collective-permute-start.11 = (bf16[136,128]{1,0:T(8,128)(2,1)S(1)}, bf16[136,128]{1,0:T(8,128)(2,1)S(1)}, u32[]{:S(2)}, u32[]{:S(2)}) collective-permute-start(bf16[136,128]{1,0:T(8,128)(2,1)S(1)} %collective-permute-done.7.refs_1_), channel_id=1, source_target_pairs={{0,1},{1,0},{2,3},{3,2},{4,5},{5,4},{6,7},{7,6},{8,9},{9,8},{10,11... | collective-permute-start | bytes 104456 | tf_op jit(solution)/shard_map/ppermute | solution.py:25

commit v10 on v9

--- a/solution.py
+++ b/solution.py
@@ -10,7 +10,7 @@
 NC = 24576
 BLOCK = 128
 BOTH = ("band", "domain")
-MEASURED = (10, 14, 12, 1, 9, 0, 3, 8, 2, 11, 7, 4, 13, 6, 15, 5)
+MEASURED = (14, 10, 8, 5, 13, 4, 7, 12, 6, 15, 3, 0, 9, 2, 11, 1)
 
 
 VMEM_LIMIT = pltpu.CompilerParams(vmem_limit_bytes=16 * 1024 * 1024)

time: 79.6 us -> 79.2 us (level)
  no operation moved by 1% of the time
where the time goes in v10:
time: 79.2 us; the launch traced here: 79 us
  blocking collectives  49.1 us (62%)
  waiting for transfers between devices  13.9 us (18%)
  starting transfers between devices  11.7 us (15%)
  local copies, waits for them, and re-layouts  2.14 us (3%)
  Pallas kernels  1.96 us (2%)
    all_to_all x1, blocking collectives, full_rows(): lax.all_to_all(cut, BOTH, split_axis=0, concat_axis=0, axis_index_groups=...  25.8 us
    all_to_all x1, blocking collectives, full_rows(): lax.all_to_all(out, BOTH, split_axis=0, concat_axis=0, axis_index_groups=...  23.3 us
    ppermute x14, waiting for transfers between devices, swap(): return lax.ppermute(value, axis, [(i, i ^ mask) for i in range(count)])  13.9 us
    ppermute x14, starting transfers between devices, swap(): return lax.ppermute(value, axis, [(i, i ^ mask) for i in range(count)])  11.7 us
  transfers between devices with their start and end apart: 14, of which 10 were waited for; matrix products, arithmetic and copies ran while one was open for 0% of the time, Pallas kernels for 1%

profile of v10, /device:TPU:0, one launch (start us, length us, event | category | flops | bytes accessed | tf_op | source)
XLA Modules:
  0.0 79.0 jit_solution(2341537257708057442)
XLA Ops:
  0.0 1.2 %copy.7 = bf16[2,16,8,1536]{3,2,0,1:T(8,128)(2,1)S(1)} copy(bf16[2,16,8,1536]{3,2,1,0:T(8,128)(2,1)} %bitcast.19) | data formatting | bytes 1572864 | tf_op jit(solution)/shard_map/reshape | solution.py:213
  1.2 25.8 %all_to_all.10 = bf16[16,16,1536]{2,1,0:T(8,128)(2,1)S(1)} all-to-all(bf16[16,16,1536]{2,1,0:T(8,128)(2,1)S(1)} %bitcast.18), channel_id=1, replica_groups={{28,20,16,10,26,8,14,24,12,30,6,0,18,4,22,2},{29,21,17,11,27,9,15,25,13..., dimensions={0} | all-to-all | bytes 1572864 | tf_op jit(solution)/shard_map/all_to_all | solution.py:214
  27.1 0.0 collective-permute-start
  27.1 0.4 shard_map.17.own_ref
  27.5 1.9 %collective-permute-done.y_ref = bf16[256,1536]{1,0:T(8,128)(2,1)S(1)} collective-permute-done((bf16[256,1536]{1,0:T(8,128)(2,1)S(1)}, bf16[256,1536]{1,0:T(8,128)(2,1)S(1)}, u32[]{:S(2)}, u32[]{:S(2)}) %collective-permute-start) | collective-permute-done | bytes 786464 | tf_op jit(solution)/shard_map/ppermute | solution.py:25
  29.3 0.4 shard_map.18
  29.8 1.1 %collective-permute-start.1 = (f32[136,128]{1,0:T(8,128)S(1)}, f32[136,128]{1,0:T(8,128)S(1)}, u32[]{:S(2)}, u32[]{:S(2)}) collective-permute-start(f32[136,128]{1,0:T(8,128)S(1)} %get-tuple-element.13), channel_id=1, source_target_pairs={{0,8},{8,0},{16,24},{24,16},{1,9},{9,1},{17,25},{25,17},{2,10},{10... | collective-permute-start | bytes 208904 | tf_op jit(solution)/shard_map/ppermute | solution.py:25
  30.9 1.7 %collective-permute-start.2 = (f32[136,128]{1,0:T(8,128)S(1)}, f32[136,128]{1,0:T(8,128)S(1)}, u32[]{:S(2)}, u32[]{:S(2)}) collective-permute-start(f32[136,128]{1,0:T(8,128)S(1)} %get-tuple-element.14), channel_id=1, source_target_pairs={{0,16},{8,24},{16,0},{24,8},{1,17},{9,25},{17,1},{25,9},{2,18},{10... | collective-permute-start | bytes 208904 | tf_op jit(solution)/shard_map/ppermute | solution.py:25
  32.6 0.7 collective-permute-start.3
  33.3 0.8 %collective-permute-done.1 = f32[136,128]{1,0:T(8,128)S(1)} collective-permute-done((f32[136,128]{1,0:T(8,128)S(1)}, f32[136,128]{1,0:T(8,128)S(1)}, u32[]{:S(2)}, u32[]{:S(2)}) %collective-permute-start.1) | collective-permute-done | bytes 69664 | tf_op jit(solution)/shard_map/ppermute | solution.py:25
  34.1 1.1 %collective-permute-done.2 = f32[136,128]{1,0:T(8,128)S(1)} collective-permute-done((f32[136,128]{1,0:T(8,128)S(1)}, f32[136,128]{1,0:T(8,128)S(1)}, u32[]{:S(2)}, u32[]{:S(2)}) %collective-permute-start.2) | collective-permute-done | bytes 69664 | tf_op jit(solution)/shard_map/ppermute | solution.py:25
  35.2 2.6 %collective-permute-done.3 = f32[136,128]{1,0:T(8,128)S(1)} collective-permute-done((f32[136,128]{1,0:T(8,128)S(1)}, f32[136,128]{1,0:T(8,128)S(1)}, u32[]{:S(2)}, u32[]{:S(2)}) %collective-permute-start.3) | collective-permute-done | bytes 69664 | tf_op jit(solution)/shard_map/ppermute | solution.py:25
  37.8 2.1 %collective-permute-start.6 = (f32[136,128]{1,0:T(8,128)S(1)}, f32[136,128]{1,0:T(8,128)S(1)}, u32[]{:S(2)}, u32[]{:S(2)}) collective-permute-start(f32[136,128]{1,0:T(8,128)S(1)} %add_add_fusion), channel_id=1, source_target_pairs={{0,6},{1,7},{2,4},{3,5},{4,2},{5,3},{6,0},{7,1},{8,14},{9,15},{10,... | collective-permute-start | bytes 208904 | tf_op jit(solution)/shard_map/ppermute | solution.py:25
  39.9 0.4 collective-permute-start.5
  40.4 1.9 %collective-permute-start.4 = (f32[136,128]{1,0:T(8,128)S(1)}, f32[136,128]{1,0:T(8,128)S(1)}, u32[]{:S(2)}, u32[]{:S(2)}) collective-permute-start(f32[136,128]{1,0:T(8,128)S(1)} %add_add_fusion), channel_id=1, source_target_pairs={{0,2},{1,3},{2,0},{3,1},{4,6},{5,7},{6,4},{7,5},{8,10},{9,11},{10,... | collective-permute-start | bytes 208904 | tf_op jit(solution)/shard_map/ppermute | solution.py:25
  42.3 2.2 %collective-permute-done.6 = f32[136,128]{1,0:T(8,128)S(1)} collective-permute-done((f32[136,128]{1,0:T(8,128)S(1)}, f32[136,128]{1,0:T(8,128)S(1)}, u32[]{:S(2)}, u32[]{:S(2)}) %collective-permute-start.6) | collective-permute-done | bytes 69664 | tf_op jit(solution)/shard_map/ppermute | solution.py:25
  44.5 1.5 %collective-permute-done.5 = f32[136,128]{1,0:T(8,128)S(1)} collective-permute-done((f32[136,128]{1,0:T(8,128)S(1)}, f32[136,128]{1,0:T(8,128)S(1)}, u32[]{:S(2)}, u32[]{:S(2)}) %collective-permute-start.5) | collective-permute-done | bytes 69664 | tf_op jit(solution)/shard_map/ppermute | solution.py:25
  46.0 0.0 collective-permute-done.4
  46.0 1.2 %collective-permute-start.9 = (bf16[136,128]{1,0:T(8,128)(2,1)S(1)}, bf16[136,128]{1,0:T(8,128)(2,1)S(1)}, u32[]{:S(2)}, u32[]{:S(2)}) collective-permute-start(bf16[136,128]{1,0:T(8,128)(2,1)S(1)} %multiply_convert_fusion.refs_0_), channel_id=1, source_target_pairs={{0,24},{8,16},{16,8},{24,0},{1,25},{9,17},{17,9},{25,1},{2,26},{10... | collective-permute-start | bytes 104456 | tf_op jit(solution)/shard_map/ppermute | solution.py:25
  47.2 1.5 %collective-permute-start.8 = (bf16[136,128]{1,0:T(8,128)(2,1)S(1)}, bf16[136,128]{1,0:T(8,128)(2,1)S(1)}, u32[]{:S(2)}, u32[]{:S(2)}) collective-permute-start(bf16[136,128]{1,0:T(8,128)(2,1)S(1)} %multiply_convert_fusion.refs_0_), channel_id=1, source_target_pairs={{0,16},{8,24},{16,0},{24,8},{1,17},{9,25},{17,1},{25,9},{2,18},{10... | collective-permute-start | bytes 104456 | tf_op jit(solution)/shard_map/ppermute | solution.py:25
  48.6 0.9 %collective-permute-start.7 = (bf16[136,128]{1,0:T(8,128)(2,1)S(1)}, bf16[136,128]{1,0:T(8,128)(2,1)S(1)}, u32[]{:S(2)}, u32[]{:S(2)}) collective-permute-start(bf16[136,128]{1,0:T(8,128)(2,1)S(1)} %multiply_convert_fusion.refs_0_), channel_id=1, source_target_pairs={{0,8},{8,0},{16,24},{24,16},{1,9},{9,1},{17,25},{25,17},{2,10},{10... | collective-permute-start | bytes 104456 | tf_op jit(solution)/shard_map/ppermute | solution.py:25
  49.6 1.4 %collective-permute-done.9.refs_3_ = bf16[136,128]{1,0:T(8,128)(2,1)S(1)} collective-permute-done((bf16[136,128]{1,0:T(8,128)(2,1)S(1)}, bf16[136,128]{1,0:T(8,128)(2,1)S(1)}, u32[]{:S(2)}, u32[]{:S(2)}) %collective-permute-start.9) | collective-permute-done | bytes 34848 | tf_op jit(solution)/shard_map/ppermute | solution.py:25
  50.9 0.0 collective-permute-start.13
  50.9 0.4 collective-permute-done.8.refs_2_
  51.3 0.2 collective-permute-start.12
  51.4 1.1 %collective-permute-done.7.refs_1_ = bf16[136,128]{1,0:T(8,128)(2,1)S(1)} collective-permute-done((bf16[136,128]{1,0:T(8,128)(2,1)S(1)}, bf16[136,128]{1,0:T(8,128)(2,1)S(1)}, u32[]{:S(2)}, u32[]{:S(2)}) %collective-permute-start.7) | collective-permute-done | bytes 34848 | tf_op jit(solution)/shard_map/ppermute | solution.py:25
  52.6 0.0 collective-permute-start.11
  52.6 0.1 shard_map.19
  52.8 1.0 %collective-permute-done.11.refs_1_ = bf16[136,128]{1,0:T(8,128)(2,1)S(1)} collective-permute-done((bf16[136,128]{1,0:T(8,128)(2,1)S(1)}, bf16[136,128]{1,0:T(8,128)(2,1)S(1)}, u32[]{:S(2)}, u32[]{:S(2)}) %collective-permute-start.11) | collective-permute-done | bytes 34848 | tf_op jit(solution)/shard_map/ppermute | solution.py:25
  53.8 1.0 %shard_map.20 = bf16[256,1536]{1,0:T(8,128)(2,1)S(1)} custom-call(bf16[256,1536]{1,0:T(8,128)(2,1)S(1)} %bitcast.15, bf16[256,1536]{1,0:T(8,128)(2,1)S(1)} %collective-permute-done.y_ref, bf16[256,256]{1,0:T(8,128)(2,1)S(1)} %get-tuple-element.16.square_ref, bf16[128,256]{1,0:T(8,128)(2,1)S(1)} %get-tuple-element.17.cross_ref, ...), custom_call_target="tpu_custom_call" | custom-call | tf_op jit(solution)/shard_map/pallas_call | solution.py:227
  54.8 23.3 %all_to_all.11 = bf16[16,16,1536]{2,1,0:T(8,128)(2,1)S(1)} all-to-all(bf16[16,16,1536]{2,1,0:T(8,128)(2,1)S(1)} %bitcast.16), channel_id=1, replica_groups={{28,20,16,10,26,8,14,24,12,30,6,0,18,4,22,2},{29,21,17,11,27,9,15,25,13..., dimensions={0} | all-to-all | bytes 1572864 | tf_op jit(solution)/shard_map/all_to_all | solution.py:228
  78.0 0.9 %copy.5 = bf16[16,2,8,1536]{3,2,0,1:T(8,128)(2,1)} copy(bf16[16,2,8,1536]{3,2,1,0:T(8,128)(2,1)S(1)} %bitcast.17) | data formatting | bytes 1572864 | tf_op jit(solution)/shard_map/reshape | solution.py:229
  (6 shorter events, 0.1 us)
Async XLA Ops:
  27.1 2.3 %collective-permute-start = (bf16[256,1536]{1,0:T(8,128)(2,1)S(1)}, bf16[256,1536]{1,0:T(8,128)(2,1)S(1)}, u32[]{:S(2)}, u32[]{:S(2)}) collective-permute-start(bf16[256,1536]{1,0:T(8,128)(2,1)S(1)} %bitcast.12), channel_id=1, source_target_pairs={{0,1},{1,0},{2,3},{3,2},{4,5},{5,4},{6,7},{7,6},{8,9},{9,8},{10,11... | collective-permute-start | bytes 2359304 | tf_op jit(solution)/shard_map/ppermute | solution.py:25
  29.8 4.4 %collective-permute-start.1 = (f32[136,128]{1,0:T(8,128)S(1)}, f32[136,128]{1,0:T(8,128)S(1)}, u32[]{:S(2)}, u32[]{:S(2)}) collective-permute-start(f32[136,128]{1,0:T(8,128)S(1)} %get-tuple-element.13), channel_id=1, source_target_pairs={{0,8},{8,0},{16,24},{24,16},{1,9},{9,1},{17,25},{25,17},{2,10},{10... | collective-permute-start | bytes 208904 | tf_op jit(solution)/shard_map/ppermute | solution.py:25
  30.9 4.3 %collective-permute-start.2 = (f32[136,128]{1,0:T(8,128)S(1)}, f32[136,128]{1,0:T(8,128)S(1)}, u32[]{:S(2)}, u32[]{:S(2)}) collective-permute-start(f32[136,128]{1,0:T(8,128)S(1)} %get-tuple-element.14), channel_id=1, source_target_pairs={{0,16},{8,24},{16,0},{24,8},{1,17},{9,25},{17,1},{25,9},{2,18},{10... | collective-permute-start | bytes 208904 | tf_op jit(solution)/shard_map/ppermute | solution.py:25
  32.6 5.2 %collective-permute-start.3 = (f32[136,128]{1,0:T(8,128)S(1)}, f32[136,128]{1,0:T(8,128)S(1)}, u32[]{:S(2)}, u32[]{:S(2)}) collective-permute-start(f32[136,128]{1,0:T(8,128)S(1)} %get-tuple-element.15), channel_id=1, source_target_pairs={{0,24},{8,16},{16,8},{24,0},{1,25},{9,17},{17,9},{25,1},{2,26},{10... | collective-permute-start | bytes 208904 | tf_op jit(solution)/shard_map/ppermute | solution.py:25
  37.8 6.7 %collective-permute-start.6 = (f32[136,128]{1,0:T(8,128)S(1)}, f32[136,128]{1,0:T(8,128)S(1)}, u32[]{:S(2)}, u32[]{:S(2)}) collective-permute-start(f32[136,128]{1,0:T(8,128)S(1)} %add_add_fusion), channel_id=1, source_target_pairs={{0,6},{1,7},{2,4},{3,5},{4,2},{5,3},{6,0},{7,1},{8,14},{9,15},{10,... | collective-permute-start | bytes 208904 | tf_op jit(solution)/shard_map/ppermute | solution.py:25
  39.9 6.0 %collective-permute-start.5 = (f32[136,128]{1,0:T(8,128)S(1)}, f32[136,128]{1,0:T(8,128)S(1)}, u32[]{:S(2)}, u32[]{:S(2)}) collective-permute-start(f32[136,128]{1,0:T(8,128)S(1)} %add_add_fusion), channel_id=1, source_target_pairs={{0,4},{1,5},{2,6},{3,7},{4,0},{5,1},{6,2},{7,3},{8,12},{9,13},{10,... | collective-permute-start | bytes 208904 | tf_op jit(solution)/shard_map/ppermute | solution.py:25
  40.4 5.6 %collective-permute-start.4 = (f32[136,128]{1,0:T(8,128)S(1)}, f32[136,128]{1,0:T(8,128)S(1)}, u32[]{:S(2)}, u32[]{:S(2)}) collective-permute-start(f32[136,128]{1,0:T(8,128)S(1)} %add_add_fusion), channel_id=1, source_target_pairs={{0,2},{1,3},{2,0},{3,1},{4,6},{5,7},{6,4},{7,5},{8,10},{9,11},{10,... | collective-permute-start | bytes 208904 | tf_op jit(solution)/shard_map/ppermute | solution.py:25
  46.0 4.9 %collective-permute-start.9 = (bf16[136,128]{1,0:T(8,128)(2,1)S(1)}, bf16[136,128]{1,0:T(8,128)(2,1)S(1)}, u32[]{:S(2)}, u32[]{:S(2)}) collective-permute-start(bf16[136,128]{1,0:T(8,128)(2,1)S(1)} %multiply_convert_fusion.refs_0_), channel_id=1, source_target_pairs={{0,24},{8,16},{16,8},{24,0},{1,25},{9,17},{17,9},{25,1},{2,26},{10... | collective-permute-start | bytes 104456 | tf_op jit(solution)/shard_map/ppermute | solution.py:25
  47.2 4.1 %collective-permute-start.8 = (bf16[136,128]{1,0:T(8,128)(2,1)S(1)}, bf16[136,128]{1,0:T(8,128)(2,1)S(1)}, u32[]{:S(2)}, u32[]{:S(2)}) collective-permute-start(bf16[136,128]{1,0:T(8,128)(2,1)S(1)} %multiply_convert_fusion.refs_0_), channel_id=1, source_target_pairs={{0,16},{8,24},{16,0},{24,8},{1,17},{9,25},{17,1},{25,9},{2,18},{10... | collective-permute-start | bytes 104456 | tf_op jit(solution)/shard_map/ppermute | solution.py:25
  48.6 3.9 %collective-permute-start.7 = (bf16[136,128]{1,0:T(8,128)(2,1)S(1)}, bf16[136,128]{1,0:T(8,128)(2,1)S(1)}, u32[]{:S(2)}, u32[]{:S(2)}) collective-permute-start(bf16[136,128]{1,0:T(8,128)(2,1)S(1)} %multiply_convert_fusion.refs_0_), channel_id=1, source_target_pairs={{0,8},{8,0},{16,24},{24,16},{1,9},{9,1},{17,25},{25,17},{2,10},{10... | collective-permute-start | bytes 104456 | tf_op jit(solution)/shard_map/ppermute | solution.py:25
  49.6 3.2 %collective-permute-start.10 = (bf16[136,128]{1,0:T(8,128)(2,1)S(1)}, bf16[136,128]{1,0:T(8,128)(2,1)S(1)}, u32[]{:S(2)}, u32[]{:S(2)}) collective-permute-start(bf16[136,128]{1,0:T(8,128)(2,1)S(1)} %multiply_convert_fusion.refs_0_), channel_id=1, source_target_pairs={{0,1},{1,0},{2,3},{3,2},{4,5},{5,4},{6,7},{7,6},{8,9},{9,8},{10,11... | collective-permute-start | bytes 104456 | tf_op jit(solution)/shard_map/ppermute | solution.py:25
  50.9 1.8 %collective-permute-start.13 = (bf16[136,128]{1,0:T(8,128)(2,1)S(1)}, bf16[136,128]{1,0:T(8,128)(2,1)S(1)}, u32[]{:S(2)}, u32[]{:S(2)}) collective-permute-start(bf16[136,128]{1,0:T(8,128)(2,1)S(1)} %collective-permute-done.9.refs_3_), channel_id=1, source_target_pairs={{0,1},{1,0},{2,3},{3,2},{4,5},{5,4},{6,7},{7,6},{8,9},{9,8},{10,11... | collective-permute-start | bytes 104456 | tf_op jit(solution)/shard_map/ppermute | solution.py:25
  51.3 1.5 %collective-permute-start.12 = (bf16[136,128]{1,0:T(8,128)(2,1)S(1)}, bf16[136,128]{1,0:T(8,128)(2,1)S(1)}, u32[]{:S(2)}, u32[]{:S(2)}) collective-permute-start(bf16[136,128]{1,0:T(8,128)(2,1)S(1)} %collective-permute-done.8.refs_2_), channel_id=1, source_target_pairs={{0,1},{1,0},{2,3},{3,2},{4,5},{5,4},{6,7},{7,6},{8,9},{9,8},{10,11... | collective-permute-start | bytes 104456 | tf_op jit(solution)/shard_map/ppermute | solution.py:25
  52.6 1.2 %collective-permute-start.11 = (bf16[136,128]{1,0:T(8,128)(2,1)S(1)}, bf16[136,128]{1,0:T(8,128)(2,1)S(1)}, u32[]{:S(2)}, u32[]{:S(2)}) collective-permute-start(bf16[136,128]{1,0:T(8,128)(2,1)S(1)} %collective-permute-done.7.refs_1_), channel_id=1, source_target_pairs={{0,1},{1,0},{2,3},{3,2},{4,5},{5,4},{6,7},{7,6},{8,9},{9,8},{10,11... | collective-permute-start | bytes 104456 | tf_op jit(solution)/shard_map/ppermute | solution.py:25
